TPU v7x, 32 devices: a whole 2x2x4 slice. The times are simulated.
32 devices in a mesh: shard: 4 (over z), ctx: 2 (over y), tensor: 4 (over x, core).
Axes of the slice: x: 2, y: 2, z: 4, core: 2. Of those that a mesh axis runs over, the one named last changes fastest.
Arguments:
- tokens: bfloat16 [4, 2048, 2048], P('shard', 'ctx'), may hold values from -6 to 6
- cotangent: bfloat16 [4, 2048, 2048], P('shard', 'ctx'), may hold values from -6 to 6
- segment_ids: int32 [4, 2048], P('shard', 'ctx'), may hold values from 0 to 2, never falling along the last dimension, each value on 1 to 1280 neighbouring positions
- query_weight: float32 [2048, 2048], P(('shard', 'ctx'), 'tensor'), may hold values from -0.125 to 0.125
- key_weight: float32 [2048, 2048], P(('shard', 'ctx'), 'tensor'), may hold values from -0.125 to 0.125
- value_weight: float32 [2048, 2048], P(('shard', 'ctx'), 'tensor'), may hold values from -0.125 to 0.125
- output_weight: float32 [2048, 2048], P('tensor', ('shard', 'ctx')), may hold values from -0.125 to 0.125
- gate_weight: float32 [2048, 8192], P(('shard', 'ctx'), 'tensor'), may hold values from -0.125 to 0.125
- upward_weight: float32 [2048, 8192], P(('shard', 'ctx'), 'tensor'), may hold values from -0.125 to 0.125
- downward_weight: float32 [8192, 2048], P('tensor', ('shard', 'ctx')), may hold values from -0.0625 to 0.0625
- querynorm_weight: float32 [16, 128], P('tensor', ('shard', 'ctx')), may hold values from 0.5 to 1.5
- keynorm_weight: float32 [16, 128], P('tensor', ('shard', 'ctx')), may hold values from 0.5 to 1.5
- postattention_weight: float32 [2048], P(('shard', 'ctx')), may hold values from 0.5 to 1.5
- postfeedforward_weight: float32 [2048], P(('shard', 'ctx')), may hold values from 0.5 to 1.5
- query_mean: float32 [2048, 2048], P(('shard', 'ctx'), 'tensor'), may hold values from -112 to 112
- key_mean: float32 [2048, 2048], P(('shard', 'ctx'), 'tensor'), may hold values from -112 to 112
- value_mean: float32 [2048, 2048], P(('shard', 'ctx'), 'tensor'), may hold values from -112 to 112
- output_mean: float32 [2048, 2048], P('tensor', ('shard', 'ctx')), may hold values from -112 to 112
- gate_mean: float32 [2048, 8192], P(('shard', 'ctx'), 'tensor'), may hold values from -56 to 56
- upward_mean: float32 [2048, 8192], P(('shard', 'ctx'), 'tensor'), may hold values from -56 to 56
- downward_mean: float32 [8192, 2048], P('tensor', ('shard', 'ctx')), may hold values from -112 to 112
- querynorm_mean: float32 [16, 128], P('tensor', ('shard', 'ctx')), may hold values from -112 to 112
- keynorm_mean: float32 [16, 128], P('tensor', ('shard', 'ctx')), may hold values from -112 to 112
- postattention_mean: float32 [2048], P(('shard', 'ctx')), may hold values from -112 to 112
- postfeedforward_mean: float32 [2048], P(('shard', 'ctx')), may hold values from -112 to 112
- query_square: float32 [2048, 2048], P(('shard', 'ctx'), 'tensor'), may hold values from 409 to 1638
- key_square: float32 [2048, 2048], P(('shard', 'ctx'), 'tensor'), may hold values from 409 to 1638
- value_square: float32 [2048, 2048], P(('shard', 'ctx'), 'tensor'), may hold values from 409 to 1638
- output_square: float32 [2048, 2048], P('tensor', ('shard', 'ctx')), may hold values from 409 to 1638
- gate_square: float32 [2048, 8192], P(('shard', 'ctx'), 'tensor'), may hold values from 81 to 327
- upward_square: float32 [2048, 8192], P(('shard', 'ctx'), 'tensor'), may hold values from 81 to 327
- downward_square: float32 [8192, 2048], P('tensor', ('shard', 'ctx')), may hold values from 409 to 1638
- querynorm_square: float32 [16, 128], P('tensor', ('shard', 'ctx')), may hold values from 819 to 3276
- keynorm_square: float32 [16, 128], P('tensor', ('shard', 'ctx')), may hold values from 819 to 3276
- postattention_square: float32 [2048], P(('shard', 'ctx')), may hold values from 204 to 819
- postfeedforward_square: float32 [2048], P(('shard', 'ctx')), may hold values from 204 to 819
Outputs:
- block_out: float32 [4, 2048, 2048], P('shard', 'ctx')
- input_grad: float32 [4, 2048, 2048], P('shard', 'ctx')
- query_gradient: float32 [2048, 2048], P(('shard', 'ctx'), 'tensor')
- key_gradient: float32 [2048, 2048], P(('shard', 'ctx'), 'tensor')
- value_gradient: float32 [2048, 2048], P(('shard', 'ctx'), 'tensor')
- output_gradient: float32 [2048, 2048], P('tensor', ('shard', 'ctx'))
- gate_gradient: float32 [2048, 8192], P(('shard', 'ctx'), 'tensor')
- upward_gradient: float32 [2048, 8192], P(('shard', 'ctx'), 'tensor')
- downward_gradient: float32 [8192, 2048], P('tensor', ('shard', 'ctx'))
- querynorm_gradient: float32 [16, 128], P('tensor', ('shard', 'ctx'))
- keynorm_gradient: float32 [16, 128], P('tensor', ('shard', 'ctx'))
- postattention_gradient: float32 [2048], P(('shard', 'ctx'))
- postfeedforward_gradient: float32 [2048], P(('shard', 'ctx'))
- query_updated: float32 [2048, 2048], P(('shard', 'ctx'), 'tensor')
- key_updated: float32 [2048, 2048], P(('shard', 'ctx'), 'tensor')
- value_updated: float32 [2048, 2048], P(('shard', 'ctx'), 'tensor')
- output_updated: float32 [2048, 2048], P('tensor', ('shard', 'ctx'))
- gate_updated: float32 [2048, 8192], P(('shard', 'ctx'), 'tensor')
- upward_updated: float32 [2048, 8192], P(('shard', 'ctx'), 'tensor')
- downward_updated: float32 [8192, 2048], P('tensor', ('shard', 'ctx'))
- querynorm_updated: float32 [16, 128], P('tensor', ('shard', 'ctx'))
- keynorm_updated: float32 [16, 128], P('tensor', ('shard', 'ctx'))
- postattention_updated: float32 [2048], P(('shard', 'ctx'))
- postfeedforward_updated: float32 [2048], P(('shard', 'ctx'))
- query_newmean: float32 [2048, 2048], P(('shard', 'ctx'), 'tensor')
- key_newmean: float32 [2048, 2048], P(('shard', 'ctx'), 'tensor')
- value_newmean: float32 [2048, 2048], P(('shard', 'ctx'), 'tensor')
- output_newmean: float32 [2048, 2048], P('tensor', ('shard', 'ctx'))
- gate_newmean: float32 [2048, 8192], P(('shard', 'ctx'), 'tensor')
- upward_newmean: float32 [2048, 8192], P(('shard', 'ctx'), 'tensor')
- downward_newmean: float32 [8192, 2048], P('tensor', ('shard', 'ctx'))
- querynorm_newmean: float32 [16, 128], P('tensor', ('shard', 'ctx'))
- keynorm_newmean: float32 [16, 128], P('tensor', ('shard', 'ctx'))
- postattention_newmean: float32 [2048], P(('shard', 'ctx'))
- postfeedforward_newmean: float32 [2048], P(('shard', 'ctx'))
- query_newsquare: float32 [2048, 2048], P(('shard', 'ctx'), 'tensor')
- key_newsquare: float32 [2048, 2048], P(('shard', 'ctx'), 'tensor')
- value_newsquare: float32 [2048, 2048], P(('shard', 'ctx'), 'tensor')
- output_newsquare: float32 [2048, 2048], P('tensor', ('shard', 'ctx'))
- gate_newsquare: float32 [2048, 8192], P(('shard', 'ctx'), 'tensor')
- upward_newsquare: float32 [2048, 8192], P(('shard', 'ctx'), 'tensor')
- downward_newsquare: float32 [8192, 2048], P('tensor', ('shard', 'ctx'))
- querynorm_newsquare: float32 [16, 128], P('tensor', ('shard', 'ctx'))
- keynorm_newsquare: float32 [16, 128], P('tensor', ('shard', 'ctx'))
- postattention_newsquare: float32 [2048], P(('shard', 'ctx'))
- postfeedforward_newsquare: float32 [2048], P(('shard', 'ctx'))
Inputs may be any that keep to these rules, and one draw needn't show every extreme that they name: `segment_ids`: document numbers never fall along a sequence; each of the 3 documents holds 1 to 1280 positions, one exactly 1280.
All inputs are finite; a program needn't handle non-finite values.
Results may differ from a plain program's by a relative error of at most 0.025.
Values may be sent and summed in bfloat16 or wider, within the bound.
No kernel may reach another device: no remote copies, remote signals or barrier semaphores. Data moves between devices by JAX's collectives and lax.ppermute only.
A program may use at most 320 MiB of HBM per device.

v0:
```python
import math

import jax
import jax.numpy as jnp
from jax import lax
from jax.sharding import Mesh
from jax.sharding import PartitionSpec as P

DOCS = 3
rope_base = 500000.0
norm_eps = 1e-06
learn_rate = 0.3
beta_one = 0.9
beta_two = 0.95
adam_eps = 1e-08
decay_rate = 0.1
step_count = 2
masked_score = -1e30

f32 = jnp.float32
b16 = jnp.bfloat16

SH, SL, CX, TX, TC = "sh", "sl", "ctx", "tx", "tc"
SHARD = (SH, SL)
TENSOR = (TX, TC)


def dot(a, b, ca, cb):
    return lax.dot_general(a, b, (((ca,), (cb,)), ((), ())), preferred_element_type=f32)


def swap(value, axis):
    return lax.ppermute(value, axis, [(0, 1), (1, 0)])


def pair(mine, other, axis):
    first = lax.axis_index(axis) == 0
    return jnp.where(
        first, jnp.concatenate([mine, other], 0), jnp.concatenate([other, mine], 0)
    )


def gather_axis(value, axis):
    if lax.axis_size(axis) == 2:
        return pair(value, swap(value, axis), axis)
    return lax.all_gather(value, axis, axis=0, tiled=True)


def scatter_axis(value, axis):
    size = lax.axis_size(axis)
    if size != 2:
        return lax.psum_scatter(value.astype(b16), axis, scatter_dimension=0, tiled=True).astype(f32)
    half = value.shape[0] // 2
    index = lax.axis_index(axis)
    mine = lax.dynamic_slice_in_dim(value, index * half, half, 0)
    theirs = lax.dynamic_slice_in_dim(value, (1 - index) * half, half, 0)
    return mine.astype(f32) + swap(theirs.astype(b16), axis).astype(f32)


def rows_sum(value):
    return scatter_axis(scatter_axis(value, TC), TX)


def rows_all(value):
    return gather_axis(gather_axis(value, TX), TC)


def gather_z(value):
    return lax.all_gather(value, SHARD, axis=0, tiled=True)


def scatter_z(value):
    return lax.psum_scatter(value, SHARD, scatter_dimension=0, tiled=True)


def rotate_half(vector):
    half_dim = vector.shape[-1] // 2
    return jnp.concatenate([-vector[..., half_dim:], vector[..., :half_dim]], axis=-1)


def apply_rope(vector, cosine, sine_table):
    return vector * cosine + rotate_half(vector) * sine_table


def rope_back(gradient, cosine, sine_table):
    return gradient * cosine - rotate_half(gradient * sine_table)


def adam_step(weight, first_moment, second_moment, gradient):
    new_first = beta_one * first_moment + (1.0 - beta_one) * gradient
    new_second = beta_two * second_moment + (1.0 - beta_two) * gradient * gradient
    first_hat = new_first / (1.0 - beta_one**step_count)
    second_hat = new_second / (1.0 - beta_two**step_count)
    updated = weight - learn_rate * (
        first_hat / (jnp.sqrt(second_hat) + adam_eps) + decay_rate * weight
    )
    return (updated, new_first, new_second)


def attention_forward(query_rot, keys_all, values_all, docs_here, docs_all, offset):
    row_count, heads_here, head_dim = query_rot.shape
    length = docs_all.shape[0]
    block_rows = min(512, row_count)
    blocks = row_count // block_rows
    key_index = jnp.arange(length, dtype=jnp.int32)
    divisor = math.sqrt(head_dim)
    firsts = jnp.arange(blocks, dtype=jnp.int32) * block_rows
    query_blocks = query_rot.reshape(blocks, block_rows, heads_here, head_dim)
    doc_blocks = docs_here.reshape(blocks, block_rows)

    def block_scores(query_block, first_row, doc_block):
        query_index = offset + first_row + jnp.arange(block_rows, dtype=jnp.int32)
        allowed = (key_index[None, :] <= query_index[:, None]) & (
            docs_all[None, :] == doc_block[:, None]
        )
        scores = (
            jnp.einsum("qhd,khd->hqk", query_block, keys_all, preferred_element_type=f32) / divisor
        )
        return jnp.where(allowed[None, :, :], scores, masked_score)

    def forward_block(operands):
        query_block, first_row, doc_block = operands
        scores = block_scores(query_block, first_row, doc_block)
        row_peak = jnp.max(scores, axis=2, keepdims=True)
        exponent = jnp.exp(scores - row_peak)
        row_total = jnp.sum(exponent, axis=2, keepdims=True)
        soft_half = (exponent / row_total).astype(b16)
        attended_block = jnp.einsum(
            "hqk,khd->qhd", soft_half, values_all, preferred_element_type=f32
        )
        return (attended_block, (row_peak + jnp.log(row_total))[:, :, 0])

    attended_blocks, log_totals = lax.map(forward_block, (query_blocks, firsts, doc_blocks))
    attended = attended_blocks.reshape(row_count, heads_here * head_dim).astype(b16)

    def backward(grad_attended):
        row_delta = jnp.sum(
            (grad_attended.astype(f32) * attended.astype(f32)).reshape(
                row_count, heads_here, head_dim
            ),
            axis=2,
        )
        delta_blocks = row_delta.reshape(blocks, block_rows, heads_here)
        grad_blocks = grad_attended.reshape(blocks, block_rows, heads_here, head_dim)

        def backward_block(state_pair, operands):
            grad_keys, grad_values = state_pair
            query_block, first_row, doc_block, log_block, grad_block, delta_block = operands
            scores = block_scores(query_block, first_row, doc_block)
            soft_back = jnp.exp(scores - log_block[:, :, None])
            back_half = soft_back.astype(b16)
            grad_values = grad_values + jnp.einsum(
                "hqk,qhd->khd", back_half, grad_block, preferred_element_type=f32
            )
            grad_soft = jnp.einsum(
                "qhd,khd->hqk", grad_block, values_all, preferred_element_type=f32
            )
            grad_scores = (
                soft_back * (grad_soft - jnp.transpose(delta_block)[:, :, None]) / divisor
            ).astype(b16)
            grad_query_block = jnp.einsum(
                "hqk,khd->qhd", grad_scores, keys_all, preferred_element_type=f32
            )
            grad_keys = grad_keys + jnp.einsum(
                "hqk,qhd->khd", grad_scores, query_block, preferred_element_type=f32
            )
            return ((grad_keys, grad_values), grad_query_block)

        zero_keys = jnp.zeros((length, heads_here, head_dim), f32)
        (grad_keys, grad_values), grad_query_blocks = lax.scan(
            backward_block,
            (zero_keys, zero_keys),
            (query_blocks, firsts, doc_blocks, log_totals, grad_blocks, delta_blocks),
        )
        return grad_query_blocks.reshape(row_count, heads_here, head_dim), grad_keys, grad_values

    return attended, backward


def shards(tokens, cotangent, segment_ids, *state):
    masters, first_moments, second_moments = state[:11], state[11:22], state[22:33]
    inputs = tokens[0]
    docs_here = segment_ids[0]
    rows, width = inputs.shape
    ring = lax.axis_size(SHARD)
    teams = lax.axis_size(TENSOR)
    y = lax.axis_index(CX)
    piece = masters[0].shape[0]
    local_width = masters[0].shape[1]
    heads_here = masters[7].shape[0]
    head_dim = width // (teams * heads_here)
    block = rows // teams
    my_block = lax.axis_index(TC) * lax.axis_size(TX) + lax.axis_index(TX)

    def halves(value):
        split = value.reshape(value.shape[:-1] + (ring, 2, piece))
        axis = split.ndim - 2
        shape = value.shape[:-1] + (ring * piece,)
        return [
            lax.dynamic_index_in_dim(split, index, axis, keepdims=False).reshape(shape)
            for index in (y, 1 - y)
        ]

    def whole(own, oth):
        lead = own.shape[:-1]
        own, oth = (half.reshape(lead + (ring, 1, piece)) for half in (own, oth))
        axis = own.ndim - 2
        return jnp.where(
            y == 0, jnp.concatenate([own, oth], axis), jnp.concatenate([oth, own], axis)
        ).reshape(lead + (width,))

    def my_rows(value):
        return lax.dynamic_slice_in_dim(value, my_block * block, block, 0)

    pieces = [weight.astype(b16) for weight in masters[:7]]
    qkv_piece = jnp.concatenate(pieces[:3], axis=1)
    out_piece = jnp.transpose(pieces[3])
    gate_piece, up_piece = pieces[4], pieces[5]
    down_piece = jnp.transpose(pieces[6])
    gains = jnp.concatenate([gain.astype(b16).reshape(-1) for gain in masters[7:]])[None]
    docs_all = gather_axis(docs_here, CX)
    gains = gather_axis(gather_axis(gather_axis(gains, CX), SL), SH)
    qkv_own = gather_z(qkv_piece)
    qkv_oth = swap(qkv_own, CX)
    out_own = gather_z(out_piece)
    out_oth = swap(out_own, CX)
    gate_own = gather_z(gate_piece)
    gate_oth = swap(gate_own, CX)
    up_own = gather_z(up_piece)
    up_oth = swap(up_own, CX)
    down_swapped = swap(down_piece, CX)
    down_own = gather_z(down_piece)
    down_oth = gather_z(down_swapped)

    count = heads_here * (masters[7].shape[1])
    head_gain = lambda part: jnp.transpose(
        part.reshape(ring * 2, heads_here, masters[7].shape[1]), (1, 0, 2)
    ).reshape(local_width)
    query_scale = head_gain(gains[:, :count]).astype(f32)
    key_scale = head_gain(gains[:, count : 2 * count]).astype(f32)
    attn_gain = halves(gains[:, 2 * count : 2 * count + piece].reshape(width).astype(f32))
    ffn_gain = halves(gains[:, 2 * count + piece :].reshape(width).astype(f32))

    length = docs_all.shape[0]
    offset = y * rows
    doc_range = jnp.arange(DOCS, dtype=jnp.int32)
    counts = jnp.sum((docs_all[:, None] == doc_range[None, :]).astype(jnp.int32), axis=0)
    starts = jnp.cumsum(counts) - counts
    own_start = jnp.sum(
        jnp.where(docs_here[:, None] == doc_range[None, :], starts[None, :], 0), axis=1
    )
    positions = offset + jnp.arange(rows, dtype=jnp.int32) - own_start
    frequencies = rope_base ** (
        -(jnp.arange(head_dim // 2, dtype=jnp.float32) * 2.0) / head_dim
    )
    angles = positions.astype(f32)[:, None] * frequencies[None, :]
    cosine, sine_table = jnp.cos(angles), jnp.sin(angles)
    cosine = jnp.concatenate([cosine, cosine], axis=1)[:, None, :]
    sine_table = jnp.concatenate([sine_table, sine_table], axis=1)[:, None, :]

    x_half = halves(inputs)
    raw = dot(x_half[0], qkv_own, 1, 0) + dot(x_half[1], qkv_oth, 1, 0)
    query_raw, key_raw = raw[:, :local_width], raw[:, local_width : 2 * local_width]
    value_half = raw[:, 2 * local_width :].astype(b16).reshape(rows, heads_here, head_dim)
    square_sums = lax.psum(
        jnp.stack([jnp.sum(query_raw * query_raw, axis=1), jnp.sum(key_raw * key_raw, axis=1)]),
        TENSOR,
    )
    inverses = lax.rsqrt(square_sums / width + norm_eps)
    query_inv, key_inv = inverses[0][:, None], inverses[1][:, None]
    query_unit = query_raw * query_inv
    key_unit = key_raw * key_inv
    query_rot = apply_rope(
        (query_unit * query_scale).reshape(rows, heads_here, head_dim), cosine, sine_table
    ).astype(b16)
    key_rot = apply_rope(
        (key_unit * key_scale).reshape(rows, heads_here, head_dim), cosine, sine_table
    ).astype(b16)
    keys_all = gather_axis(key_rot, CX)
    values_all = gather_axis(value_half, CX)
    attended, attention_backward = attention_forward(
        query_rot, keys_all, values_all, docs_here, docs_all, offset
    )
    branch = [rows_sum(dot(attended, w, 1, 1)) for w in (out_own, out_oth)]
    mean_of = lambda a, b: sum(jnp.sum(u * v, axis=1, keepdims=True) for u, v in zip(a, b)) / width
    branch_inv = lax.rsqrt(mean_of(branch, branch) + norm_eps)
    branch_unit = [part * branch_inv for part in branch]
    x_rows = halves(my_rows(inputs).astype(f32))
    residual = [x + u * g for x, u, g in zip(x_rows, branch_unit, attn_gain)]
    res_half = [rows_all(part.astype(b16)) for part in residual]

    gate_pre = dot(res_half[0], gate_own, 1, 0) + dot(res_half[1], gate_oth, 1, 0)
    up_pre = dot(res_half[0], up_own, 1, 0) + dot(res_half[1], up_oth, 1, 0)
    gate_sigmoid = jax.nn.sigmoid(gate_pre)
    silu_value = gate_pre * gate_sigmoid
    activated = (silu_value * up_pre).astype(b16)
    ffn_out = [rows_sum(dot(activated, w, 1, 1)) for w in (down_own, down_oth)]
    ffn_inv = lax.rsqrt(mean_of(ffn_out, ffn_out) + norm_eps)
    ffn_unit = [part * ffn_inv for part in ffn_out]
    grad_out = halves(my_rows(cotangent[0]).astype(f32))
    scaled_out = [g * w for g, w in zip(grad_out, ffn_gain)]
    dots = mean_of(scaled_out, ffn_unit)
    d_ffn = [
        rows_all((ffn_inv * (s - u * dots)).astype(b16)) for s, u in zip(scaled_out, ffn_unit)
    ]
    grad_ffn_gain = [jnp.sum(g * u, axis=0) for g, u in zip(grad_out, ffn_unit)]
    block_rows = whole(*[r + u * g for r, u, g in zip(residual, ffn_unit, ffn_gain)])
    block_share = rows_all(block_rows.astype(b16)).astype(f32)

    def finish(own, oth):
        received = swap(oth.astype(b16), CX)
        return scatter_z((own + received.astype(f32)).astype(b16)).astype(f32)

    down_parts = [scatter_z(dot(d, activated, 0, 0).astype(b16)) for d in d_ffn]
    grad_down = down_parts[0].astype(f32) + swap(down_parts[1], CX).astype(f32)
    grad_act = dot(d_ffn[0], down_own, 1, 0) + dot(d_ffn[1], down_oth, 1, 0)
    d_gate = (grad_act * up_pre * gate_sigmoid * (1.0 + gate_pre * (1.0 - gate_sigmoid))).astype(
        b16
    )
    d_up = (grad_act * silu_value).astype(b16)
    back_ffn = [
        rows_sum(dot(d_gate, g, 1, 1) + dot(d_up, u, 1, 1))
        for g, u in ((gate_own, up_own), (gate_oth, up_oth))
    ]
    grad_gate = finish(dot(res_half[0], d_gate, 0, 0), dot(res_half[1], d_gate, 0, 0))
    grad_upward = finish(dot(res_half[0], d_up, 0, 0), dot(res_half[1], d_up, 0, 0))
    grad_res = [g + b for g, b in zip(grad_out, back_ffn)]
    grad_attn_gain = [jnp.sum(g * u, axis=0) for g, u in zip(grad_res, branch_unit)]
    scaled_res = [g * w for g, w in zip(grad_res, attn_gain)]
    dots = mean_of(scaled_res, branch_unit)
    d_branch = [
        rows_all((branch_inv * (s - u * dots)).astype(b16))
        for s, u in zip(scaled_res, branch_unit)
    ]

    d_att = (dot(d_branch[0], out_own, 1, 0) + dot(d_branch[1], out_oth, 1, 0)).astype(b16)
    grad_outw = finish(dot(d_branch[0], attended, 0, 0), dot(d_branch[1], attended, 0, 0))
    grad_query_rot, grad_keys, grad_values = attention_backward(d_att)
    grad_key_rot = scatter_axis(grad_keys, CX)
    d_vals = scatter_axis(grad_values, CX).astype(b16).reshape(rows, local_width)
    grad_query_unit = rope_back(grad_query_rot, cosine, sine_table).reshape(rows, local_width)
    grad_key_unit = rope_back(grad_key_rot, cosine, sine_table).reshape(rows, local_width)
    grad_gain_query = jnp.sum(grad_query_unit * query_unit, axis=0)
    grad_gain_key = jnp.sum(grad_key_unit * key_unit, axis=0)
    scaled_query = grad_query_unit * query_scale
    scaled_key = grad_key_unit * key_scale
    norm_sums = lax.psum(
        jnp.stack(
            [jnp.sum(scaled_query * query_unit, axis=1), jnp.sum(scaled_key * key_unit, axis=1)]
        ),
        TENSOR,
    )
    d_q = (query_inv * (scaled_query - query_unit * (norm_sums[0] / width)[:, None])).astype(b16)
    d_k = (key_inv * (scaled_key - key_unit * (norm_sums[1] / width)[:, None])).astype(b16)
    d_qkv = jnp.concatenate([d_q, d_k, d_vals], axis=1)
    grad_qkv = finish(dot(x_half[0], d_qkv, 0, 0), dot(x_half[1], d_qkv, 0, 0))
    back_attn = [rows_sum(dot(d_qkv, w, 1, 1)) for w in (qkv_own, qkv_oth)]
    input_rows = whole(*[g + b for g, b in zip(grad_res, back_attn)])
    input_share = rows_all(input_rows.astype(b16)).astype(f32)

    index = lax.axis_index(SHARD) * 2 + y
    head_sums = lax.psum(jnp.stack([grad_gain_query, grad_gain_key]), (SH, SL, CX))
    head_sums = head_sums.reshape(2, heads_here, head_dim)
    head_piece = masters[7].shape[1]
    head_sums = lax.dynamic_slice_in_dim(head_sums, index * head_piece, head_piece, 2)
    wide_sums = lax.psum(
        jnp.stack([whole(*grad_attn_gain), whole(*grad_ffn_gain)]), (SH, SL, CX, TX, TC)
    )
    wide_sums = lax.dynamic_slice_in_dim(wide_sums, index * piece, piece, 1)

    grads = [
        grad_qkv[:, :local_width],
        grad_qkv[:, local_width : 2 * local_width],
        grad_qkv[:, 2 * local_width :],
        jnp.transpose(grad_outw),
        grad_gate,
        grad_upward,
        jnp.transpose(grad_down),
        head_sums[0],
        head_sums[1],
        wide_sums[0],
        wide_sums[1],
    ]
    stepped = [
        adam_step(masters[i], first_moments[i], second_moments[i], grads[i]) for i in range(11)
    ]
    return tuple(
        [block_share[None], input_share[None]]
        + grads
        + [triple[part] for part in range(3) for triple in stepped]
    )


def solution(mesh):
    ring, ctx, teams = (mesh.shape[name] for name in mesh.axis_names)
    fine = Mesh(
        mesh.devices.reshape(ring // 2, 2, ctx, teams // 2, 2), (SH, SL, CX, TX, TC)
    )
    owners = (SH, SL, CX)
    column = P(owners, TENSOR)
    row = P(TENSOR, owners)
    vector = P(owners)
    act = P(SHARD, CX, None)
    weights = (column, column, column, row, column, column, row, row, row, vector, vector)
    return jax.shard_map(
        shards,
        mesh=fine,
        in_specs=(act, act, P(SHARD, CX)) + weights * 3,
        out_specs=(act, act) + weights * 4,
        check_vma=False,
    )
```

profile of v0, /device:TPU:0, one launch (start us, length us, event | category | flops | bytes accessed | tf_op | source)
XLA Modules:
  0.0 1267.0 jit_solution(17863630650613885521)
XLA Ops:
  36.9 41.1 %all-gather.7.cloned.1.call-done = bf16[1024,1536]{1,0:T(8,128)(2,1)} async-done(((bf16[256,1536]{1,0:T(8,128)(2,1)}), bf16[1024,1536]{1,0:T(8,128)(2,1)}) %all-gather.7.cloned.1.call-update) | async-done | bytes 3145744 | tf_op jit(solution)/shard_map/all_gather | solution.py:69
  94.6 14.5 %all-gather.9.cloned.1.call-done = bf16[1024,512]{0,1:T(8,128)(2,1)} async-done(((bf16[256,512]{0,1:T(8,128)(2,1)}), bf16[1024,512]{0,1:T(8,128)(2,1)}) %all-gather.9.cloned.1.call-update) | async-done | bytes 1048592 | tf_op jit(solution)/shard_map/all_gather | solution.py:69
  115.1 34.2 %collective-permute-done.1 = bf16[1024,1536]{1,0:T(8,128)(2,1)} collective-permute-done((bf16[1024,1536]{1,0:T(8,128)(2,1)}, bf16[1024,1536]{1,0:T(8,128)(2,1)}, u32[]{:S(2)}, u32[]{:S(2)}) %collective-permute-start.1) | collective-permute-done | bytes 3145760 | tf_op jit(solution)/shard_map/ppermute | solution.py:33
  194.2 9.3 collective-permute-done.5
  206.4 18.0 %collective-permute-done.6 = bf16[1024,4,128]{2,0,1:T(8,128)(2,1)} collective-permute-done((bf16[1024,4,128]{2,0,1:T(8,128)(2,1)}, bf16[1024,4,128]{2,0,1:T(8,128)(2,1)}, u32[]{:S(2)}, u32[]{:S(2)}) %collective-permute-start.6) | collective-permute-done | bytes 1048608 | tf_op jit(solution)/shard_map/ppermute | solution.py:33
  228.6 33.1 %while.30 = (s32[]{:T(128)}, bf16[2,512,4,128]{3,1,2,0:T(8,128)(2,1)}, f32[2,4,512]{2,1,0:T(4,128)S(1)}, s32[2]{0:T(128)S(1)}, s32[]{:T(128)}, /*index=5*/s32[20...) while((s32[]{:T(128)}, ...), condition=%wide.region_9.10_spmd.clone.clone, body=%wide.region_6.9_spmd.clone.sunk.clone | while | flops 2200959488 | bytes 68766376 | solution.py:133
  308.4 9.9 collective-permute-done.11
  319.9 7.9 collective-permute-done.8
  332.2 11.0 collective-permute-done.14
  347.2 12.8 %collective-permute-done.12 = bf16[256,1024]{0,1:T(8,128)(2,1)S(1)} collective-permute-done((bf16[256,1024]{0,1:T(8,128)(2,1)S(1)}, bf16[256,1024]{0,1:T(8,128)(2,1)S(1)}, u32[]{:S(2)}, u32[]{:S(2)}) %collective-permute-start.12) | collective-permute-done | bytes 524320 | tf_op jit(solution)/shard_map/ppermute | solution.py:33
  360.4 18.2 %collective-permute-done.17 = bf16[1024,2048]{1,0:T(8,128)(2,1)} collective-permute-done((bf16[1024,2048]{1,0:T(8,128)(2,1)}, bf16[1024,2048]{1,0:T(8,128)(2,1)}, u32[]{:S(2)}, u32[]{:S(2)}) %collective-permute-start.17) | collective-permute-done | bytes 4194336 | tf_op jit(solution)/shard_map/ppermute | solution.py:33
  378.6 11.6 fusion.84
  390.1 77.4 %collective-permute-done.16 = bf16[1024,2048]{1,0:T(8,128)(2,1)} collective-permute-done((bf16[1024,2048]{1,0:T(8,128)(2,1)}, bf16[1024,2048]{1,0:T(8,128)(2,1)}, u32[]{:S(2)}, u32[]{:S(2)}) %collective-permute-start.16) | collective-permute-done | bytes 4194336 | tf_op jit(solution)/shard_map/ppermute | solution.py:33
  467.5 8.8 fusion.85
  483.8 13.0 %multiply_convert_fusion.3 = (bf16[1024,2048]{1,0:T(8,128)(2,1)}, f32[1024,2048]{1,0:T(8,128)}) fusion(f32[1024,2048]{1,0:T(8,128)} %convolution_add_fusion.3, f32[1024,2048]{1,0:T(8,128)} %fusion.84, bf16[1024,2048]{1,0:T(8,128)(2,1)S(1)} %copy-done.145, bf16[512,1024]{0,1:T(8,128)(2,1)S(1)} %collective-permute-done.13, ...), kind=kOutput, calls=%fused_computation.55 | convolution fusion | flops 4319084544 | bytes 35651584 | tf_op jit(solution)/shard_map/dot_general | solution.py:29
  522.4 9.4 collective-permute-done.22
  533.4 8.7 collective-permute-done.19
  546.9 11.6 collective-permute-done.27
  560.4 12.8 %collective-permute-done.25 = bf16[256,1024]{0,1:T(8,128)(2,1)S(1)} collective-permute-done((bf16[256,1024]{0,1:T(8,128)(2,1)S(1)}, bf16[256,1024]{0,1:T(8,128)(2,1)S(1)}, u32[]{:S(2)}, u32[]{:S(2)}) %collective-permute-start.25) | collective-permute-done | bytes 524320 | tf_op jit(solution)/shard_map/ppermute | solution.py:33
  580.9 11.3 fusion.63
  592.2 16.8 %multiply_convert_fusion.1 = (bf16[1024,2048]{1,0:T(8,128)(2,1)}, bf16[1024,2048]{1,0:T(8,128)(2,1)}) fusion(f32[1024,2048]{1,0:T(8,128)} %convolution_add_fusion.3, f32[1024,2048]{1,0:T(8,128)} %get-tuple-element.719, f32[1024,2048]{1,0:T(8,128)} %fusion.63, bf16[1024,2048]{0,1:T(8,128)(2,1)} %all-gather.15.cloned.1.call-done, ...), kind=kOutput, calls=%fused_computation.53 | convolution fusion | flops 4333764608 | bytes 39845888 | tf_op jit(solution)/shard_map/dot_general | solution.py:29
  638.8 10.6 collective-permute-done.32
  649.5 10.8 collective-permute-done.30
  664.8 12.0 collective-permute-done.35
  678.8 12.7 %collective-permute-done.33 = bf16[256,1024]{0,1:T(8,128)(2,1)S(1)} collective-permute-done((bf16[256,1024]{0,1:T(8,128)(2,1)S(1)}, bf16[256,1024]{0,1:T(8,128)(2,1)S(1)}, u32[]{:S(2)}, u32[]{:S(2)}) %collective-permute-start.33) | collective-permute-done | bytes 524320 | tf_op jit(solution)/shard_map/ppermute | solution.py:33
  694.9 24.1 %collective-permute-done.46 = bf16[1024,512]{1,0:T(8,128)(2,1)S(1)} collective-permute-done((bf16[1024,512]{1,0:T(8,128)(2,1)S(1)}, bf16[1024,512]{1,0:T(8,128)(2,1)S(1)}, u32[]{:S(2)}, u32[]{:S(2)}) %collective-permute-start.46) | collective-permute-done | bytes 1048608 | tf_op jit(solution)/shard_map/ppermute | solution.py:33
  721.4 9.4 convolution_convert_fusion.2
  730.9 10.0 convolution_convert_fusion.3
  742.5 10.0 convolution_convert_fusion.4
  761.5 73.3 %collective-permute-done.48 = bf16[1024,2048]{1,0:T(8,128)(2,1)} collective-permute-done((bf16[1024,2048]{1,0:T(8,128)(2,1)}, bf16[1024,2048]{1,0:T(8,128)(2,1)}, u32[]{:S(2)}, u32[]{:S(2)}) %collective-permute-start.48) | collective-permute-done | bytes 4194336 | tf_op jit(solution)/shard_map/ppermute | solution.py:33
  834.8 10.5 add_convert_fusion
  847.2 92.3 %while.31 = (s32[]{:T(128)}, f32[2048,4,128]{0,2,1:T(8,128)}, f32[2048,4,128]{0,2,1:T(8,128)}, f32[2,512,4,128]{3,1,2,0:T(8,128)}, bf16[2,512,4,128]{3,1,2,0:T(8...) while((s32[]{:T(128)}, f32[2048,4,128]{0,2,1:T(8,128)}, ...), condition=%wide.region_20.21_spmd.clone.clone, body=%wide.region_19.20_spmd.clone.sunk.clone | while | flops 5422187008 | bytes 180431296 | solution.py:170
  849.9 8.1 fusion.213
  858.0 12.0 multiply_convert_fusion.12
  881.1 10.9 bitcast_add_fusion.13
  894.4 8.1 fusion.213
  902.5 12.0 multiply_convert_fusion.12
  914.5 8.2 bitcast_add_fusion.12
  927.1 12.1 bitcast_add_fusion.13
  957.4 8.9 add_convert_fusion.1
  966.3 12.4 collective-permute-done.37
  983.2 14.4 %collective-permute-done.38 = bf16[1024,4,128]{0,2,1:T(8,128)(2,1)} collective-permute-done((bf16[1024,4,128]{0,2,1:T(8,128)(2,1)}, bf16[1024,4,128]{0,2,1:T(8,128)(2,1)}, u32[]{:S(2)}, u32[]{:S(2)}) %collective-permute-start.38) | collective-permute-done | bytes 1048608 | tf_op jit(solution)/shard_map/ppermute | solution.py:33
  1058.1 18.2 %collective-permute-done.23 = bf16[256,2048]{1,0:T(8,128)(2,1)S(1)} collective-permute-done((bf16[256,2048]{1,0:T(8,128)(2,1)S(1)}, bf16[256,2048]{1,0:T(8,128)(2,1)S(1)}, u32[]{:S(2)}, u32[]{:S(2)}) %collective-permute-start.23) | collective-permute-done | bytes 1048608 | tf_op jit(solution)/shard_map/ppermute | solution.py:33
  1078.6 8.9 collective-permute-done.40
  1087.8 10.5 collective-permute-done.42
  1102.9 8.6 add_convert_fusion.2
  1137.2 41.0 %psum.31 = f32[2,2048]{1,0:T(2,128)S(1)} all-reduce(f32[2,2048]{1,0:T(2,128)S(1)} %pad_maximum_fusion.6), channel_id=1, replica_groups=mesh['sh'=2,'sl'=2,'ctx'=2,'tx'=2,'tc'=2] {'sh','sl','ctx','tx','tc'}, use_global_device_ids=true, to_apply=%region_37.38 | all-reduce | flops 4096 | bytes 32768 | tf_op jit(solution)/shard_map/psum | solution.py:366
  1179.5 20.9 %psum.30 = f32[2,4,128]{2,1,0:T(4,128)S(1)} all-reduce(f32[2,4,128]{2,1,0:T(4,128)S(1)} %reshape.855), channel_id=1, replica_groups=mesh['sh'=2,'sl'=2,'ctx'=2,'tx'=2,'tc'=2] {'sh','sl','ctx'}, use_global_device_ids=true, to_apply=%region_32.33 | all-reduce | flops 1024 | bytes 8192 | tf_op jit(solution)/shard_map/psum | solution.py:362
  (698 shorter events, 489.4 us)
Async XLA Ops:
  7.2 70.8 %all-gather.7.cloned.1.call-start = ((), (), s32[]{:S(2)}) async-start(), calls=%async_computation.6 | async-start | bytes 3932160 | tf_op jit(solution)/shard_map/all_gather | solution.py:69
  11.7 97.4 %all-gather.9.cloned.1.call-start = ((), (), s32[]{:S(2)}) async-start(), calls=%async_computation.7 | async-start | bytes 1310720 | tf_op jit(solution)/shard_map/all_gather | solution.py:69
  12.5 272.2 %all-gather.13.cloned.1.call-start = ((), (), s32[]{:S(2)}) async-start(), calls=%async_computation.9 | async-start | bytes 5242880 | tf_op jit(solution)/shard_map/all_gather | solution.py:69
  13.8 284.7 %all-gather.11.cloned.1.call-start = ((), (), s32[]{:S(2)}) async-start(), calls=%async_computation.8 | async-start | bytes 5242880 | tf_op jit(solution)/shard_map/all_gather | solution.py:69
  16.7 480.1 %all-gather.17.cloned.1.call-start = ((), (), s32[]{:S(2)}) async-start(), calls=%async_computation.11 | async-start | bytes 5242880 | tf_op jit(solution)/shard_map/all_gather | solution.py:69
  17.1 62.5 %collective-permute-start.2 = (bf16[1,640]{1,0:T(2,128)(2,1)S(1)}, bf16[1,640]{1,0:T(2,128)(2,1)S(1)}, u32[]{:S(2)}, u32[]{:S(2)}) collective-permute-start(bf16[1,640]{1,0:T(2,128)(2,1)S(1)} %broadcast_in_dim.55), channel_id=1, source_target_pairs={{0,4},{4,0},{1,5},{5,1},{2,6},{6,2},{3,7},{7,3},{8,12},{12,8},{9,1... | collective-permute-start | bytes 3848 | tf_op jit(solution)/shard_map/ppermute | solution.py:33
  20.1 65.1 %collective-permute-start = (s32[1024]{0:T(1024)S(1)}, s32[1024]{0:T(1024)S(1)}, u32[]{:S(2)}, u32[]{:S(2)}) collective-permute-start(s32[1024]{0:T(1024)S(1)} %bitcast.363), channel_id=1, source_target_pairs={{0,4},{4,0},{1,5},{5,1},{2,6},{6,2},{3,7},{7,3},{8,12},{12,8},{9,1... | collective-permute-start | bytes 12296 | tf_op jit(solution)/shard_map/ppermute | solution.py:33
  21.2 72.9 %collective-permute-start.20 = (bf16[256,2048]{0,1:T(8,128)(2,1)}, bf16[256,2048]{0,1:T(8,128)(2,1)}, u32[]{:S(2)}, u32[]{:S(2)}) collective-permute-start(bf16[256,2048]{0,1:T(8,128)(2,1)} %convert_bitcast_fusion), channel_id=1, source_target_pairs={{0,4},{4,0},{1,5},{5,1},{2,6},{6,2},{3,7},{7,3},{8,12},{12,8},{9,1... | collective-permute-start | bytes 3145736 | tf_op jit(solution)/shard_map/ppermute | solution.py:33
  78.1 71.3 %collective-permute-start.1 = (bf16[1024,1536]{1,0:T(8,128)(2,1)}, bf16[1024,1536]{1,0:T(8,128)(2,1)}, u32[]{:S(2)}, u32[]{:S(2)}) collective-permute-start(bf16[1024,1536]{1,0:T(8,128)(2,1)} %all-gather.7.cloned.1.call-done), channel_id=1, source_target_pairs={{0,4},{4,0},{1,5},{5,1},{2,6},{6,2},{3,7},{7,3},{8,12},{12,8},{9,1... | collective-permute-start | bytes 9437192 | tf_op jit(solution)/shard_map/ppermute | solution.py:33
  94.2 412.5 %all-gather.15.cloned.1.call-start = ((), (), s32[]{:S(2)}) async-start(), calls=%async_computation.10 | async-start | bytes 5242880 | tf_op jit(solution)/shard_map/all_gather | solution.py:69
  109.1 158.1 %collective-permute-start.9 = (bf16[1024,512]{0,1:T(8,128)(2,1)}, bf16[1024,512]{0,1:T(8,128)(2,1)}, u32[]{:S(2)}, u32[]{:S(2)}) collective-permute-start(bf16[1024,512]{0,1:T(8,128)(2,1)} %all-gather.9.cloned.1.call-done), channel_id=1, source_target_pairs={{0,4},{4,0},{1,5},{5,1},{2,6},{6,2},{3,7},{7,3},{8,12},{12,8},{9,1... | collective-permute-start | bytes 3145736 | tf_op jit(solution)/shard_map/ppermute | solution.py:33
  177.1 26.4 %collective-permute-start.5 = (bf16[1024,4,128]{2,0,1:T(8,128)(2,1)}, bf16[1024,4,128]{2,0,1:T(8,128)(2,1)}, u32[]{:S(2)}, u32[]{:S(2)}) collective-permute-start(bf16[1024,4,128]{2,0,1:T(8,128)(2,1)} %fusion.50), channel_id=1, source_target_pairs={{0,4},{4,0},{1,5},{5,1},{2,6},{6,2},{3,7},{7,3},{8,12},{12,8},{9,1... | collective-permute-start | bytes 3145736 | tf_op jit(solution)/shard_map/ppermute | solution.py:33
  181.3 43.1 %collective-permute-start.6 = (bf16[1024,4,128]{2,0,1:T(8,128)(2,1)}, bf16[1024,4,128]{2,0,1:T(8,128)(2,1)}, u32[]{:S(2)}, u32[]{:S(2)}) collective-permute-start(bf16[1024,4,128]{2,0,1:T(8,128)(2,1)} %copy_bitcast_fusion.1), channel_id=1, source_target_pairs={{0,4},{4,0},{1,5},{5,1},{2,6},{6,2},{3,7},{7,3},{8,12},{12,8},{9,1... | collective-permute-start | bytes 3145736 | tf_op jit(solution)/shard_map/ppermute | solution.py:33
  272.5 26.7 %collective-permute-start.10 = (bf16[512,1024]{0,1:T(8,128)(2,1)}, bf16[512,1024]{0,1:T(8,128)(2,1)}, u32[]{:S(2)}, u32[]{:S(2)}) collective-permute-start(bf16[512,1024]{0,1:T(8,128)(2,1)} %dynamic-slice_convert_fusion.8), channel_id=1, source_target_pairs={{0,1},{1,0},{2,3},{3,2},{4,5},{5,4},{6,7},{7,6},{8,9},{9,8},{10,11... | collective-permute-start | bytes 3145736 | tf_op jit(solution)/shard_map/ppermute | solution.py:33
  277.0 27.6 %collective-permute-start.7 = (bf16[512,1024]{0,1:T(8,128)(2,1)}, bf16[512,1024]{0,1:T(8,128)(2,1)}, u32[]{:S(2)}, u32[]{:S(2)}) collective-permute-start(bf16[512,1024]{0,1:T(8,128)(2,1)} %dynamic-slice_convert_fusion.9), channel_id=1, source_target_pairs={{0,1},{1,0},{2,3},{3,2},{4,5},{5,4},{6,7},{7,6},{8,9},{9,8},{10,11... | collective-permute-start | bytes 3145736 | tf_op jit(solution)/shard_map/ppermute | solution.py:33
  284.7 93.8 %collective-permute-start.17 = (bf16[1024,2048]{1,0:T(8,128)(2,1)}, bf16[1024,2048]{1,0:T(8,128)(2,1)}, u32[]{:S(2)}, u32[]{:S(2)}) collective-permute-start(bf16[1024,2048]{1,0:T(8,128)(2,1)} %all-gather.13.cloned.1.call-done), channel_id=1, source_target_pairs={{0,4},{4,0},{1,5},{5,1},{2,6},{6,2},{3,7},{7,3},{8,12},{12,8},{9,1... | collective-permute-start | bytes 12582920 | tf_op jit(solution)/shard_map/ppermute | solution.py:33
  298.5 169.0 %collective-permute-start.16 = (bf16[1024,2048]{1,0:T(8,128)(2,1)}, bf16[1024,2048]{1,0:T(8,128)(2,1)}, u32[]{:S(2)}, u32[]{:S(2)}) collective-permute-start(bf16[1024,2048]{1,0:T(8,128)(2,1)} %all-gather.11.cloned.1.call-done), channel_id=1, source_target_pairs={{0,4},{4,0},{1,5},{5,1},{2,6},{6,2},{3,7},{7,3},{8,12},{12,8},{9,1... | collective-permute-start | bytes 12582920 | tf_op jit(solution)/shard_map/ppermute | solution.py:33
  303.1 15.2 %collective-permute-start.11 = (bf16[256,1024]{0,1:T(8,128)(2,1)}, bf16[256,1024]{0,1:T(8,128)(2,1)}, u32[]{:S(2)}, u32[]{:S(2)}) collective-permute-start(bf16[256,1024]{0,1:T(8,128)(2,1)} %dynamic-slice_convert_fusion.17), channel_id=1, source_target_pairs={{0,2},{2,0},{1,3},{3,1},{4,6},{6,4},{5,7},{7,5},{8,10},{10,8},{9,1... | collective-permute-start | bytes 1572872 | tf_op jit(solution)/shard_map/ppermute | solution.py:33
  307.7 20.2 %collective-permute-start.8 = (bf16[256,1024]{0,1:T(8,128)(2,1)}, bf16[256,1024]{0,1:T(8,128)(2,1)}, u32[]{:S(2)}, u32[]{:S(2)}) collective-permute-start(bf16[256,1024]{0,1:T(8,128)(2,1)} %dynamic-slice_convert_fusion.18), channel_id=1, source_target_pairs={{0,2},{2,0},{1,3},{3,1},{4,6},{6,4},{5,7},{7,5},{8,10},{10,8},{9,1... | collective-permute-start | bytes 1572872 | tf_op jit(solution)/shard_map/ppermute | solution.py:33
  345.7 32.9 %collective-permute-start.15 = (bf16[512,1024]{0,1:T(8,128)(2,1)}, bf16[512,1024]{0,1:T(8,128)(2,1)}, u32[]{:S(2)}, u32[]{:S(2)}) collective-permute-start(bf16[512,1024]{0,1:T(8,128)(2,1)} %maximum_select_fusion.15), channel_id=1, source_target_pairs={{0,1},{1,0},{2,3},{3,2},{4,5},{5,4},{6,7},{7,6},{8,9},{9,8},{10,11... | collective-permute-start | bytes 3145736 | tf_op jit(solution)/shard_map/ppermute | solution.py:33
  347.2 853.3 %reduce-scatter.17.cloned.1.call-start = ((), (), s32[]{:S(2)}) async-start(), calls=%async_computation.17 | async-start | bytes 5242880 | tf_op jit(solution)/shard_map/reduce_scatter | solution.py:73
  360.3 116.0 %collective-permute-start.13 = (bf16[512,1024]{0,1:T(8,128)(2,1)S(1)}, bf16[512,1024]{0,1:T(8,128)(2,1)S(1)}, u32[]{:S(2)}, u32[]{:S(2)}) collective-permute-start(bf16[512,1024]{0,1:T(8,128)(2,1)S(1)} %maximum_select_fusion.14), channel_id=1, source_target_pairs={{0,1},{1,0},{2,3},{3,2},{4,5},{5,4},{6,7},{7,6},{8,9},{9,8},{10,11... | collective-permute-start | bytes 3145736 | tf_op jit(solution)/shard_map/ppermute | solution.py:33
  516.7 15.1 %collective-permute-start.22 = (bf16[256,1024]{0,1:T(8,128)(2,1)}, bf16[256,1024]{0,1:T(8,128)(2,1)}, u32[]{:S(2)}, u32[]{:S(2)}) collective-permute-start(bf16[256,1024]{0,1:T(8,128)(2,1)} %dynamic-slice_convert_fusion.15), channel_id=1, source_target_pairs={{0,2},{2,0},{1,3},{3,1},{4,6},{6,4},{5,7},{7,5},{8,10},{10,8},{9,1... | collective-permute-start | bytes 1572872 | tf_op jit(solution)/shard_map/ppermute | solution.py:33
  519.5 22.7 %collective-permute-start.19 = (bf16[256,1024]{0,1:T(8,128)(2,1)}, bf16[256,1024]{0,1:T(8,128)(2,1)}, u32[]{:S(2)}, u32[]{:S(2)}) collective-permute-start(bf16[256,1024]{0,1:T(8,128)(2,1)} %dynamic-slice_convert_fusion.16), channel_id=1, source_target_pairs={{0,2},{2,0},{1,3},{3,1},{4,6},{6,4},{5,7},{7,5},{8,10},{10,8},{9,1... | collective-permute-start | bytes 1572872 | tf_op jit(solution)/shard_map/ppermute | solution.py:33
  558.7 14.8 %collective-permute-start.28 = (bf16[512,1024]{0,1:T(8,128)(2,1)S(1)}, bf16[512,1024]{0,1:T(8,128)(2,1)S(1)}, u32[]{:S(2)}, u32[]{:S(2)}) collective-permute-start(bf16[512,1024]{0,1:T(8,128)(2,1)S(1)} %maximum_select_fusion.17), channel_id=1, source_target_pairs={{0,1},{1,0},{2,3},{3,2},{4,5},{5,4},{6,7},{7,6},{8,9},{9,8},{10,11... | collective-permute-start | bytes 3145736 | tf_op jit(solution)/shard_map/ppermute | solution.py:33
  558.8 14.3 %collective-permute-start.25 = (bf16[256,1024]{0,1:T(8,128)(2,1)S(1)}, bf16[256,1024]{0,1:T(8,128)(2,1)S(1)}, u32[]{:S(2)}, u32[]{:S(2)}) collective-permute-start(bf16[256,1024]{0,1:T(8,128)(2,1)S(1)} %get-tuple-element.712), channel_id=1, source_target_pairs={{0,2},{2,0},{1,3},{3,1},{4,6},{6,4},{5,7},{7,5},{8,10},{10,8},{9,1... | collective-permute-start | bytes 1572872 | tf_op jit(solution)/shard_map/ppermute | solution.py:33
  573.4 18.7 %collective-permute-start.26 = (bf16[512,1024]{0,1:T(8,128)(2,1)S(1)}, bf16[512,1024]{0,1:T(8,128)(2,1)}, u32[]{:S(2)}, u32[]{:S(2)}) collective-permute-start(bf16[512,1024]{0,1:T(8,128)(2,1)S(1)} %maximum_select_fusion.16), channel_id=1, source_target_pairs={{0,1},{1,0},{2,3},{3,2},{4,5},{5,4},{6,7},{7,6},{8,9},{9,8},{10,11... | collective-permute-start | bytes 3145736 | tf_op jit(solution)/shard_map/ppermute | solution.py:33
  580.6 620.7 %reduce-scatter.9.cloned.1.call-start = ((), (), s32[]{:S(2)}) async-start(), calls=%async_computation.13 | async-start | bytes 1310720 | tf_op jit(solution)/shard_map/reduce_scatter | solution.py:73
  634.7 14.8 %collective-permute-start.32 = (bf16[256,1024]{0,1:T(8,128)(2,1)S(1)}, bf16[256,1024]{0,1:T(8,128)(2,1)S(1)}, u32[]{:S(2)}, u32[]{:S(2)}) collective-permute-start(bf16[256,1024]{0,1:T(8,128)(2,1)S(1)} %dynamic-slice_convert_fusion.12), channel_id=1, source_target_pairs={{0,2},{2,0},{1,3},{3,1},{4,6},{6,4},{5,7},{7,5},{8,10},{10,8},{9,1... | collective-permute-start | bytes 1572872 | tf_op jit(solution)/shard_map/ppermute | solution.py:33
  637.3 23.0 %collective-permute-start.30 = (bf16[256,1024]{0,1:T(8,128)(2,1)S(1)}, bf16[256,1024]{0,1:T(8,128)(2,1)S(1)}, u32[]{:S(2)}, u32[]{:S(2)}) collective-permute-start(bf16[256,1024]{0,1:T(8,128)(2,1)S(1)} %dynamic-slice_convert_fusion.13), channel_id=1, source_target_pairs={{0,2},{2,0},{1,3},{3,1},{4,6},{6,4},{5,7},{7,5},{8,10},{10,8},{9,1... | collective-permute-start | bytes 1572872 | tf_op jit(solution)/shard_map/ppermute | solution.py:33
  677.1 14.8 %collective-permute-start.36 = (bf16[512,1024]{0,1:T(8,128)(2,1)S(1)}, bf16[512,1024]{0,1:T(8,128)(2,1)S(1)}, u32[]{:S(2)}, u32[]{:S(2)}) collective-permute-start(bf16[512,1024]{0,1:T(8,128)(2,1)S(1)} %maximum_select_fusion.19), channel_id=1, source_target_pairs={{0,1},{1,0},{2,3},{3,2},{4,5},{5,4},{6,7},{7,6},{8,9},{9,8},{10,11... | collective-permute-start | bytes 3145736 | tf_op jit(solution)/shard_map/ppermute | solution.py:33
  693.4 25.6 %collective-permute-start.46 = (bf16[1024,512]{1,0:T(8,128)(2,1)S(1)}, bf16[1024,512]{1,0:T(8,128)(2,1)S(1)}, u32[]{:S(2)}, u32[]{:S(2)}) collective-permute-start(bf16[1024,512]{1,0:T(8,128)(2,1)S(1)} %convolution_convert_fusion.5), channel_id=1, source_target_pairs={{0,4},{4,0},{1,5},{5,1},{2,6},{6,2},{3,7},{7,3},{8,12},{12,8},{9,1... | collective-permute-start | bytes 3145736 | tf_op jit(solution)/shard_map/ppermute | solution.py:33
  721.4 498.9 %reduce-scatter.15.cloned.1.call-start = ((), (), s32[]{:S(2)}) async-start(), calls=%async_computation.16 | async-start | bytes 5242880 | tf_op jit(solution)/shard_map/reduce_scatter | solution.py:73
  730.9 510.5 %reduce-scatter.13.cloned.1.call-start = ((), (), s32[]{:S(2)}) async-start(), calls=%async_computation.15 | async-start | bytes 5242880 | tf_op jit(solution)/shard_map/reduce_scatter | solution.py:73
  741.0 93.8 %collective-permute-start.48 = (bf16[1024,2048]{1,0:T(8,128)(2,1)}, bf16[1024,2048]{1,0:T(8,128)(2,1)}, u32[]{:S(2)}, u32[]{:S(2)}) collective-permute-start(bf16[1024,2048]{1,0:T(8,128)(2,1)} %convolution_convert_fusion.3), channel_id=1, source_target_pairs={{0,4},{4,0},{1,5},{5,1},{2,6},{6,2},{3,7},{7,3},{8,12},{12,8},{9,1... | collective-permute-start | bytes 12582920 | tf_op jit(solution)/shard_map/ppermute | solution.py:33
  752.5 204.8 %collective-permute-start.47 = (bf16[1024,2048]{1,0:T(8,128)(2,1)}, bf16[1024,2048]{1,0:T(8,128)(2,1)}, u32[]{:S(2)}, u32[]{:S(2)}) collective-permute-start(bf16[1024,2048]{1,0:T(8,128)(2,1)} %convolution_convert_fusion.4), channel_id=1, source_target_pairs={{0,4},{4,0},{1,5},{5,1},{2,6},{6,2},{3,7},{7,3},{8,12},{12,8},{9,1... | collective-permute-start | bytes 12582920 | tf_op jit(solution)/shard_map/ppermute | solution.py:33
  845.3 402.6 %reduce-scatter.11.cloned.1.call-start = ((), (), s32[]{:S(2)}) async-start(), calls=%async_computation.14 | async-start | bytes 5242880 | tf_op jit(solution)/shard_map/reduce_scatter | solution.py:73
  952.5 26.2 %collective-permute-start.37 = (bf16[1024,4,128]{2,0,1:T(8,128)(2,1)S(1)}, bf16[1024,4,128]{2,0,1:T(8,128)(2,1)S(1)}, u32[]{:S(2)}, u32[]{:S(2)}) collective-permute-start(bf16[1024,4,128]{2,0,1:T(8,128)(2,1)S(1)} %dynamic-slice_convert_fusion.3), channel_id=1, source_target_pairs={{0,4},{4,0},{1,5},{5,1},{2,6},{6,2},{3,7},{7,3},{8,12},{12,8},{9,1... | collective-permute-start | bytes 3145736 | tf_op jit(solution)/shard_map/ppermute | solution.py:33
  956.8 40.8 %collective-permute-start.38 = (bf16[1024,4,128]{0,2,1:T(8,128)(2,1)}, bf16[1024,4,128]{0,2,1:T(8,128)(2,1)}, u32[]{:S(2)}, u32[]{:S(2)}) collective-permute-start(bf16[1024,4,128]{0,2,1:T(8,128)(2,1)} %dynamic-slice_convert_fusion.2), channel_id=1, source_target_pairs={{0,4},{4,0},{1,5},{5,1},{2,6},{6,2},{3,7},{7,3},{8,12},{12,8},{9,1... | collective-permute-start | bytes 3145736 | tf_op jit(solution)/shard_map/ppermute | solution.py:33
  966.3 289.0 %reduce-scatter.7.cloned.1.call-start = ((), (), s32[]{:S(2)}) async-start(), calls=%async_computation.12 | async-start | bytes 3932160 | tf_op jit(solution)/shard_map/reduce_scatter | solution.py:73
  1031.0 71.9 %collective-permute-start.45 = (bf16[1024,1536]{1,0:T(8,128)(2,1)}, bf16[1024,1536]{1,0:T(8,128)(2,1)}, u32[]{:S(2)}, u32[]{:S(2)}) collective-permute-start(bf16[1024,1536]{1,0:T(8,128)(2,1)} %convolution_convert_fusion), channel_id=1, source_target_pairs={{0,4},{4,0},{1,5},{5,1},{2,6},{6,2},{3,7},{7,3},{8,12},{12,8},{9,1... | collective-permute-start | bytes 9437192 | tf_op jit(solution)/shard_map/ppermute | solution.py:33
  1050.3 26.0 %collective-permute-start.23 = (bf16[256,2048]{1,0:T(8,128)(2,1)S(1)}, bf16[256,2048]{1,0:T(8,128)(2,1)S(1)}, u32[]{:S(2)}, u32[]{:S(2)}) collective-permute-start(bf16[256,2048]{1,0:T(8,128)(2,1)S(1)} %convert_element_type.424), channel_id=1, source_target_pairs={{0,2},{2,0},{1,3},{3,1},{4,6},{6,4},{5,7},{7,5},{8,10},{10,8},{9,1... | collective-permute-start | bytes 3145736 | tf_op jit(solution)/shard_map/ppermute | solution.py:33
  1054.3 33.3 %collective-permute-start.40 = (bf16[256,1024]{0,1:T(8,128)(2,1)S(1)}, bf16[256,1024]{0,1:T(8,128)(2,1)S(1)}, u32[]{:S(2)}, u32[]{:S(2)}) collective-permute-start(bf16[256,1024]{0,1:T(8,128)(2,1)S(1)} %dynamic-slice_convert_fusion.11), channel_id=1, source_target_pairs={{0,2},{2,0},{1,3},{3,1},{4,6},{6,4},{5,7},{7,5},{8,10},{10,8},{9,1... | collective-permute-start | bytes 1572872 | tf_op jit(solution)/shard_map/ppermute | solution.py:33
  1056.7 41.6 %collective-permute-start.42 = (bf16[256,1024]{0,1:T(8,128)(2,1)S(1)}, bf16[256,1024]{0,1:T(8,128)(2,1)S(1)}, u32[]{:S(2)}, u32[]{:S(2)}) collective-permute-start(bf16[256,1024]{0,1:T(8,128)(2,1)S(1)} %dynamic-slice_convert_fusion.10), channel_id=1, source_target_pairs={{0,2},{2,0},{1,3},{3,1},{4,6},{6,4},{5,7},{7,5},{8,10},{10,8},{9,1... | collective-permute-start | bytes 1572872 | tf_op jit(solution)/shard_map/ppermute | solution.py:33
  1078.6 51.6 %collective-permute-start.24 = (bf16[512,2048]{1,0:T(8,128)(2,1)}, bf16[512,2048]{1,0:T(8,128)(2,1)}, u32[]{:S(2)}, u32[]{:S(2)}) collective-permute-start(bf16[512,2048]{1,0:T(8,128)(2,1)} %maximum_select_fusion.7), channel_id=1, source_target_pairs={{0,1},{1,0},{2,3},{3,2},{4,5},{5,4},{6,7},{7,6},{8,9},{9,8},{10,11... | collective-permute-start | bytes 6291464 | tf_op jit(solution)/shard_map/ppermute | solution.py:33
  1101.2 25.0 %collective-permute-start.43 = (bf16[256,2048]{1,0:T(8,128)(2,1)S(1)}, bf16[256,2048]{1,0:T(8,128)(2,1)}, u32[]{:S(2)}, u32[]{:S(2)}) collective-permute-start(bf16[256,2048]{1,0:T(8,128)(2,1)S(1)} %convert_element_type.461), channel_id=1, source_target_pairs={{0,2},{2,0},{1,3},{3,1},{4,6},{6,4},{5,7},{7,5},{8,10},{10,8},{9,1... | collective-permute-start | bytes 3145736 | tf_op jit(solution)/shard_map/ppermute | solution.py:33
  1130.2 83.0 %collective-permute-start.44 = (bf16[512,2048]{1,0:T(8,128)(2,1)}, bf16[512,2048]{1,0:T(8,128)(2,1)}, u32[]{:S(2)}, u32[]{:S(2)}) collective-permute-start(bf16[512,2048]{1,0:T(8,128)(2,1)} %maximum_select_fusion.13), channel_id=1, source_target_pairs={{0,1},{1,0},{2,3},{3,2},{4,5},{5,4},{6,7},{7,6},{8,9},{9,8},{10,11... | collective-permute-start | bytes 6291464 | tf_op jit(solution)/shard_map/ppermute | solution.py:33
  1200.5 20.3 %collective-permute-start.49 = (bf16[256,2048]{1,0:T(8,128)(2,1)}, bf16[256,2048]{1,0:T(8,128)(2,1)S(1)}, u32[]{:S(2)}, u32[]{:S(2)}) collective-permute-start(bf16[256,2048]{1,0:T(8,128)(2,1)} %reduce-scatter.17.cloned.1.call-done), channel_id=1, source_target_pairs={{0,4},{4,0},{1,5},{5,1},{2,6},{6,2},{3,7},{7,3},{8,12},{12,8},{9,1... | collective-permute-start | bytes 3145736 | tf_op jit(solution)/shard_map/ppermute | solution.py:33
  (187 other events, 3138.5 us)
Sparse Core Ops, SparseCore 0:
  11.8 66.1 all-gather.6
  80.2 28.8 all-gather.8
  111.2 79.0 all-gather.12
  192.3 79.2 all-gather.10
  273.0 79.0 all-gather.16
  354.2 78.7 all-gather.14
  580.7 75.5 reduce-scatter.16
  721.5 25.8 reduce-scatter.8
  749.7 75.4 reduce-scatter.14
  845.5 75.4 reduce-scatter.12
  966.4 75.2 reduce-scatter.10
  1111.6 58.3 reduce-scatter.6
where the time goes:
time: 1270 us
  waiting for transfers between devices  507 us (40%)
  matrix products  314 us (25%)
  other arithmetic  156 us (12%)
  local copies, waits for them, and re-layouts  149 us (12%)
  blocking collectives  74.8 us (6%)
  starting transfers between devices  46.2 us (4%)
  between operations  16.9 us (1%)
    ppermute x50, waiting for transfers between devices, swap(): return lax.ppermute(value, axis, [(0, 1), (1, 0)])  451 us
    dot_general x30, matrix products, dot(): lax.dot_general(a, b, (((ca,), (cb,)), ((), ())), preferred_element_type=...  211 us
    unnamed x333, local copies, waits for them, and re-layouts  74.3 us
    all_gather x6, waiting for transfers between devices, gather_z(): return lax.all_gather(value, SHARD, axis=0, tiled=True)  55.7 us
    ppermute x50, starting transfers between devices, swap(): return lax.ppermute(value, axis, [(0, 1), (1, 0)])  45.2 us
    psum x1, blocking collectives, shards(): lax.psum(jnp.stack([whole(*grad_attn_gain), whole(*grad_ffn_gain)]), (SH,...  41 us
    sub x8, other arithmetic, adam_step(): weight - learn_rate * (first_hat / (jnp.sqrt(second_hat) + adam_eps) + de...  30.1 us
  transfers between devices with their start and end apart: 62, of which 29 were waited for; matrix products, arithmetic and copies ran while one was open for 46% of the time, Pallas kernels for 0%

commit v1 on v0

v1 whole, which is shorter than its diff:
```python
import functools
import math

import jax
import jax.numpy as jnp
from jax import lax
from jax.experimental import pallas as pl
from jax.experimental.pallas import tpu as pltpu
from jax.sharding import Mesh
from jax.sharding import PartitionSpec as P

DOCS = 3
rope_base = 500000.0
norm_eps = 1e-06
learn_rate = 0.3
beta_one = 0.9
beta_two = 0.95
adam_eps = 1e-08
decay_rate = 0.1
step_count = 2
masked_score = -1e30

f32 = jnp.float32
b16 = jnp.bfloat16
i32 = jnp.int32

SH, SL, CX, TX, TC = "sh", "sl", "ctx", "tx", "tc"
SHARD = (SH, SL)
TENSOR = (TX, TC)
PLANE = (CX, TX, TC)


def dot(a, b, ca, cb):
    return lax.dot_general(a, b, (((ca,), (cb,)), ((), ())), preferred_element_type=f32)


def swap(value, axis):
    return lax.ppermute(value, axis, [(0, 1), (1, 0)])


def pair(mine, other, axis, at=0):
    return jnp.where(
        lax.axis_index(axis) == 0,
        jnp.concatenate([mine, other], at),
        jnp.concatenate([other, mine], at),
    )


def gather_axis(value, axis):
    if lax.axis_size(axis) == 2:
        return pair(value, swap(value, axis), axis)
    return lax.all_gather(value, axis, axis=0, tiled=True)


def sum_axis(value, axis):
    if lax.axis_size(axis) == 2:
        return value + swap(value, axis)
    return lax.psum(value, axis)


def plane_sum(value):
    return sum_axis(sum_axis(sum_axis(value, TC), TX), CX)


def tie(*values):
    return lax.optimization_barrier(values)


def part(value, index, at):
    return lax.dynamic_index_in_dim(value, index, at, keepdims=False)


def rows_all(value):
    return gather_axis(gather_axis(value, TX), TC)


def spread(value, axis):
    if lax.axis_size(TX) == 2:
        half = value.shape[0] // 2
        over_x = swap(value, TX)
        over_y = swap(value, axis)
        near = swap(over_y[:half], TX)
        far = swap(over_x[half:], axis)
        mine = [value, over_x, over_y, near, far]
    else:
        line = lax.all_gather(value, TX, axis=0, tiled=True)
        mine = [line, swap(line, axis)]
    return mine, [swap(block, TC) for block in mine]


def joined(groups):
    return [jnp.concatenate(blocks, 0) for blocks in groups]


def across(mine, theirs):
    return (mine + swap(theirs.astype(b16), TC).astype(f32)).astype(b16)


def collect(both, axis):
    count = lax.axis_size(TX)
    block = both.shape[0] // (2 * count)
    if count == 2:
        half = block // 2
        near = swap(both[3 * block : 3 * block + half], TX)
        far = swap(both[3 * block + half :], axis)
        over_x = jnp.concatenate(
            [both[block : block + half], both[block + half : 2 * block] + far], 0
        )
        over_y = jnp.concatenate(
            [both[2 * block : 2 * block + half] + near, both[2 * block + half : 3 * block]], 0
        )
        return (
            both[:block].astype(f32)
            + swap(over_x, TX).astype(f32)
            + swap(over_y, axis).astype(f32)
        )
    line = both[: count * block] + swap(both[count * block :], axis)
    return lax.psum_scatter(line, TX, scatter_dimension=0, tiled=True).astype(f32)


def block_places(axis):
    count = lax.axis_size(TX)
    spot = jnp.arange(4 * count, dtype=i32)
    side = (spot // (2 * count)) ^ lax.axis_index(axis)
    core = (spot // count % 2) ^ lax.axis_index(TC)
    along = spot % count
    if count == 2:
        along = along ^ lax.axis_index(TX)
    return (core * 2 + side) * count + along


def params(steps):
    return pltpu.CompilerParams(
        dimension_semantics=("arbitrary",) * steps, vmem_limit_bytes=40 * 1024 * 1024
    )


def lasting(us):
    return pl.CostEstimate(flops=0, transcendentals=0, bytes_accessed=int(us * 0.5e6))


def upright(row, columns):
    return jnp.transpose(jnp.broadcast_to(row, (columns, row.shape[1])))


def row_sums(value):
    return jnp.sum(jnp.transpose(value), axis=0, keepdims=True)


def project_body(side, local, remote, weight, raw, squares):
    half = pl.num_programs(0) // 2
    mine = (pl.program_id(0) // half) == side[0]
    raw[...] = dot(jnp.where(mine, local[...], remote[...]), weight[...], 1, 0)
    width = raw.shape[1] // 3
    for which in range(2):
        total = jnp.zeros((raw.shape[0], 128), f32)
        for at in range(which * width, (which + 1) * width, 128):
            total += raw[:, at : at + 128] * raw[:, at : at + 128]
        squares[which : which + 1, :] = row_sums(total)


def project(side, local, remote, weight):
    rows, width = local.shape
    columns = weight.shape[1]
    step = min(256, rows)
    half = rows // step
    tokens = pl.BlockSpec((step, width), lambda i, side: (i % half, 0))
    return pl.pallas_call(
        project_body,
        grid_spec=pltpu.PrefetchScalarGridSpec(
            num_scalar_prefetch=1,
            grid=(2 * half,),
            in_specs=[
                tokens,
                tokens,
                pl.BlockSpec((width, columns), lambda i, side: (0, 0)),
            ],
            out_specs=[
                pl.BlockSpec((step, columns), lambda i, side: (i, 0)),
                pl.BlockSpec((2, step), lambda i, side: (0, i)),
            ],
        ),
        out_shape=[
            jax.ShapeDtypeStruct((2 * rows, columns), f32),
            jax.ShapeDtypeStruct((2, 2 * rows), f32),
        ],
        compiler_params=params(1),
        cost_estimate=lasting(12),
    )(side, local, remote, weight)


def turn(value, cosine, sine):
    return value * cosine + pltpu.roll(value, value.shape[1] // 2, 1) * sine


def turn_back(value, cosine, sine):
    return value * cosine + pltpu.roll(value * sine, value.shape[1] // 2, 1)


def prepare_body(raw, inverse, gain, cosine, sine, query, key, val):
    width = query.shape[1]
    size = cosine.shape[1]
    for which, out in ((0, query), (1, key)):
        scale = upright(inverse[which : which + 1, :], size)
        for at in range(0, width, size):
            unit = raw[:, which * width + at : which * width + at + size] * scale
            out[:, at : at + size] = turn(
                unit * gain[which : which + 1, at : at + size], cosine[...], sine[...]
            ).astype(b16)
    val[...] = raw[:, 2 * width :].astype(b16)


def prepare(raw, inverse, gain, cosine, sine):
    rows, width = raw.shape[0], raw.shape[1] // 3
    size = cosine.shape[1]
    step = min(256, rows)
    by_row = lambda columns: pl.BlockSpec((step, columns), lambda i: (i, 0))
    return pl.pallas_call(
        prepare_body,
        grid=(rows // step,),
        in_specs=[
            by_row(3 * width),
            pl.BlockSpec((2, step), lambda i: (0, i)),
            pl.BlockSpec((2, width), lambda i: (0, 0)),
            by_row(size),
            by_row(size),
        ],
        out_specs=[by_row(width)] * 3,
        out_shape=[jax.ShapeDtypeStruct((rows, width), b16)] * 3,
        compiler_params=params(1),
        cost_estimate=lasting(3),
    )(raw, inverse, gain, cosine, sine)


def allowed(start, first_key, first_query, shape):
    keys = first_key + lax.broadcasted_iota(i32, shape, 0)
    queries = first_query + lax.broadcasted_iota(i32, shape, 1)
    return (keys >= start) & (keys <= queries)


def forward_body(span, spot, low, query, keys, values, start, out, log_total):
    i = pl.program_id(1)
    rows, size = query.shape
    scale = 1.0 / math.sqrt(size)

    def step(j, carry):
        peak, total, summed = carry
        at = pl.multiple_of(j * span, span)
        scores = dot(keys[pl.ds(at, span), :], query[...], 1, 1) * scale
        scores = jnp.where(allowed(start[...], at, i * rows, scores.shape), scores, masked_score)
        new_peak = jnp.maximum(peak, jnp.max(scores, axis=0, keepdims=True))
        shrink = jnp.exp(peak - new_peak)
        exponent = jnp.exp(scores - new_peak)
        total = total * shrink + jnp.sum(exponent, axis=0, keepdims=True)
        summed = summed * shrink + dot(values[pl.ds(at, span), :], exponent.astype(b16), 0, 0)
        return new_peak, total, summed

    begin = (
        jnp.full((1, rows), masked_score, f32),
        jnp.zeros((1, rows), f32),
        jnp.zeros((size, rows), f32),
    )
    last = ((i + 1) * rows + span - 1) // span
    peak, total, summed = lax.fori_loop(low[i], last, step, begin)
    out[...] = jnp.transpose(summed / total).astype(b16)
    log_total[0] = peak + jnp.log(total)


def flash_forward(query, keys, values, start, spot, block, size):
    rows, width = query.shape
    heads = width // size
    blocks = rows // block
    span = min(512, rows)
    low = start.reshape(blocks, block)[:, 0] // span
    return pl.pallas_call(
        functools.partial(forward_body, span),
        grid_spec=pltpu.PrefetchScalarGridSpec(
            num_scalar_prefetch=2,
            grid=(heads, blocks),
            in_specs=[
                pl.BlockSpec((block, size), lambda h, i, spot, low: (i, h)),
                pl.BlockSpec((rows, size), lambda h, i, spot, low: (0, h)),
                pl.BlockSpec((rows, size), lambda h, i, spot, low: (0, h)),
                pl.BlockSpec((1, block), lambda h, i, spot, low: (0, i)),
            ],
            out_specs=[
                pl.BlockSpec((block, size), lambda h, i, spot, low: (spot[i], h)),
                pl.BlockSpec((1, 1, block), lambda h, i, spot, low: (h, 0, i)),
            ],
        ),
        out_shape=[
            jax.ShapeDtypeStruct((rows, width), b16),
            jax.ShapeDtypeStruct((heads, 1, rows), f32),
        ],
        compiler_params=params(2),
        cost_estimate=lasting(18),
    )(spot, low, query, keys, values, start[None])


def backward_body(
    span, spot, low, query, keys, values, start, log_total, grad, out, d_query, d_keys, d_values
):
    i = pl.program_id(1)
    rows, size = query.shape
    scale = 1.0 / math.sqrt(size)

    @pl.when(i == 0)
    def _():
        d_keys[...] = jnp.zeros_like(d_keys)
        d_values[...] = jnp.zeros_like(d_values)

    delta = row_sums(grad[...].astype(f32) * out[...].astype(f32))

    def step(j, summed):
        at = pl.multiple_of(j * span, span)
        here = pl.ds(at, span)
        scores = dot(keys[here, :], query[...], 1, 1) * scale
        mask = allowed(start[...], at, i * rows, scores.shape)
        soft = jnp.where(mask, jnp.exp(scores - log_total[0]), 0.0)
        d_soft = dot(values[here, :], grad[...], 1, 1)
        d_scores = (soft * (d_soft - delta) * scale).astype(b16)
        d_values[here, :] += dot(soft.astype(b16), grad[...], 1, 0)
        d_keys[here, :] += dot(d_scores, query[...], 1, 0)
        return summed + dot(keys[here, :], d_scores, 0, 0)

    last = ((i + 1) * rows + span - 1) // span
    summed = lax.fori_loop(low[i], last, step, jnp.zeros((size, rows), f32))
    d_query[...] = jnp.transpose(summed)


def flash_backward(query, keys, values, start, log_total, grad, out, spot, block, size):
    rows, width = query.shape
    heads = width // size
    blocks = rows // block
    span = min(512, rows)
    low = start.reshape(blocks, block)[:, 0] // span
    natural = pl.BlockSpec((block, size), lambda h, i, spot, low: (i, h))
    moved = pl.BlockSpec((block, size), lambda h, i, spot, low: (spot[i], h))
    full = pl.BlockSpec((rows, size), lambda h, i, spot, low: (0, h))
    return pl.pallas_call(
        functools.partial(backward_body, span),
        grid_spec=pltpu.PrefetchScalarGridSpec(
            num_scalar_prefetch=2,
            grid=(heads, blocks),
            in_specs=[
                natural,
                full,
                full,
                pl.BlockSpec((1, block), lambda h, i, spot, low: (0, i)),
                pl.BlockSpec((1, 1, block), lambda h, i, spot, low: (h, 0, i)),
                moved,
                moved,
            ],
            out_specs=[natural, full, full],
        ),
        out_shape=[jax.ShapeDtypeStruct((rows, width), f32)] * 3,
        compiler_params=params(2),
        cost_estimate=lasting(22),
    )(spot, low, query, keys, values, start[None], log_total, grad, out)


def turned_sums_body(raw, inverse, gain, cosine, sine, d_query, d_key, sums, gains):
    width = d_query.shape[1]
    size = cosine.shape[1]

    @pl.when(pl.program_id(0) == 0)
    def _():
        gains[...] = jnp.zeros_like(gains)

    for which, grad in ((0, d_query), (1, d_key)):
        row = jnp.zeros((raw.shape[0], size), f32)
        scale = upright(inverse[which : which + 1, :], size)
        for at in range(0, width, size):
            unit = raw[:, which * width + at : which * width + at + size] * scale
            product = turn_back(grad[:, at : at + size], cosine[...], sine[...]) * unit
            gains[which : which + 1, at : at + size] += jnp.sum(product, axis=0, keepdims=True)
            row += product * gain[which : which + 1, at : at + size]
        sums[which : which + 1, :] = row_sums(row)


def turned_sums(raw, inverse, gain, cosine, sine, d_query, d_key):
    rows, width = d_query.shape
    size = cosine.shape[1]
    step = min(256, rows)
    by_row = lambda columns: pl.BlockSpec((step, columns), lambda i: (i, 0))
    return pl.pallas_call(
        turned_sums_body,
        grid=(rows // step,),
        in_specs=[
            by_row(3 * width),
            pl.BlockSpec((2, step), lambda i: (0, i)),
            pl.BlockSpec((2, width), lambda i: (0, 0)),
            by_row(size),
            by_row(size),
            by_row(width),
            by_row(width),
        ],
        out_specs=[
            pl.BlockSpec((2, step), lambda i: (0, i)),
            pl.BlockSpec((2, width), lambda i: (0, 0)),
        ],
        out_shape=[
            jax.ShapeDtypeStruct((2, rows), f32),
            jax.ShapeDtypeStruct((2, width), f32),
        ],
        compiler_params=params(1),
        cost_estimate=lasting(4),
    )(raw, inverse, gain, cosine, sine, d_query, d_key)


def raw_grads_body(
    spot, raw, inverse, gain, cosine, sine, d_query, d_key, d_val, means, out, moved
):
    width = d_query.shape[1]
    size = cosine.shape[1]
    for which, grad in ((0, d_query), (1, d_key)):
        scale = upright(inverse[which : which + 1, :], size)
        mean = upright(means[which : which + 1, :], size)
        for at in range(0, width, size):
            place = slice(which * width + at, which * width + at + size)
            unit = raw[:, place] * scale
            scaled = (
                turn_back(grad[:, at : at + size], cosine[...], sine[...])
                * gain[which : which + 1, at : at + size]
            )
            out[:, place] = (scale * (scaled - unit * mean)).astype(b16)
    out[:, 2 * width :] = d_val[...].astype(b16)
    moved[...] = out[...]


def raw_grads(raw, inverse, gain, cosine, sine, d_query, d_key, d_val, means, spot, block):
    rows, width = d_query.shape
    size = cosine.shape[1]
    by_row = lambda columns: pl.BlockSpec((block, columns), lambda i, spot: (i, 0))
    in_line = pl.BlockSpec((2, block), lambda i, spot: (0, i))
    return pl.pallas_call(
        raw_grads_body,
        grid_spec=pltpu.PrefetchScalarGridSpec(
            num_scalar_prefetch=1,
            grid=(rows // block,),
            in_specs=[
                by_row(3 * width),
                in_line,
                pl.BlockSpec((2, width), lambda i, spot: (0, 0)),
                by_row(size),
                by_row(size),
                by_row(width),
                by_row(width),
                by_row(width),
                in_line,
            ],
            out_specs=[
                by_row(3 * width),
                pl.BlockSpec((block, 3 * width), lambda i, spot: (spot[i], 0)),
            ],
        ),
        out_shape=[jax.ShapeDtypeStruct((rows, 3 * width), b16)] * 2,
        compiler_params=params(1),
        cost_estimate=lasting(5),
    )(spot, raw, inverse, gain, cosine, sine, d_query, d_key, d_val, means)


def ffn_forward_body(count, *refs):
    blocks, (w_gate, w_up, full, gate, up, act) = refs[:count], refs[count:]

    @pl.when(pl.program_id(0) == 0)
    def _():
        at = 0
        for block in blocks:
            full[at : at + block.shape[0], :] = block[...]
            at += block.shape[0]

    gate_pre = dot(full[...], w_gate[...], 1, 0)
    up_pre = dot(full[...], w_up[...], 1, 0)
    gate[...] = gate_pre.astype(b16)
    up[...] = up_pre.astype(b16)
    act[...] = (gate_pre * jax.nn.sigmoid(gate_pre) * up_pre).astype(b16)


def ffn_forward(blocks, w_both):
    rows = sum(block.shape[0] for block in blocks)
    width, columns = w_both.shape
    step = min(256, columns // 2)
    count = columns // 2 // step
    out = pl.BlockSpec((rows, step), lambda j: (0, j))
    hidden = jax.ShapeDtypeStruct((rows, columns // 2), b16)
    return pl.pallas_call(
        functools.partial(ffn_forward_body, len(blocks)),
        grid=(count,),
        in_specs=[pl.BlockSpec(block.shape, lambda j: (0, 0)) for block in blocks]
        + [
            pl.BlockSpec((width, step), lambda j: (0, j)),
            pl.BlockSpec((width, step), lambda j: (0, j + count)),
        ],
        out_specs=[pl.BlockSpec((rows, width), lambda j: (0, 0)), out, out, out],
        out_shape=[jax.ShapeDtypeStruct((rows, width), b16), hidden, hidden, hidden],
        compiler_params=params(1),
        cost_estimate=lasting(10),
    )(*blocks, w_both, w_both)


def ffn_backward_body(grad, w_down, gate, up, d_gate, d_up):
    d_act = dot(grad[...], w_down[...], 1, 0)
    gate_pre, up_pre = gate[...].astype(f32), up[...].astype(f32)
    sigmoid = jax.nn.sigmoid(gate_pre)
    d_gate[...] = (d_act * up_pre * sigmoid * (1.0 + gate_pre * (1.0 - sigmoid))).astype(b16)
    d_up[...] = (d_act * gate_pre * sigmoid).astype(b16)


def ffn_backward(grad, w_down, gate, up):
    rows, width = grad.shape
    columns = w_down.shape[1]
    step = min(256, columns)
    out = pl.BlockSpec((rows, step), lambda j: (0, j))
    return pl.pallas_call(
        ffn_backward_body,
        grid=(columns // step,),
        in_specs=[
            pl.BlockSpec((rows, width), lambda j: (0, 0)),
            pl.BlockSpec((width, step), lambda j: (0, j)),
            out,
            out,
        ],
        out_specs=[out, out],
        out_shape=[jax.ShapeDtypeStruct((rows, columns), b16)] * 2,
        compiler_params=params(1),
        cost_estimate=lasting(6),
    )(grad, w_down, gate, up)


def ffn_residual_body(d_gate, d_up, w_gate, w_up, *rest):
    value = dot(d_gate[...], w_gate[...], 1, 1) + dot(d_up[...], w_up[...], 1, 1)
    if len(rest) == 2:
        value += rest[0][...].astype(f32)
    rest[-1][...] = value.astype(b16)


def ffn_residual(d_gate, d_up, w_both, *received):
    rows, columns = d_gate.shape
    width = w_both.shape[0]
    step = min(256, width)
    full = pl.BlockSpec((rows, columns), lambda j: (0, 0))
    out = pl.BlockSpec((rows, step), lambda j: (0, j))
    return pl.pallas_call(
        ffn_residual_body,
        grid=(width // step,),
        in_specs=[
            full,
            full,
            pl.BlockSpec((step, columns), lambda j: (j, 0)),
            pl.BlockSpec((step, columns), lambda j: (j, 1)),
        ]
        + [out] * len(received),
        out_specs=out,
        out_shape=jax.ShapeDtypeStruct((rows, width), b16),
        compiler_params=params(1),
        cost_estimate=lasting(9),
    )(d_gate, d_up, w_both, w_both, *received)


def flip_body(value, out):
    out[...] = jnp.transpose(value[...])


def flip(value):
    rows, columns = value.shape
    step = min(256, columns)
    return pl.pallas_call(
        flip_body,
        grid=(columns // step,),
        in_specs=[pl.BlockSpec((rows, step), lambda i: (0, i))],
        out_specs=pl.BlockSpec((step, rows), lambda i: (i, 0)),
        out_shape=jax.ShapeDtypeStruct((columns, rows), value.dtype),
        compiler_params=params(1),
    )(value)


def adam_step(weight, first_moment, second_moment, gradient):
    new_first = beta_one * first_moment + (1.0 - beta_one) * gradient
    new_second = beta_two * second_moment + (1.0 - beta_two) * gradient * gradient
    first_hat = new_first / (1.0 - beta_one**step_count)
    second_hat = new_second / (1.0 - beta_two**step_count)
    updated = weight - learn_rate * (
        first_hat / (jnp.sqrt(second_hat) + adam_eps) + decay_rate * weight
    )
    return (updated, new_first, new_second)


def assemble_body(flags, mine, theirs, out):
    own = (pl.program_id(0) // flags[1]) == flags[0]
    out[0] = jnp.where(own, mine[...], theirs[...]).astype(f32)


def assemble(mine, theirs, block):
    count = lax.axis_size(TX)
    width = mine.shape[1]
    shift = lax.axis_index(TX) if count == 2 else jnp.zeros((), i32)
    flags = jnp.stack([lax.axis_index(TC), jnp.full((), count, i32), shift])
    here = pl.BlockSpec((block, width), lambda i, flags: ((i % count) ^ flags[2], 0))
    return pl.pallas_call(
        assemble_body,
        grid_spec=pltpu.PrefetchScalarGridSpec(
            num_scalar_prefetch=1,
            grid=(2 * count,),
            in_specs=[here, here],
            out_specs=pl.BlockSpec((1, block, width), lambda i, flags: (0, i, 0)),
        ),
        out_shape=jax.ShapeDtypeStruct((1, 2 * count * block, width), f32),
        compiler_params=params(1),
        cost_estimate=lasting(5),
    )(flags, mine, theirs)


def over_chips(value):
    if lax.axis_size(TX) == 2:
        return jnp.concatenate([value, swap(value, TX)], 0)
    return lax.all_gather(value, TX, axis=0, tiled=True)


def adam_body(turned, flag, weight, first, second, own, other, grad, updated, mean, square):
    value = jnp.where(pl.program_id(0) == flag[0], own[...].astype(f32), other[...].astype(f32))
    if turned:
        value = jnp.transpose(value)
    grad[...] = value
    updated[...], mean[...], square[...] = adam_step(
        weight[...], first[...], second[...], value
    )


def adam(weight, first, second, own, other, flag, turned=False, column=0):
    rows, columns = weight.shape
    if turned:
        half = rows // 2
        step = min(256, half)
        count = half // step
        mine = pl.BlockSpec((step, columns), lambda j, i, flag: (j * count + i, 0))
        halves = pl.BlockSpec((columns, step), lambda j, i, flag: (0, i))
    else:
        half = columns // 2
        step = min(128, rows)
        count = rows // step
        mine = pl.BlockSpec((step, half), lambda j, i, flag: (i, j))
        halves = pl.BlockSpec((step, half), lambda j, i, flag: (i, column))
    return pl.pallas_call(
        functools.partial(adam_body, turned),
        grid_spec=pltpu.PrefetchScalarGridSpec(
            num_scalar_prefetch=1,
            grid=(2, count),
            in_specs=[mine] * 3 + [halves] * 2,
            out_specs=[mine] * 4,
        ),
        out_shape=[jax.ShapeDtypeStruct(weight.shape, f32)] * 4,
        compiler_params=params(2),
        cost_estimate=lasting(weight.size * 8e-6),
    )(flag, weight, first, second, own, other)


def row_mean(a, b):
    return jnp.mean(a * b, axis=1, keepdims=True)


def shards(tokens, cotangent, segment_ids, *state):
    masters, first_moments, second_moments = state[:11], state[11:22], state[22:33]
    inputs = tokens[0]
    docs_here = segment_ids[0]
    rows, width = inputs.shape
    ring = lax.axis_size(SHARD)
    teams = lax.axis_size(TENSOR)
    y = lax.axis_index(CX)
    piece = masters[0].shape[0]
    heads_here = masters[7].shape[0]
    head_piece = masters[7].shape[1]
    size = head_piece * ring * 2
    wide = heads_here * size // 2
    hidden = masters[4].shape[1] // 2
    block = rows // teams
    length = 2 * rows
    my_block = lax.axis_index(TC) * lax.axis_size(TX) + lax.axis_index(TX)

    def my_rows(value):
        return lax.dynamic_slice_in_dim(value, my_block * block, block, 0)

    docs_all = gather_axis(docs_here, CX)
    gains = jnp.concatenate([gain.astype(b16).reshape(-1) for gain in masters[7:]])[None]
    gains = gather_axis(gather_axis(gather_axis(gains, CX), SL), SH).astype(f32)
    gains, docs_all, inputs, *first = tie(gains, docs_all, inputs, *masters[:7])

    def columns_of(weight, index, count):
        return lax.dynamic_slice_in_dim(weight, index * count, count, 1).astype(b16)

    def over_ctx(weights, count):
        mine, theirs = [
            jnp.concatenate([columns_of(w, index, count) for w in weights], axis=1)
            for index in (y, 1 - y)
        ]
        return mine, swap(theirs, CX)

    def over_shard(value):
        return lax.all_gather(value, SHARD, axis=0, tiled=True)

    mine, theirs = over_ctx(first[:3] + [flip(first[3].astype(b16))], wide)
    theirs, local_rows = tie(theirs, my_rows(inputs))
    columns = pair(mine, theirs, CX)
    w_qkv, w_out = over_shard(columns[:, : 3 * wide]), columns[:, 3 * wide :]

    remote, gate_w, up_w, down_w = tie(swap(local_rows, CX), *first[4:])
    remote = gather_axis(remote, TX)
    gate_w = pair(*over_ctx([gate_w], hidden), CX)
    remote, gate_w = tie(remote, gate_w)
    remote = gather_axis(remote, TC)
    w_qkv, remote, w_out, gate_w = tie(w_qkv, remote, w_out, gate_w)
    w_out = over_shard(w_out)
    up_w = pair(*over_ctx([up_w], hidden), CX)
    down_w = pair(*over_ctx([flip(down_w.astype(b16))], hidden), CX)

    count = heads_here * head_piece
    head_gain = jnp.stack(
        [
            part(
                jnp.transpose(
                    gains[:, which * count : (which + 1) * count].reshape(
                        ring * 2, heads_here, head_piece
                    ),
                    (1, 0, 2),
                ).reshape(2, wide),
                y,
                0,
            )
            for which in range(2)
        ]
    )
    attn_gain = gains[:, 2 * count : 2 * count + piece].reshape(1, width)
    ffn_gain = gains[:, 2 * count + piece :].reshape(1, width)

    doc_range = jnp.arange(DOCS, dtype=i32)
    counts = jnp.sum((docs_all[:, None] == doc_range[None, :]).astype(i32), axis=0)
    starts = jnp.cumsum(counts) - counts
    own_start = jnp.sum(
        jnp.where(docs_all[:, None] == doc_range[None, :], starts[None, :], 0), axis=1
    )
    positions = jnp.arange(length, dtype=i32) - own_start
    frequencies = rope_base ** (-(jnp.arange(size // 2, dtype=f32) * 2.0) / size)
    angles = positions.astype(f32)[:, None] * frequencies[None, :]
    cosine, sine = jnp.cos(angles), jnp.sin(angles)
    cosine = jnp.concatenate([cosine, cosine], axis=1)
    sine = jnp.concatenate([-sine, sine], axis=1)

    raw, squares = project(y[None], inputs, remote, w_qkv)
    inverse = lax.rsqrt(plane_sum(squares) / width + norm_eps)
    query, key, val = prepare(raw, inverse, head_gain, cosine, sine)
    query, w_out, gate_w, up_w = tie(query, w_out, gate_w, up_w)
    w_both = over_shard(jnp.concatenate([gate_w, up_w], axis=1))
    spot = block_places(CX)
    attended, log_total = flash_forward(query, key, val, own_start, spot, block, size)
    group = length // 2
    branch = collect(
        across(dot(attended[:group], w_out, 1, 1), dot(attended[group:], w_out, 1, 1)), CX
    )
    branch_inv = lax.rsqrt(row_mean(branch, branch) + norm_eps)
    branch_unit = branch * branch_inv
    residual = my_rows(inputs).astype(f32) + branch_unit * attn_gain
    res, w_both, down_w = tie(residual.astype(b16), w_both, down_w)
    w_down = over_shard(down_w)
    res = spread(res, CX)

    res, gate_pre, up_pre, activated = zip(*[ffn_forward(blocks, w_both) for blocks in res])
    *activated, w_down = tie(*activated, w_down)
    ffn_out = collect(across(*[dot(a, w_down, 1, 1) for a in activated]), CX)
    ffn_inv = lax.rsqrt(row_mean(ffn_out, ffn_out) + norm_eps)
    ffn_unit = ffn_out * ffn_inv
    grad_out = my_rows(cotangent[0]).astype(f32)
    scaled_out = grad_out * ffn_gain
    d_ffn = joined(
        spread(
            (ffn_inv * (scaled_out - ffn_unit * row_mean(scaled_out, ffn_unit))).astype(b16), CX
        )
    )
    grad_ffn_gain = jnp.sum(grad_out * ffn_unit, axis=0)
    block_rows = (residual + ffn_unit * ffn_gain).astype(b16)

    def both(left, right):
        return (dot(left[0], right[0], 0, 0) + dot(left[1], right[1], 0, 0)).astype(b16)

    def to_shard(partial):
        return lax.psum_scatter(partial, SHARD, scatter_dimension=0, tiled=True)

    def to_owner(summed):
        summed = summed.reshape(2, piece, -1)
        return part(summed, y, 0), swap(part(summed, 1 - y, 0), CX)

    *d_ffn, block_rows = tie(*d_ffn, block_rows)
    block_rows = over_chips(block_rows)
    grad_down = both(d_ffn, activated)
    grad_down, *d_ffn = tie(grad_down, *d_ffn)
    grad_down = to_shard(grad_down)
    d_gate, d_up = zip(
        *[ffn_backward(d, w_down, g, u) for d, g, u in zip(d_ffn, gate_pre, up_pre)]
    )
    grad_gate = both(res, d_gate)
    grad_gate = to_shard(grad_gate)
    both_ffn = ffn_residual(
        d_gate[0], d_up[0], w_both, swap(ffn_residual(d_gate[1], d_up[1], w_both), TC)
    )
    both_ffn, grad_down, block_rows, *d_up = tie(both_ffn, grad_down, block_rows, *d_up)
    back_ffn = collect(both_ffn, CX)
    block_theirs = swap(block_rows, TC)
    grad_upward = both(res, d_up)
    grad_res = grad_out + back_ffn
    scaled_res = grad_res * attn_gain
    d_branch = (
        branch_inv * (scaled_res - branch_unit * row_mean(scaled_res, branch_unit))
    ).astype(b16)
    d_branch, grad_upward = tie(d_branch, grad_upward)
    grad_upward = to_shard(grad_upward)
    grad_attn_gain = jnp.sum(grad_res * branch_unit, axis=0)
    triple = lambda i: (masters[i], first_moments[i], second_moments[i])

    *d_branch, grad_gate, grad_down, block_theirs = tie(
        *joined(spread(d_branch, CX)), grad_gate, grad_down, block_theirs
    )
    down_halves, gate_halves = to_owner(grad_down), to_owner(grad_gate)
    d_att = jnp.concatenate([dot(d, w_out, 1, 0).astype(b16) for d in d_branch], 0)
    grad_out_w = both(d_branch, [attended[:group], attended[group:]])
    d_att, grad_out_w = tie(d_att, grad_out_w)
    d_query, d_key, d_val = flash_backward(
        query, key, val, own_start, log_total, d_att, attended, spot, block, size
    )
    grad_out_w = to_shard(grad_out_w)
    d_query, grad_upward, *turned = tie(d_query, grad_upward, *down_halves, *gate_halves)
    down_halves, gate_halves = turned[:2], turned[2:]
    sums, grad_heads = turned_sums(raw, inverse, head_gain, cosine, sine, d_query, d_key)
    plane_sums = plane_sum(
        jnp.concatenate([sums, grad_attn_gain[None], grad_ffn_gain[None]])
    )
    means = plane_sums[:2] / width
    small = jnp.concatenate([plane_sums[2:].reshape(1, -1), grad_heads.reshape(1, -1)], 1)
    small = sum_axis(sum_axis(small, SL), SH)
    means, grad_out_w, grad_upward = tie(means, grad_out_w, grad_upward)
    d_qkv, moved = raw_grads(
        raw, inverse, head_gain, cosine, sine, d_query, d_key, d_val, means, spot, block
    )

    sides = d_qkv.reshape(2, rows, 3 * wide)
    grad_qkv = both((inputs, remote), (part(sides, y, 0), part(sides, 1 - y, 0)))
    grad_qkv, moved = tie(grad_qkv, moved)
    grad_qkv = to_shard(grad_qkv)
    up_halves = to_owner(grad_upward)
    both_attn = across(dot(moved[:group], w_qkv, 1, 1), dot(moved[group:], w_qkv, 1, 1))
    both_attn, *up_halves = tie(both_attn, *up_halves)
    back_attn = collect(both_attn, CX)
    down_step = adam(*triple(6), *down_halves, y[None], turned=True)
    gate_step = adam(*triple(4), *gate_halves, y[None])
    up_step = adam(*triple(5), *up_halves, y[None])
    block_share = assemble(block_rows, block_theirs, block)
    back_attn, small, block_share, *turned = tie(
        back_attn, small, block_share, *down_step, *gate_step, *up_step
    )
    down_step, gate_step, up_step = turned[:4], turned[4:8], turned[8:]
    out_step = adam(*triple(3), *to_owner(grad_out_w), y[None], turned=True)
    grad_qkv = to_owner(grad_qkv)
    input_rows = over_chips((grad_res + back_attn).astype(b16))
    input_share = assemble(input_rows, swap(input_rows, TC), block)

    index = lax.axis_index(SHARD) * 2 + y
    wide_sums = lax.dynamic_slice_in_dim(
        small[0, : 2 * width].reshape(2, width), index * piece, piece, 1
    )
    head_sums = small[0, 2 * width :].reshape(2, 1, heads_here // 2, size)
    head_sums = pair(head_sums, swap(head_sums, CX), CX, 1).reshape(2, heads_here, size)
    head_sums = lax.dynamic_slice_in_dim(head_sums, index * head_piece, head_piece, 2)

    stepped = [adam(*triple(i), *grad_qkv, y[None], column=i) for i in range(3)]
    stepped += [out_step, gate_step, up_step, down_step]
    for i, grad in enumerate((head_sums[0], head_sums[1], wide_sums[0], wide_sums[1])):
        stepped.append((grad,) + adam_step(*triple(7 + i), grad))
    return tuple(
        [block_share, input_share]
        + [result[which] for which in range(4) for result in stepped]
    )


def solution(mesh):
    ring, ctx, teams = (mesh.shape[name] for name in mesh.axis_names)
    fine = Mesh(
        mesh.devices.reshape(ring // 2, 2, ctx, teams // 2, 2), (SH, SL, CX, TX, TC)
    )
    owners = (SH, SL, CX)
    column = P(owners, TENSOR)
    row = P(TENSOR, owners)
    vector = P(owners)
    act = P(SHARD, CX, None)
    weights = (column, column, column, row, column, column, row, row, row, vector, vector)
    return jax.shard_map(
        shards,
        mesh=fine,
        in_specs=(act, act, P(SHARD, CX)) + weights * 3,
        out_specs=(act, act) + weights * 4,
        check_vma=False,
    )
```

time: 1270 us -> 939 us (0.74)
  matrix products: 314 us -> 86.5 us
  Pallas kernels: 0 us -> 177 us
  other arithmetic: 156 us -> 60.5 us
  local copies, waits for them, and re-layouts: 149 us -> 72.3 us
  blocking collectives: 74.8 us -> 0 us
  waiting for transfers between devices: 507 us -> 441 us
  starting transfers between devices: 46.2 us -> 77.8 us
    pallas_call x0 -> x23, Pallas kernels: none -> 177 us  [the longest x2 26.8 us: ffn_residual(): pl.pallas_call(ffn_residual_body, grid=(width // step,), in_specs=[full,...]
    dot_general x30 -> x18, matrix products: 211 us -> 86.5 us  [dot(): lax.dot_general(a, b, (((ca,), (cb,)), ((), ())), preferred_element_type=...]
    ppermute x50 -> x76, waiting for transfers between devices: 451 us -> 342 us  [swap(): return lax.ppermute(value, axis, [(0, 1), (1, 0)])]
    dot_general x14 -> x0, matrix products: 103 us -> none  [the longest x2 23.9 us: backward_block(): jnp.einsum('qhd,khd->hqk', grad_block, values_all, preferred_element_type...]
    psum x4 -> x0, blocking collectives: 74.8 us -> none  [the longest x1 41 us: shards(): lax.psum(jnp.stack([whole(*grad_attn_gain), whole(*grad_ffn_gain)]), (SH,...]
    convert_element_type x20 -> x6, other arithmetic: 41.7 us -> 4.31 us  [the longest x1 2.37 us: shards(): res, w_both, down_w = tie(residual.astype(b16), w_both, down_w)]
    ppermute x50 -> x76, starting transfers between devices: 45.2 us -> 76.5 us  [swap(): return lax.ppermute(value, axis, [(0, 1), (1, 0)])]
    sub x8 -> x3, other arithmetic: 30.1 us -> 4.01 us  [adam_step(): weight - learn_rate * (first_hat / (jnp.sqrt(second_hat) + adam_eps) + de...]
  transfers between devices with their start and end apart: 62 -> 85, of which waited for: 29 -> 52; matrix products, arithmetic and copies ran while one was open for 46% -> 12% of each run, Pallas kernels for 0% -> 17%
where the time goes in v1:
time: 939 us; the launch traced here: 931 us
  waiting for transfers between devices  441 us (47%)
  Pallas kernels  177 us (19%)
  matrix products  86.5 us (9%)
  starting transfers between devices  77.8 us (8%)
  local copies, waits for them, and re-layouts  72.3 us (8%)
  other arithmetic  60.5 us (6%)
  between operations  16.2 us (2%)
    ppermute x76, waiting for transfers between devices, swap(): return lax.ppermute(value, axis, [(0, 1), (1, 0)])  342 us
    dot_general x18, matrix products, dot(): lax.dot_general(a, b, (((ca,), (cb,)), ((), ())), preferred_element_type=...  86.5 us
    all_gather x4, waiting for transfers between devices, over_shard(): return lax.all_gather(value, SHARD, axis=0, tiled=True)  81.1 us
    ppermute x76, starting transfers between devices, swap(): return lax.ppermute(value, axis, [(0, 1), (1, 0)])  76.5 us
    unnamed x277, local copies, waits for them, and re-layouts  54.3 us
    pallas_call x2, Pallas kernels, ffn_residual(): pl.pallas_call(ffn_residual_body, grid=(width // step,), in_specs=[full,...  26.8 us
    pallas_call x2, Pallas kernels, ffn_forward(): pl.pallas_call(functools.partial(ffn_forward_body, len(blocks)), grid=(co...  26.5 us
    pallas_call x1, Pallas kernels, flash_backward(): pl.pallas_call(functools.partial(backward_body, span), grid_spec=pltpu.Pr...  24.3 us
  transfers between devices with their start and end apart: 85, of which 52 were waited for; matrix products, arithmetic and copies ran while one was open for 12% of the time, Pallas kernels for 17%

profile of v1, /device:TPU:0, one launch (start us, length us, event | category | flops | bytes accessed | tf_op | source)
XLA Modules:
  0.0 931.2 jit_solution(6929547443895198693)
XLA Ops:
  30.8 7.7 collective-permute-done.4
  43.1 16.7 %collective-permute-done.5 = bf16[256,2048]{1,0:T(8,128)(2,1)} collective-permute-done((bf16[256,2048]{1,0:T(8,128)(2,1)}, bf16[256,2048]{1,0:T(8,128)(2,1)}, u32[]{:S(2)}, u32[]{:S(2)}) %collective-permute-start.5) | collective-permute-done | bytes 1048608 | tf_op jit(solution)/shard_map/ppermute | solution.py:38
  64.9 7.5 collective-permute-done.7
  75.0 5.2 collective-permute-done.6
  92.9 14.3 %all-gather.5.cloned.1.call-done.weight = bf16[2048,768]{1,0:T(8,128)(2,1)} async-done(((bf16[512,768]{1,0:T(8,128)(2,1)}), bf16[2048,768]{1,0:T(8,128)(2,1)}) %all-gather.5.cloned.1.call-update) | async-done | bytes 3145744 | tf_op jit(solution)/shard_map/all_gather | solution.py:699
  107.3 5.5 fusion.26
  123.3 9.5 %shard_map.700 = (f32[2048,768]{1,0:T(8,128)}, f32[2,2048]{1,0:T(2,128)S(1)}) custom-call(s32[1]{0:T(128)} %bitcast.2.side.flag, bf16[1024,2048]{1,0:T(8,128)(2,1)S(1)} %bitcast.111, bf16[1024,2048]{1,0:T(8,128)(2,1)S(1)} %copy-done.3, bf16[2048,768]{1,0:T(8,128)(2,1)S(1)} %copy-done.38), custom_call_target="tpu_custom_call" | custom-call | bytes 6000000 | tf_op jit(solution)/shard_map/pallas_call | solution.py:168
  152.6 20.2 %shard_map.702 = (bf16[2048,256]{1,0:T(8,128)(2,1)S(1)}, f32[2,1,2048]{2,1,0:T(1,128)S(1)}) custom-call(s32[8]{0:T(128)S(1)} %fusion.37.spot, s32[8]{0:T(128)S(1)} %and_select_fusion.low, bf16[2048,256]{1,0:T(8,128)(2,1)S(1)} %get-tuple-element.205.query, bf16[2048,256]{1,0:T(8,128)(2,1)S(1)} %get-tuple-element.206.keys, ...), custom_call_target="tpu_custom_call" | custom-call | bytes 9000000 | tf_op jit(solution)/shard_map/pallas_call | solution.py:275
  174.3 7.1 collective-permute-done.13
  185.2 11.8 %collective-permute-done.14 = bf16[128,2048]{1,0:T(8,128)(2,1)S(1)} collective-permute-done((bf16[128,2048]{1,0:T(8,128)(2,1)S(1)}, bf16[128,2048]{1,0:T(8,128)(2,1)S(1)}, u32[]{:S(2)}, u32[]{:S(2)}) %collective-permute-start.14) | collective-permute-done | bytes 524320 | tf_op jit(solution)/shard_map/ppermute | solution.py:38
  201.9 31.1 %collective-permute-done.18 = bf16[256,1024]{1,0:T(8,128)(2,1)S(1)} collective-permute-done((bf16[256,1024]{1,0:T(8,128)(2,1)S(1)}, bf16[256,1024]{1,0:T(8,128)(2,1)S(1)}, u32[]{:S(2)}, u32[]{:S(2)}) %collective-permute-start.18) | collective-permute-done | bytes 524320 | tf_op jit(solution)/shard_map/ppermute | solution.py:38
  239.0 60.4 %all-gather.9.cloned.1.call-done.refs_5_.refs_6_.w_gate.w_up = bf16[2048,2048]{1,0:T(8,128)(2,1)} async-done(((bf16[512,2048]{1,0:T(8,128)(2,1)}), bf16[2048,2048]{1,0:T(8,128)(2,1)}) %all-gather.9.cloned.1.call-update) | async-done | bytes 8388624 | tf_op jit(solution)/shard_map/all_gather | solution.py:699
  302.7 22.2 %collective-permute-done.20.refs_2_ = bf16[256,2048]{1,0:T(8,128)(2,1)S(1)} collective-permute-done((bf16[256,2048]{1,0:T(8,128)(2,1)S(1)}, bf16[256,2048]{1,0:T(8,128)(2,1)S(1)}, u32[]{:S(2)}, u32[]{:S(2)}) %collective-permute-start.20) | collective-permute-done | bytes 1048608 | tf_op jit(solution)/shard_map/ppermute | solution.py:38
  328.6 9.6 %collective-permute-done.21.refs_3_ = bf16[128,2048]{1,0:T(8,128)(2,1)S(1)} collective-permute-done((bf16[128,2048]{1,0:T(8,128)(2,1)S(1)}, bf16[128,2048]{1,0:T(8,128)(2,1)S(1)}, u32[]{:S(2)}, u32[]{:S(2)}) %collective-permute-start.21) | collective-permute-done | bytes 524320 | tf_op jit(solution)/shard_map/ppermute | solution.py:38
  341.0 13.3 %shard_map.704 = (bf16[1024,2048]{1,0:T(8,128)(2,1)}, bf16[1024,1024]{1,0:T(8,128)(2,1)S(1)}, bf16[1024,1024]{1,0:T(8,128)(2,1)S(1)}, bf16[1024,1024]{1,0:T(8,128)(2,1)S(1)}) custom-call(bf16[256,2048]{1,0:T(8,128)(2,1)S(1)} %fusion.17.refs_0_, bf16[256,2048]{1,0:T(8,128)(2,1)S(1)} %collective-permute-done.19.refs_1_, ...), custom_call_target="tpu_custom_call" | custom-call | bytes 5000000 | tf_op jit(solution)/shard_map/pallas_call | solution.py:487
  357.0 13.3 %shard_map.705 = (bf16[1024,2048]{1,0:T(8,128)(2,1)}, bf16[1024,1024]{1,0:T(8,128)(2,1)S(1)}, bf16[1024,1024]{1,0:T(8,128)(2,1)S(1)}, bf16[1024,1024]{1,0:T(8,128)(2,1)S(1)}) custom-call(bf16[256,2048]{1,0:T(8,128)(2,1)S(1)} %collective-permute-done.23.refs_0_, bf16[256,2048]{1,0:T(8,128)(2,1)S(1)} %collective-permute-done.24.refs_1_, ...), custom_call_target="tpu_custom_call" | custom-call | bytes 5000000 | tf_op jit(solution)/shard_map/pallas_call | solution.py:487
  374.2 6.3 all-gather.11.cloned.1.call-done.w_down
  380.5 7.5 convolution_convert_fusion.2
  388.1 7.1 collective-permute-done.28
  403.5 11.0 %collective-permute-done.29 = bf16[128,2048]{1,0:T(8,128)(2,1)S(1)} collective-permute-done((bf16[128,2048]{1,0:T(8,128)(2,1)S(1)}, bf16[128,2048]{1,0:T(8,128)(2,1)S(1)}, u32[]{:S(2)}, u32[]{:S(2)}) %collective-permute-start.29) | collective-permute-done | bytes 524320 | tf_op jit(solution)/shard_map/ppermute | solution.py:38
  418.3 21.8 %collective-permute-done.32 = bf16[256,2048]{1,0:T(8,128)(2,1)S(1)} collective-permute-done((bf16[256,2048]{1,0:T(8,128)(2,1)S(1)}, bf16[256,2048]{1,0:T(8,128)(2,1)S(1)}, u32[]{:S(2)}, u32[]{:S(2)}) %collective-permute-start.32) | collective-permute-done | bytes 1048608 | tf_op jit(solution)/shard_map/ppermute | solution.py:38
  448.2 20.1 %collective-permute-done.34 = bf16[256,2048]{1,0:T(8,128)(2,1)S(1)} collective-permute-done((bf16[256,2048]{1,0:T(8,128)(2,1)S(1)}, bf16[256,2048]{1,0:T(8,128)(2,1)S(1)}, u32[]{:S(2)}, u32[]{:S(2)}) %collective-permute-start.34) | collective-permute-done | bytes 1048608 | tf_op jit(solution)/shard_map/ppermute | solution.py:38
  472.1 8.4 collective-permute-done.35
  484.2 6.9 fusion.58
  493.1 8.4 add_convert_fusion.3
  507.3 8.3 shard_map.707
  515.6 13.5 %shard_map.708 = bf16[1024,2048]{1,0:T(8,128)(2,1)} custom-call(bf16[1024,1024]{1,0:T(8,128)(2,1)S(1)} %get-tuple-element.232.d_gate, bf16[1024,1024]{1,0:T(8,128)(2,1)S(1)} %get-tuple-element.240.d_up, bf16[2048,2048]{1,0:T(8,128)(2,1)} %all-gather.9.cloned.1.call-done.refs_5_.refs_6_.w_gate.w_up, ...), custom_call_target="tpu_custom_call" | custom-call | bytes 4500000 | tf_op jit(solution)/shard_map/pallas_call | solution.py:544
  529.3 8.0 shard_map.706
  537.3 6.8 fusion.60
  544.2 8.4 add_convert_fusion.1
  554.3 23.9 %collective-permute-done.43 = bf16[256,2048]{1,0:T(8,128)(2,1)S(1)} collective-permute-done((bf16[256,2048]{1,0:T(8,128)(2,1)S(1)}, bf16[256,2048]{1,0:T(8,128)(2,1)S(1)}, u32[]{:S(2)}, u32[]{:S(2)}) %collective-permute-start.43) | collective-permute-done | bytes 1048608 | tf_op jit(solution)/shard_map/ppermute | solution.py:38
  578.5 13.3 %shard_map.709 = bf16[1024,2048]{1,0:T(8,128)(2,1)S(1)} custom-call(bf16[1024,1024]{1,0:T(8,128)(2,1)S(1)} %copy-done.44, bf16[1024,1024]{1,0:T(8,128)(2,1)S(1)} %copy-done.41, bf16[2048,2048]{1,0:T(8,128)(2,1)} %all-gather.9.cloned.1.call-done.refs_5_.refs_6_.w_gate.w_up, bf16[2048,2048]{1,0:T(8,128)(2,1)} %all-gather.9.cloned.1.call-done.refs_5_.refs_6_.w_gate.w_up, ...), custom_call_target="tpu_custom_call" | custom-call | bytes 4500000 | tf_op jit(solution)/shard_map/pallas_call | solution.py:544
  597.9 6.4 fusion.59
  616.2 6.1 add_convert_fusion.2
  622.3 13.8 %collective-permute-done.47 = bf16[256,2048]{1,0:T(8,128)(2,1)S(1)} collective-permute-done((bf16[256,2048]{1,0:T(8,128)(2,1)}, bf16[256,2048]{1,0:T(8,128)(2,1)S(1)}, u32[]{:S(2)}, u32[]{:S(2)}) %collective-permute-start.47) | collective-permute-done | bytes 1048608 | tf_op jit(solution)/shard_map/ppermute | solution.py:38
  647.1 19.4 %collective-permute-done.49 = bf16[256,2048]{1,0:T(8,128)(2,1)S(1)} collective-permute-done((bf16[256,2048]{1,0:T(8,128)(2,1)S(1)}, bf16[256,2048]{1,0:T(8,128)(2,1)S(1)}, u32[]{:S(2)}, u32[]{:S(2)}) %collective-permute-start.49) | collective-permute-done | bytes 1048608 | tf_op jit(solution)/shard_map/ppermute | solution.py:38
  671.7 6.6 collective-permute-done.50
  699.4 24.3 %shard_map.710 = (f32[2048,256]{1,0:T(8,128)S(1)}, f32[2048,256]{1,0:T(8,128)S(1)}, f32[2048,256]{1,0:T(8,128)S(1)}) custom-call(s32[8]{0:T(128)S(1)} %copy-done.91, s32[8]{0:T(128)S(1)} %copy-done.93, bf16[2048,256]{1,0:T(8,128)(2,1)S(1)} %copy-done.32, bf16[2048,256]{1,0:T(8,128)(2,1)S(1)} %copy-done.34, bf16[2048,256]{1,0:T(8,128)(2,1)S(1)} %copy-done.36, ...), custom_call_target="tpu_custom_call" | custom-call | bytes 11000000 | tf_op jit(solution)/shard_map/pallas_call | solution.py:340
  729.2 6.1 reduce-scatter.10.cloned.1.call-done
  754.4 11.5 %reduce-scatter.12.cloned.1.call-done = bf16[512,256]{1,0:T(8,128)(2,1)} async-done(((bf16[2048,256]{1,0:T(8,128)(2,1)}), bf16[512,256]{1,0:T(8,128)(2,1)}) %reduce-scatter.12.cloned.1.call-update) | async-done | bytes 262160 | tf_op jit(solution)/shard_map/reduce_scatter | solution.py:785
  770.7 9.1 shard_map.712
  788.5 5.2 convolution_convert_fusion.1
  812.8 10.6 %collective-permute-done.65 = bf16[128,2048]{1,0:T(8,128)(2,1)S(1)} collective-permute-done((bf16[128,2048]{1,0:T(8,128)(2,1)S(1)}, bf16[128,2048]{1,0:T(8,128)(2,1)S(1)}, u32[]{:S(2)}, u32[]{:S(2)}) %collective-permute-start.65) | collective-permute-done | bytes 524320 | tf_op jit(solution)/shard_map/ppermute | solution.py:38
  833.7 7.7 shard_map.713
  841.5 5.7 shard_map.714
  860.7 22.1 %collective-permute-done.71 = bf16[256,2048]{1,0:T(8,128)(2,1)S(1)} collective-permute-done((bf16[256,2048]{1,0:T(8,128)(2,1)S(1)}, bf16[256,2048]{1,0:T(8,128)(2,1)S(1)}, u32[]{:S(2)}, u32[]{:S(2)}) %collective-permute-start.71) | collective-permute-done | bytes 1048608 | tf_op jit(solution)/shard_map/ppermute | solution.py:38
  901.8 7.1 collective-permute-done.73.other
  917.6 6.6 shard_map.717
  (567 shorter events, 311.2 us)
Async XLA Ops:
  7.3 99.9 %all-gather.5.cloned.1.call-start = ((), (), s32[]{:S(2)}) async-start(), calls=%async_computation.5 | async-start | bytes 3932160 | tf_op jit(solution)/shard_map/all_gather | solution.py:699
  38.5 21.3 %collective-permute-start.5 = (bf16[256,2048]{1,0:T(8,128)(2,1)}, bf16[256,2048]{1,0:T(8,128)(2,1)}, u32[]{:S(2)}, u32[]{:S(2)}) collective-permute-start(bf16[256,2048]{1,0:T(8,128)(2,1)} %constant_dynamic-slice_fusion.7), channel_id=1, source_target_pairs={{0,4},{4,0},{1,5},{5,1},{2,6},{6,2},{3,7},{7,3},{8,12},{12,8},{9,1... | collective-permute-start | bytes 3145736 | tf_op jit(solution)/shard_map/ppermute | solution.py:38
  43.0 104.6 %all-gather.7.cloned.1.call-start = ((), (), s32[]{:S(2)}) async-start(), calls=%async_computation.6 | async-start | bytes 1310720 | tf_op jit(solution)/shard_map/all_gather | solution.py:699
  59.8 20.4 %collective-permute-start.6 = (bf16[256,2048]{1,0:T(8,128)(2,1)}, bf16[256,2048]{1,0:T(8,128)(2,1)}, u32[]{:S(2)}, u32[]{:S(2)}) collective-permute-start(bf16[256,2048]{1,0:T(8,128)(2,1)} %collective-permute-done.5), channel_id=1, source_target_pairs={{0,2},{2,0},{1,3},{3,1},{4,6},{6,4},{5,7},{7,5},{8,10},{10,8},{9,1... | collective-permute-start | bytes 3145736 | tf_op jit(solution)/shard_map/ppermute | solution.py:38
  107.2 192.3 %all-gather.9.cloned.1.call-start = ((), (), s32[]{:S(2)}) async-start(), calls=%async_computation.7 | async-start | bytes 10485760 | tf_op jit(solution)/shard_map/all_gather | solution.py:699
  113.9 24.6 %collective-permute-start.12 = (bf16[256,1024]{1,0:T(8,128)(2,1)}, bf16[256,1024]{1,0:T(8,128)(2,1)S(1)}, u32[]{:S(2)}, u32[]{:S(2)}) collective-permute-start(bf16[256,1024]{1,0:T(8,128)(2,1)} %get-tuple-element.365), channel_id=1, source_target_pairs={{0,4},{4,0},{1,5},{5,1},{2,6},{6,2},{3,7},{7,3},{8,12},{12,8},{9,1... | collective-permute-start | bytes 1572872 | tf_op jit(solution)/shard_map/ppermute | solution.py:38
  151.8 228.7 %all-gather.11.cloned.1.call-start = ((), (), s32[]{:S(2)}) async-start(), calls=%async_computation.8 | async-start | bytes 5242880 | tf_op jit(solution)/shard_map/all_gather | solution.py:699
  183.0 14.0 %collective-permute-start.14 = (bf16[128,2048]{1,0:T(8,128)(2,1)S(1)}, bf16[128,2048]{1,0:T(8,128)(2,1)S(1)}, u32[]{:S(2)}, u32[]{:S(2)}) collective-permute-start(bf16[128,2048]{1,0:T(8,128)(2,1)S(1)} %get-tuple-element.361), channel_id=1, source_target_pairs={{0,4},{4,0},{1,5},{5,1},{2,6},{6,2},{3,7},{7,3},{8,12},{12,8},{9,1... | collective-permute-start | bytes 1572872 | tf_op jit(solution)/shard_map/ppermute | solution.py:38
  183.7 13.7 %collective-permute-start.16 = (bf16[128,2048]{1,0:T(8,128)(2,1)S(1)}, bf16[128,2048]{1,0:T(8,128)(2,1)S(1)}, u32[]{:S(2)}, u32[]{:S(2)}) collective-permute-start(bf16[128,2048]{1,0:T(8,128)(2,1)S(1)} %get-tuple-element.360), channel_id=1, source_target_pairs={{0,2},{2,0},{1,3},{3,1},{4,6},{6,4},{5,7},{7,5},{8,10},{10,8},{9,1... | collective-permute-start | bytes 1572872 | tf_op jit(solution)/shard_map/ppermute | solution.py:38
  197.6 36.9 %collective-permute-start.17 = (bf16[256,2048]{1,0:T(8,128)(2,1)S(1)}, bf16[256,2048]{1,0:T(8,128)(2,1)S(1)}, u32[]{:S(2)}, u32[]{:S(2)}) collective-permute-start(bf16[256,2048]{1,0:T(8,128)(2,1)S(1)} %pad_maximum_fusion.6), channel_id=1, source_target_pairs={{0,4},{4,0},{1,5},{5,1},{2,6},{6,2},{3,7},{7,3},{8,12},{12,8},{9,1... | collective-permute-start | bytes 3145736 | tf_op jit(solution)/shard_map/ppermute | solution.py:38
  199.1 35.4 %collective-permute-start.15 = (bf16[256,2048]{1,0:T(8,128)(2,1)S(1)}, bf16[256,2048]{1,0:T(8,128)(2,1)}, u32[]{:S(2)}, u32[]{:S(2)}) collective-permute-start(bf16[256,2048]{1,0:T(8,128)(2,1)S(1)} %pad_maximum_fusion.5), channel_id=1, source_target_pairs={{0,2},{2,0},{1,3},{3,1},{4,6},{6,4},{5,7},{7,5},{8,10},{10,8},{9,1... | collective-permute-start | bytes 3145736 | tf_op jit(solution)/shard_map/ppermute | solution.py:38
  201.3 31.8 %collective-permute-start.18 = (bf16[256,1024]{1,0:T(8,128)(2,1)S(1)}, bf16[256,1024]{1,0:T(8,128)(2,1)S(1)}, u32[]{:S(2)}, u32[]{:S(2)}) collective-permute-start(bf16[256,1024]{1,0:T(8,128)(2,1)S(1)} %get-tuple-element.375), channel_id=1, source_target_pairs={{0,4},{4,0},{1,5},{5,1},{2,6},{6,2},{3,7},{7,3},{8,12},{12,8},{9,1... | collective-permute-start | bytes 1572872 | tf_op jit(solution)/shard_map/ppermute | solution.py:38
  299.5 294.3 %reduce-scatter.6.cloned.1.call-start = ((), (), s32[]{:S(2)}) async-start(), calls=%async_computation.9 | async-start | bytes 5242880 | tf_op jit(solution)/shard_map/reduce_scatter | solution.py:785
  299.7 25.2 %collective-permute-start.20 = (bf16[256,2048]{1,0:T(8,128)(2,1)S(1)}, bf16[256,2048]{1,0:T(8,128)(2,1)S(1)}, u32[]{:S(2)}, u32[]{:S(2)}) collective-permute-start(bf16[256,2048]{1,0:T(8,128)(2,1)S(1)} %fusion.17.refs_0_), channel_id=1, source_target_pairs={{0,4},{4,0},{1,5},{5,1},{2,6},{6,2},{3,7},{7,3},{8,12},{12,8},{9,1... | collective-permute-start | bytes 3145736 | tf_op jit(solution)/shard_map/ppermute | solution.py:38
  301.3 25.2 %collective-permute-start.19 = (bf16[256,2048]{1,0:T(8,128)(2,1)S(1)}, bf16[256,2048]{1,0:T(8,128)(2,1)S(1)}, u32[]{:S(2)}, u32[]{:S(2)}) collective-permute-start(bf16[256,2048]{1,0:T(8,128)(2,1)S(1)} %fusion.17.refs_0_), channel_id=1, source_target_pairs={{0,2},{2,0},{1,3},{3,1},{4,6},{6,4},{5,7},{7,5},{8,10},{10,8},{9,1... | collective-permute-start | bytes 3145736 | tf_op jit(solution)/shard_map/ppermute | solution.py:38
  302.7 54.2 %collective-permute-start.23 = (bf16[256,2048]{1,0:T(8,128)(2,1)S(1)}, bf16[256,2048]{1,0:T(8,128)(2,1)S(1)}, u32[]{:S(2)}, u32[]{:S(2)}) collective-permute-start(bf16[256,2048]{1,0:T(8,128)(2,1)S(1)} %fusion.17.refs_0_), channel_id=1, source_target_pairs={{0,1},{1,0},{2,3},{3,2},{4,5},{5,4},{6,7},{7,6},{8,9},{9,8},{10,11... | collective-permute-start | bytes 3145736 | tf_op jit(solution)/shard_map/ppermute | solution.py:38
  326.5 30.4 %collective-permute-start.24 = (bf16[256,2048]{1,0:T(8,128)(2,1)S(1)}, bf16[256,2048]{1,0:T(8,128)(2,1)S(1)}, u32[]{:S(2)}, u32[]{:S(2)}) collective-permute-start(bf16[256,2048]{1,0:T(8,128)(2,1)S(1)} %collective-permute-done.19.refs_1_), channel_id=1, source_target_pairs={{0,1},{1,0},{2,3},{3,2},{4,5},{5,4},{6,7},{7,6},{8,9},{9,8},{10,11... | collective-permute-start | bytes 3145736 | tf_op jit(solution)/shard_map/ppermute | solution.py:38
  326.6 30.3 %collective-permute-start.25 = (bf16[256,2048]{1,0:T(8,128)(2,1)S(1)}, bf16[256,2048]{1,0:T(8,128)(2,1)S(1)}, u32[]{:S(2)}, u32[]{:S(2)}) collective-permute-start(bf16[256,2048]{1,0:T(8,128)(2,1)S(1)} %collective-permute-done.20.refs_2_), channel_id=1, source_target_pairs={{0,1},{1,0},{2,3},{3,2},{4,5},{5,4},{6,7},{7,6},{8,9},{9,8},{10,11... | collective-permute-start | bytes 3145736 | tf_op jit(solution)/shard_map/ppermute | solution.py:38
  327.1 13.9 %collective-permute-start.22 = (bf16[128,2048]{1,0:T(8,128)(2,1)S(1)}, bf16[128,2048]{1,0:T(8,128)(2,1)S(1)}, u32[]{:S(2)}, u32[]{:S(2)}) collective-permute-start(bf16[128,2048]{1,0:T(8,128)(2,1)S(1)} %slice.226), channel_id=1, source_target_pairs={{0,4},{4,0},{1,5},{5,1},{2,6},{6,2},{3,7},{7,3},{8,12},{12,8},{9,1... | collective-permute-start | bytes 1572872 | tf_op jit(solution)/shard_map/ppermute | solution.py:38
  338.2 18.8 %collective-permute-start.26 = (bf16[128,2048]{1,0:T(8,128)(2,1)S(1)}, bf16[128,2048]{1,0:T(8,128)(2,1)S(1)}, u32[]{:S(2)}, u32[]{:S(2)}) collective-permute-start(bf16[128,2048]{1,0:T(8,128)(2,1)S(1)} %collective-permute-done.21.refs_3_), channel_id=1, source_target_pairs={{0,1},{1,0},{2,3},{3,2},{4,5},{5,4},{6,7},{7,6},{8,9},{9,8},{10,11... | collective-permute-start | bytes 1572872 | tf_op jit(solution)/shard_map/ppermute | solution.py:38
  341.0 15.9 %collective-permute-start.27 = (bf16[128,2048]{1,0:T(8,128)(2,1)S(1)}, bf16[128,2048]{1,0:T(8,128)(2,1)S(1)}, u32[]{:S(2)}, u32[]{:S(2)}) collective-permute-start(bf16[128,2048]{1,0:T(8,128)(2,1)S(1)} %collective-permute-done.22.refs_4_), channel_id=1, source_target_pairs={{0,1},{1,0},{2,3},{3,2},{4,5},{5,4},{6,7},{7,6},{8,9},{9,8},{10,11... | collective-permute-start | bytes 1572872 | tf_op jit(solution)/shard_map/ppermute | solution.py:38
  400.5 14.0 %collective-permute-start.29 = (bf16[128,2048]{1,0:T(8,128)(2,1)S(1)}, bf16[128,2048]{1,0:T(8,128)(2,1)S(1)}, u32[]{:S(2)}, u32[]{:S(2)}) collective-permute-start(bf16[128,2048]{1,0:T(8,128)(2,1)S(1)} %get-tuple-element.355), channel_id=1, source_target_pairs={{0,4},{4,0},{1,5},{5,1},{2,6},{6,2},{3,7},{7,3},{8,12},{12,8},{9,1... | collective-permute-start | bytes 1572872 | tf_op jit(solution)/shard_map/ppermute | solution.py:38
  402.1 13.7 %collective-permute-start.31 = (bf16[128,2048]{1,0:T(8,128)(2,1)S(1)}, bf16[128,2048]{1,0:T(8,128)(2,1)S(1)}, u32[]{:S(2)}, u32[]{:S(2)}) collective-permute-start(bf16[128,2048]{1,0:T(8,128)(2,1)S(1)} %get-tuple-element.354), channel_id=1, source_target_pairs={{0,2},{2,0},{1,3},{3,1},{4,6},{6,4},{5,7},{7,5},{8,10},{10,8},{9,1... | collective-permute-start | bytes 1572872 | tf_op jit(solution)/shard_map/ppermute | solution.py:38
  416.0 24.1 %collective-permute-start.32 = (bf16[256,2048]{1,0:T(8,128)(2,1)S(1)}, bf16[256,2048]{1,0:T(8,128)(2,1)S(1)}, u32[]{:S(2)}, u32[]{:S(2)}) collective-permute-start(bf16[256,2048]{1,0:T(8,128)(2,1)S(1)} %pad_maximum_fusion.8), channel_id=1, source_target_pairs={{0,4},{4,0},{1,5},{5,1},{2,6},{6,2},{3,7},{7,3},{8,12},{12,8},{9,1... | collective-permute-start | bytes 3145736 | tf_op jit(solution)/shard_map/ppermute | solution.py:38
  416.7 23.9 %collective-permute-start.30 = (bf16[256,2048]{1,0:T(8,128)(2,1)S(1)}, bf16[256,2048]{1,0:T(8,128)(2,1)S(1)}, u32[]{:S(2)}, u32[]{:S(2)}) collective-permute-start(bf16[256,2048]{1,0:T(8,128)(2,1)S(1)} %pad_maximum_fusion.7), channel_id=1, source_target_pairs={{0,2},{2,0},{1,3},{3,1},{4,6},{6,4},{5,7},{7,5},{8,10},{10,8},{9,1... | collective-permute-start | bytes 3145736 | tf_op jit(solution)/shard_map/ppermute | solution.py:38
  445.2 23.0 %collective-permute-start.34 = (bf16[256,2048]{1,0:T(8,128)(2,1)S(1)}, bf16[256,2048]{1,0:T(8,128)(2,1)S(1)}, u32[]{:S(2)}, u32[]{:S(2)}) collective-permute-start(bf16[256,2048]{1,0:T(8,128)(2,1)S(1)} %get-tuple-element.336), channel_id=1, source_target_pairs={{0,4},{4,0},{1,5},{5,1},{2,6},{6,2},{3,7},{7,3},{8,12},{12,8},{9,1... | collective-permute-start | bytes 3145736 | tf_op jit(solution)/shard_map/ppermute | solution.py:38
  446.7 23.9 %collective-permute-start.33 = (bf16[256,2048]{1,0:T(8,128)(2,1)S(1)}, bf16[256,2048]{1,0:T(8,128)(2,1)S(1)}, u32[]{:S(2)}, u32[]{:S(2)}) collective-permute-start(bf16[256,2048]{1,0:T(8,128)(2,1)S(1)} %get-tuple-element.336), channel_id=1, source_target_pairs={{0,2},{2,0},{1,3},{3,1},{4,6},{6,4},{5,7},{7,5},{8,10},{10,8},{9,1... | collective-permute-start | bytes 3145736 | tf_op jit(solution)/shard_map/ppermute | solution.py:38
  448.2 23.8 %collective-permute-start.37 = (bf16[256,2048]{1,0:T(8,128)(2,1)S(1)}, bf16[256,2048]{1,0:T(8,128)(2,1)S(1)}, u32[]{:S(2)}, u32[]{:S(2)}) collective-permute-start(bf16[256,2048]{1,0:T(8,128)(2,1)S(1)} %get-tuple-element.336), channel_id=1, source_target_pairs={{0,1},{1,0},{2,3},{3,2},{4,5},{5,4},{6,7},{7,6},{8,9},{9,8},{10,11... | collective-permute-start | bytes 3145736 | tf_op jit(solution)/shard_map/ppermute | solution.py:38
  501.5 181.3 %reduce-scatter.8.cloned.1.call-start = ((), (), s32[]{:S(2)}) async-start(), calls=%async_computation.10 | async-start | bytes 5242880 | tf_op jit(solution)/shard_map/reduce_scatter | solution.py:785
  529.1 49.4 %collective-permute-start.42 = (bf16[1024,2048]{1,0:T(8,128)(2,1)}, bf16[1024,2048]{1,0:T(8,128)(2,1)}, u32[]{:S(2)}, u32[]{:S(2)}) collective-permute-start(bf16[1024,2048]{1,0:T(8,128)(2,1)} %shard_map.708), channel_id=1, source_target_pairs={{0,1},{1,0},{2,3},{3,2},{4,5},{5,4},{6,7},{7,6},{8,9},{9,8},{10,11... | collective-permute-start | bytes 12582920 | tf_op jit(solution)/shard_map/ppermute | solution.py:38
  552.6 182.7 %reduce-scatter.10.cloned.1.call-start = ((), (), s32[]{:S(2)}) async-start(), calls=%async_computation.11 | async-start | bytes 5242880 | tf_op jit(solution)/shard_map/reduce_scatter | solution.py:785
  552.7 25.6 %collective-permute-start.43 = (bf16[256,2048]{1,0:T(8,128)(2,1)S(1)}, bf16[256,2048]{1,0:T(8,128)(2,1)S(1)}, u32[]{:S(2)}, u32[]{:S(2)}) collective-permute-start(bf16[256,2048]{1,0:T(8,128)(2,1)S(1)} %get-tuple-element.235), channel_id=1, source_target_pairs={{0,2},{2,0},{1,3},{3,1},{4,6},{6,4},{5,7},{7,5},{8,10},{10,8},{9,1... | collective-permute-start | bytes 3145736 | tf_op jit(solution)/shard_map/ppermute | solution.py:38
  612.1 23.9 %collective-permute-start.47 = (bf16[256,2048]{1,0:T(8,128)(2,1)}, bf16[256,2048]{1,0:T(8,128)(2,1)S(1)}, u32[]{:S(2)}, u32[]{:S(2)}) collective-permute-start(bf16[256,2048]{1,0:T(8,128)(2,1)} %pad_maximum_fusion.10), channel_id=1, source_target_pairs={{0,4},{4,0},{1,5},{5,1},{2,6},{6,2},{3,7},{7,3},{8,12},{12,8},{9,1... | collective-permute-start | bytes 3145736 | tf_op jit(solution)/shard_map/ppermute | solution.py:38
  614.6 23.8 %collective-permute-start.45 = (bf16[256,2048]{1,0:T(8,128)(2,1)}, bf16[256,2048]{1,0:T(8,128)(2,1)}, u32[]{:S(2)}, u32[]{:S(2)}) collective-permute-start(bf16[256,2048]{1,0:T(8,128)(2,1)} %pad_maximum_fusion.9), channel_id=1, source_target_pairs={{0,2},{2,0},{1,3},{3,1},{4,6},{6,4},{5,7},{7,5},{8,10},{10,8},{9,1... | collective-permute-start | bytes 3145736 | tf_op jit(solution)/shard_map/ppermute | solution.py:38
  643.7 122.2 %reduce-scatter.12.cloned.1.call-start = ((), (), s32[]{:S(2)}) async-start(), calls=%async_computation.12 | async-start | bytes 1310720 | tf_op jit(solution)/shard_map/reduce_scatter | solution.py:785
  644.0 22.5 %collective-permute-start.49 = (bf16[256,2048]{1,0:T(8,128)(2,1)S(1)}, bf16[256,2048]{1,0:T(8,128)(2,1)S(1)}, u32[]{:S(2)}, u32[]{:S(2)}) collective-permute-start(bf16[256,2048]{1,0:T(8,128)(2,1)S(1)} %multiply_convert_fusion), channel_id=1, source_target_pairs={{0,4},{4,0},{1,5},{5,1},{2,6},{6,2},{3,7},{7,3},{8,12},{12,8},{9,1... | collective-permute-start | bytes 3145736 | tf_op jit(solution)/shard_map/ppermute | solution.py:38
  644.8 23.7 %collective-permute-start.48 = (bf16[256,2048]{1,0:T(8,128)(2,1)S(1)}, bf16[256,2048]{1,0:T(8,128)(2,1)S(1)}, u32[]{:S(2)}, u32[]{:S(2)}) collective-permute-start(bf16[256,2048]{1,0:T(8,128)(2,1)S(1)} %multiply_convert_fusion), channel_id=1, source_target_pairs={{0,2},{2,0},{1,3},{3,1},{4,6},{6,4},{5,7},{7,5},{8,10},{10,8},{9,1... | collective-permute-start | bytes 3145736 | tf_op jit(solution)/shard_map/ppermute | solution.py:38
  646.6 23.4 %collective-permute-start.52 = (bf16[256,2048]{1,0:T(8,128)(2,1)S(1)}, bf16[256,2048]{1,0:T(8,128)(2,1)S(1)}, u32[]{:S(2)}, u32[]{:S(2)}) collective-permute-start(bf16[256,2048]{1,0:T(8,128)(2,1)S(1)} %multiply_convert_fusion), channel_id=1, source_target_pairs={{0,1},{1,0},{2,3},{3,2},{4,5},{5,4},{6,7},{7,6},{8,9},{9,8},{10,11... | collective-permute-start | bytes 3145736 | tf_op jit(solution)/shard_map/ppermute | solution.py:38
  646.6 36.3 %collective-permute-start.57 = (bf16[512,2048]{1,0:T(8,128)(2,1)S(1)}, bf16[512,2048]{1,0:T(8,128)(2,1)}, u32[]{:S(2)}, u32[]{:S(2)}) collective-permute-start(bf16[512,2048]{1,0:T(8,128)(2,1)S(1)} %pad_maximum_fusion.1.mine), channel_id=1, source_target_pairs={{0,1},{1,0},{2,3},{3,2},{4,5},{5,4},{6,7},{7,6},{8,9},{9,8},{10,11... | collective-permute-start | bytes 6291464 | tf_op jit(solution)/shard_map/ppermute | solution.py:38
  695.4 201.8 %reduce-scatter.14.cloned.1.call-start = ((), (), s32[]{:S(2)}) async-start(), calls=%async_computation.13 | async-start | bytes 3932160 | tf_op jit(solution)/shard_map/reduce_scatter | solution.py:785
  696.4 31.2 %collective-permute-start.58 = (bf16[256,1024]{1,0:T(8,128)(2,1)S(1)}, bf16[256,1024]{1,0:T(8,128)(2,1)S(1)}, u32[]{:S(2)}, u32[]{:S(2)}) collective-permute-start(bf16[256,1024]{1,0:T(8,128)(2,1)S(1)} %get-tuple-element.372), channel_id=1, source_target_pairs={{0,4},{4,0},{1,5},{5,1},{2,6},{6,2},{3,7},{7,3},{8,12},{12,8},{9,1... | collective-permute-start | bytes 1572872 | tf_op jit(solution)/shard_map/ppermute | solution.py:38
  698.4 30.0 %collective-permute-start.59 = (bf16[256,1024]{1,0:T(8,128)(2,1)S(1)}, bf16[256,1024]{1,0:T(8,128)(2,1)S(1)}, u32[]{:S(2)}, u32[]{:S(2)}) collective-permute-start(bf16[256,1024]{1,0:T(8,128)(2,1)S(1)} %get-tuple-element.370), channel_id=1, source_target_pairs={{0,4},{4,0},{1,5},{5,1},{2,6},{6,2},{3,7},{7,3},{8,12},{12,8},{9,1... | collective-permute-start | bytes 1572872 | tf_op jit(solution)/shard_map/ppermute | solution.py:38
  794.7 14.3 %collective-permute-start.64 = (bf16[256,1024]{1,0:T(8,128)(2,1)S(1)}, bf16[256,1024]{1,0:T(8,128)(2,1)S(1)}, u32[]{:S(2)}, u32[]{:S(2)}) collective-permute-start(bf16[256,1024]{1,0:T(8,128)(2,1)S(1)} %get-tuple-element.368), channel_id=1, source_target_pairs={{0,4},{4,0},{1,5},{5,1},{2,6},{6,2},{3,7},{7,3},{8,12},{12,8},{9,1... | collective-permute-start | bytes 1572872 | tf_op jit(solution)/shard_map/ppermute | solution.py:38
  826.0 31.8 %collective-permute-start.68 = (bf16[256,2048]{1,0:T(8,128)(2,1)S(1)}, bf16[256,2048]{1,0:T(8,128)(2,1)S(1)}, u32[]{:S(2)}, u32[]{:S(2)}) collective-permute-start(bf16[256,2048]{1,0:T(8,128)(2,1)S(1)} %pad_maximum_fusion.13), channel_id=1, source_target_pairs={{0,4},{4,0},{1,5},{5,1},{2,6},{6,2},{3,7},{7,3},{8,12},{12,8},{9,1... | collective-permute-start | bytes 3145736 | tf_op jit(solution)/shard_map/ppermute | solution.py:38
  826.7 31.0 %collective-permute-start.66 = (bf16[256,2048]{1,0:T(8,128)(2,1)S(1)}, bf16[256,2048]{1,0:T(8,128)(2,1)S(1)}, u32[]{:S(2)}, u32[]{:S(2)}) collective-permute-start(bf16[256,2048]{1,0:T(8,128)(2,1)S(1)} %pad_maximum_fusion.12), channel_id=1, source_target_pairs={{0,2},{2,0},{1,3},{3,1},{4,6},{6,4},{5,7},{7,5},{8,10},{10,8},{9,1... | collective-permute-start | bytes 3145736 | tf_op jit(solution)/shard_map/ppermute | solution.py:38
  832.5 19.7 %collective-permute-start.70 = (f32[1,4608]{1,0:T(1,128)S(1)}, f32[1,4608]{1,0:T(1,128)S(1)}, u32[]{:S(2)}, u32[]{:S(2)}) collective-permute-start(f32[1,4608]{1,0:T(1,128)S(1)} %add.322), channel_id=1, source_target_pairs={{0,16},{16,0},{1,17},{17,1},{2,18},{18,2},{3,19},{19,3},{4,20},{20... | collective-permute-start | bytes 55304 | tf_op jit(solution)/shard_map/ppermute | solution.py:38
  860.0 22.8 %collective-permute-start.71 = (bf16[256,2048]{1,0:T(8,128)(2,1)S(1)}, bf16[256,2048]{1,0:T(8,128)(2,1)S(1)}, u32[]{:S(2)}, u32[]{:S(2)}) collective-permute-start(bf16[256,2048]{1,0:T(8,128)(2,1)S(1)} %add_convert_fusion.7), channel_id=1, source_target_pairs={{0,2},{2,0},{1,3},{3,1},{4,6},{6,4},{5,7},{7,5},{8,10},{10,8},{9,1... | collective-permute-start | bytes 3145736 | tf_op jit(solution)/shard_map/ppermute | solution.py:38
  883.0 34.6 %collective-permute-start.72 = (bf16[512,2048]{1,0:T(8,128)(2,1)S(1)}, bf16[512,2048]{1,0:T(8,128)(2,1)}, u32[]{:S(2)}, u32[]{:S(2)}) collective-permute-start(bf16[512,2048]{1,0:T(8,128)(2,1)S(1)} %pad_maximum_fusion.2.mine), channel_id=1, source_target_pairs={{0,1},{1,0},{2,3},{3,2},{4,5},{5,4},{6,7},{7,6},{8,9},{9,8},{10,11... | collective-permute-start | bytes 6291464 | tf_op jit(solution)/shard_map/ppermute | solution.py:38
  (165 other events, 1554.8 us)
Sparse Core Ops, SparseCore 0:
  43.1 64.0 all-gather.4
  109.3 26.5 all-gather.6
  151.9 147.4 all-gather.8
  301.5 78.9 all-gather.10
  501.7 74.4 reduce-scatter.5
  578.4 77.2 reduce-scatter.7
  658.0 77.2 reduce-scatter.9
  738.2 27.6 reduce-scatter.11
  812.9 57.8 reduce-scatter.13

commit v2 on v1

--- a/solution.py
+++ b/solution.py
@@ -129,9 +129,9 @@
     return (core * 2 + side) * count + along
 
 
-def params(steps):
+def params(steps, mebibytes=30):
     return pltpu.CompilerParams(
-        dimension_semantics=("arbitrary",) * steps, vmem_limit_bytes=40 * 1024 * 1024
+        dimension_semantics=("arbitrary",) * steps, vmem_limit_bytes=mebibytes * 1024 * 1024
     )
 
 
@@ -161,7 +161,7 @@
 
 def project(side, local, remote, weight):
     rows, width = local.shape
-    columns = weight.shape[1]
+    columns = weight.shape[1] // 4 * 3
     step = min(256, rows)
     half = rows // step
     tokens = pl.BlockSpec((step, width), lambda i, side: (i % half, 0))
@@ -238,22 +238,27 @@
     return (keys >= start) & (keys <= queries)
 
 
-def forward_body(span, spot, low, query, keys, values, start, out, log_total):
-    i = pl.program_id(1)
-    rows, size = query.shape
+def forward_body(span, size, spot, low, query, keys, values, start, out, log_total):
+    i = pl.program_id(0)
+    rows = query.shape[0]
     scale = 1.0 / math.sqrt(size)
+    heads = [slice(at, at + size) for at in range(0, query.shape[1], size)]
 
     def step(j, carry):
-        peak, total, summed = carry
         at = pl.multiple_of(j * span, span)
-        scores = dot(keys[pl.ds(at, span), :], query[...], 1, 1) * scale
-        scores = jnp.where(allowed(start[...], at, i * rows, scores.shape), scores, masked_score)
-        new_peak = jnp.maximum(peak, jnp.max(scores, axis=0, keepdims=True))
-        shrink = jnp.exp(peak - new_peak)
-        exponent = jnp.exp(scores - new_peak)
-        total = total * shrink + jnp.sum(exponent, axis=0, keepdims=True)
-        summed = summed * shrink + dot(values[pl.ds(at, span), :], exponent.astype(b16), 0, 0)
-        return new_peak, total, summed
+        here = pl.ds(at, span)
+        mask = allowed(start[...], at, i * rows, (span, rows))
+        after = []
+        for head, (peak, total, summed) in zip(heads, carry):
+            scores = dot(keys[here, head], query[:, head], 1, 1) * scale
+            scores = jnp.where(mask, scores, masked_score)
+            new_peak = jnp.maximum(peak, jnp.max(scores, axis=0, keepdims=True))
+            shrink = jnp.exp(peak - new_peak)
+            exponent = jnp.exp(scores - new_peak)
+            total = total * shrink + jnp.sum(exponent, axis=0, keepdims=True)
+            summed = summed * shrink + dot(values[here, head], exponent.astype(b16), 0, 0)
+            after.append((new_peak, total, summed))
+        return tuple(after)
 
     begin = (
         jnp.full((1, rows), masked_score, f32),
@@ -261,9 +266,10 @@
         jnp.zeros((size, rows), f32),
     )
     last = ((i + 1) * rows + span - 1) // span
-    peak, total, summed = lax.fori_loop(low[i], last, step, begin)
-    out[...] = jnp.transpose(summed / total).astype(b16)
-    log_total[0] = peak + jnp.log(total)
+    carry = lax.fori_loop(low[i], last, step, (begin,) * len(heads))
+    for at, (head, (peak, total, summed)) in enumerate(zip(heads, carry)):
+        out[:, head] = jnp.transpose(summed / total).astype(b16)
+        log_total[at : at + 1, :] = peak + jnp.log(total)
 
 
 def flash_forward(query, keys, values, start, spot, block, size):
@@ -272,60 +278,81 @@
     blocks = rows // block
     span = min(512, rows)
     low = start.reshape(blocks, block)[:, 0] // span
-    return pl.pallas_call(
-        functools.partial(forward_body, span),
+    full = pl.BlockSpec((rows, width), lambda i, spot, low: (0, 0))
+    return pl.pallas_call(
+        functools.partial(forward_body, span, size),
         grid_spec=pltpu.PrefetchScalarGridSpec(
             num_scalar_prefetch=2,
-            grid=(heads, blocks),
+            grid=(blocks,),
             in_specs=[
-                pl.BlockSpec((block, size), lambda h, i, spot, low: (i, h)),
-                pl.BlockSpec((rows, size), lambda h, i, spot, low: (0, h)),
-                pl.BlockSpec((rows, size), lambda h, i, spot, low: (0, h)),
-                pl.BlockSpec((1, block), lambda h, i, spot, low: (0, i)),
+                pl.BlockSpec((block, width), lambda i, spot, low: (i, 0)),
+                full,
+                full,
+                pl.BlockSpec((1, block), lambda i, spot, low: (0, i)),
             ],
             out_specs=[
-                pl.BlockSpec((block, size), lambda h, i, spot, low: (spot[i], h)),
-                pl.BlockSpec((1, 1, block), lambda h, i, spot, low: (h, 0, i)),
+                pl.BlockSpec((block, width), lambda i, spot, low: (spot[i], 0)),
+                pl.BlockSpec((heads, block), lambda i, spot, low: (0, i)),
             ],
         ),
         out_shape=[
             jax.ShapeDtypeStruct((rows, width), b16),
-            jax.ShapeDtypeStruct((heads, 1, rows), f32),
+            jax.ShapeDtypeStruct((heads, rows), f32),
         ],
-        compiler_params=params(2),
+        compiler_params=params(1),
         cost_estimate=lasting(18),
     )(spot, low, query, keys, values, start[None])
 
 
 def backward_body(
-    span, spot, low, query, keys, values, start, log_total, grad, out, d_query, d_keys, d_values
+    span,
+    size,
+    spot,
+    low,
+    query,
+    keys,
+    values,
+    start,
+    log_total,
+    grad,
+    out,
+    d_query,
+    d_keys,
+    d_values,
 ):
-    i = pl.program_id(1)
-    rows, size = query.shape
+    i = pl.program_id(0)
+    rows = query.shape[0]
     scale = 1.0 / math.sqrt(size)
+    heads = [slice(at, at + size) for at in range(0, query.shape[1], size)]
 
     @pl.when(i == 0)
     def _():
         d_keys[...] = jnp.zeros_like(d_keys)
         d_values[...] = jnp.zeros_like(d_values)
 
-    delta = row_sums(grad[...].astype(f32) * out[...].astype(f32))
-
-    def step(j, summed):
+    deltas = [row_sums(grad[:, head].astype(f32) * out[:, head].astype(f32)) for head in heads]
+
+    def step(j, carry):
         at = pl.multiple_of(j * span, span)
         here = pl.ds(at, span)
-        scores = dot(keys[here, :], query[...], 1, 1) * scale
-        mask = allowed(start[...], at, i * rows, scores.shape)
-        soft = jnp.where(mask, jnp.exp(scores - log_total[0]), 0.0)
-        d_soft = dot(values[here, :], grad[...], 1, 1)
-        d_scores = (soft * (d_soft - delta) * scale).astype(b16)
-        d_values[here, :] += dot(soft.astype(b16), grad[...], 1, 0)
-        d_keys[here, :] += dot(d_scores, query[...], 1, 0)
-        return summed + dot(keys[here, :], d_scores, 0, 0)
+        mask = allowed(start[...], at, i * rows, (span, rows))
+        after = []
+        for which, (head, summed) in enumerate(zip(heads, carry)):
+            scores = dot(keys[here, head], query[:, head], 1, 1) * scale
+            soft = jnp.where(mask, jnp.exp(scores - log_total[which : which + 1, :]), 0.0)
+            d_soft = dot(values[here, head], grad[:, head], 1, 1)
+            d_scores = (soft * (d_soft - deltas[which]) * scale).astype(b16)
+            d_values[here, head] += dot(soft.astype(b16), grad[:, head], 1, 0)
+            d_keys[here, head] += dot(d_scores, query[:, head], 1, 0)
+            after.append(summed + dot(keys[here, head], d_scores, 0, 0))
+        return tuple(after)
 
     last = ((i + 1) * rows + span - 1) // span
-    summed = lax.fori_loop(low[i], last, step, jnp.zeros((size, rows), f32))
-    d_query[...] = jnp.transpose(summed)
+    carry = lax.fori_loop(
+        low[i], last, step, (jnp.zeros((size, rows), f32),) * len(heads)
+    )
+    for head, summed in zip(heads, carry):
+        d_query[:, head] = jnp.transpose(summed)
 
 
 def flash_backward(query, keys, values, start, log_total, grad, out, spot, block, size):
@@ -334,27 +361,27 @@
     blocks = rows // block
     span = min(512, rows)
     low = start.reshape(blocks, block)[:, 0] // span
-    natural = pl.BlockSpec((block, size), lambda h, i, spot, low: (i, h))
-    moved = pl.BlockSpec((block, size), lambda h, i, spot, low: (spot[i], h))
-    full = pl.BlockSpec((rows, size), lambda h, i, spot, low: (0, h))
-    return pl.pallas_call(
-        functools.partial(backward_body, span),
+    natural = pl.BlockSpec((block, width), lambda i, spot, low: (i, 0))
+    moved = pl.BlockSpec((block, width), lambda i, spot, low: (spot[i], 0))
+    full = pl.BlockSpec((rows, width), lambda i, spot, low: (0, 0))
+    return pl.pallas_call(
+        functools.partial(backward_body, span, size),
         grid_spec=pltpu.PrefetchScalarGridSpec(
             num_scalar_prefetch=2,
-            grid=(heads, blocks),
+            grid=(blocks,),
             in_specs=[
                 natural,
                 full,
                 full,
-                pl.BlockSpec((1, block), lambda h, i, spot, low: (0, i)),
-                pl.BlockSpec((1, 1, block), lambda h, i, spot, low: (h, 0, i)),
+                pl.BlockSpec((1, block), lambda i, spot, low: (0, i)),
+                pl.BlockSpec((heads, block), lambda i, spot, low: (0, i)),
                 moved,
                 moved,
             ],
             out_specs=[natural, full, full],
         ),
         out_shape=[jax.ShapeDtypeStruct((rows, width), f32)] * 3,
-        compiler_params=params(2),
+        compiler_params=params(1),
         cost_estimate=lasting(22),
     )(spot, low, query, keys, values, start[None], log_total, grad, out)
 
@@ -558,6 +585,68 @@
     )(d_gate, d_up, w_both, w_both, *received)
 
 
+def columns_body(side, query, key, val, out_weight, out):
+    width = query.shape[1]
+    for at, piece in enumerate((query, key, val)):
+        out[:, at * width : (at + 1) * width] = piece[...].astype(b16)
+    out[:, 3 * width :] = jnp.transpose(out_weight[...]).astype(b16)
+
+
+def attention_columns(side, query, key, val, out_weight):
+    piece, width = query.shape[0], query.shape[1] // 2
+    upper = pl.BlockSpec((piece, width), lambda i, side: (0, side[0]))
+    return pl.pallas_call(
+        columns_body,
+        grid_spec=pltpu.PrefetchScalarGridSpec(
+            num_scalar_prefetch=1,
+            grid=(1,),
+            in_specs=[
+                upper,
+                upper,
+                upper,
+                pl.BlockSpec((width, piece), lambda i, side: (side[0], 0)),
+            ],
+            out_specs=pl.BlockSpec((piece, 4 * width), lambda i, side: (0, 0)),
+        ),
+        out_shape=jax.ShapeDtypeStruct((piece, 4 * width), b16),
+        compiler_params=params(1, 60),
+        cost_estimate=lasting(2),
+    )(side, query, key, val, out_weight)
+
+
+def paired_columns_body(side, query, key, val, out_weight, other, out):
+    @pl.when(pl.program_id(0) == side[0])
+    def _():
+        columns_body(side, query, key, val, out_weight, out)
+
+    @pl.when(pl.program_id(0) != side[0])
+    def _():
+        out[...] = other[...]
+
+
+def paired_columns(side, query, key, val, out_weight, other):
+    piece, width = query.shape[0], query.shape[1] // 2
+    upper = pl.BlockSpec((piece, width), lambda i, side: (0, side[0]))
+    return pl.pallas_call(
+        paired_columns_body,
+        grid_spec=pltpu.PrefetchScalarGridSpec(
+            num_scalar_prefetch=1,
+            grid=(2,),
+            in_specs=[
+                upper,
+                upper,
+                upper,
+                pl.BlockSpec((width, piece), lambda i, side: (side[0], 0)),
+                pl.BlockSpec((piece, 4 * width), lambda i, side: (0, 0)),
+            ],
+            out_specs=pl.BlockSpec((piece, 4 * width), lambda i, side: (i, 0)),
+        ),
+        out_shape=jax.ShapeDtypeStruct((2 * piece, 4 * width), b16),
+        compiler_params=params(1, 60),
+        cost_estimate=lasting(2),
+    )(side, query, key, val, out_weight, other)
+
+
 def flip_body(value, out):
     out[...] = jnp.transpose(value[...])
 
@@ -634,19 +723,23 @@
         step = min(256, half)
         count = half // step
         mine = pl.BlockSpec((step, columns), lambda j, i, flag: (j * count + i, 0))
-        halves = pl.BlockSpec((columns, step), lambda j, i, flag: (0, i))
+        halves = pl.BlockSpec((columns, step), lambda j, i, flag: (0, column * count + i))
+        both = pl.BlockSpec(
+            (None, columns, step), lambda j, i, flag: (flag[0], 0, column * count + i)
+        )
     else:
         half = columns // 2
         step = min(128, rows)
         count = rows // step
         mine = pl.BlockSpec((step, half), lambda j, i, flag: (i, j))
         halves = pl.BlockSpec((step, half), lambda j, i, flag: (i, column))
+        both = pl.BlockSpec((None, step, half), lambda j, i, flag: (flag[0], i, column))
     return pl.pallas_call(
         functools.partial(adam_body, turned),
         grid_spec=pltpu.PrefetchScalarGridSpec(
             num_scalar_prefetch=1,
             grid=(2, count),
-            in_specs=[mine] * 3 + [halves] * 2,
+            in_specs=[mine] * 3 + [both, halves],
             out_specs=[mine] * 4,
         ),
         out_shape=[jax.ShapeDtypeStruct(weight.shape, f32)] * 4,
@@ -683,7 +776,7 @@
     docs_all = gather_axis(docs_here, CX)
     gains = jnp.concatenate([gain.astype(b16).reshape(-1) for gain in masters[7:]])[None]
     gains = gather_axis(gather_axis(gather_axis(gains, CX), SL), SH).astype(f32)
-    gains, docs_all, inputs, *first = tie(gains, docs_all, inputs, *masters[:7])
+    first = list(masters[:7])
 
     def columns_of(weight, index, count):
         return lax.dynamic_slice_in_dim(weight, index * count, count, 1).astype(b16)
@@ -698,19 +791,19 @@
     def over_shard(value):
         return lax.all_gather(value, SHARD, axis=0, tiled=True)
 
-    mine, theirs = over_ctx(first[:3] + [flip(first[3].astype(b16))], wide)
-    theirs, local_rows = tie(theirs, my_rows(inputs))
-    columns = pair(mine, theirs, CX)
-    w_qkv, w_out = over_shard(columns[:, : 3 * wide]), columns[:, 3 * wide :]
+    theirs = swap(attention_columns(1 - y[None], *first[:4]), CX)
+    theirs, local_rows, gains, docs_all = tie(theirs, my_rows(inputs), gains, docs_all)
+    w_attn = over_shard(paired_columns(y[None], *first[:4], theirs))
 
     remote, gate_w, up_w, down_w = tie(swap(local_rows, CX), *first[4:])
     remote = gather_axis(remote, TX)
     gate_w = pair(*over_ctx([gate_w], hidden), CX)
     remote, gate_w = tie(remote, gate_w)
     remote = gather_axis(remote, TC)
-    w_qkv, remote, w_out, gate_w = tie(w_qkv, remote, w_out, gate_w)
-    w_out = over_shard(w_out)
     up_w = pair(*over_ctx([up_w], hidden), CX)
+    w_attn, remote, w_both = tie(w_attn, remote, jnp.concatenate([gate_w, up_w], axis=1))
+    w_both = over_shard(w_both)
+    w_qkv, w_out = w_attn[:, : 3 * wide], w_attn[:, 3 * wide :]
     down_w = pair(*over_ctx([flip(down_w.astype(b16))], hidden), CX)
 
     count = heads_here * head_piece
@@ -745,11 +838,10 @@
     cosine = jnp.concatenate([cosine, cosine], axis=1)
     sine = jnp.concatenate([-sine, sine], axis=1)
 
-    raw, squares = project(y[None], inputs, remote, w_qkv)
+    raw, squares = project(y[None], inputs, remote, w_attn)
     inverse = lax.rsqrt(plane_sum(squares) / width + norm_eps)
     query, key, val = prepare(raw, inverse, head_gain, cosine, sine)
-    query, w_out, gate_w, up_w = tie(query, w_out, gate_w, up_w)
-    w_both = over_shard(jnp.concatenate([gate_w, up_w], axis=1))
+    query, down_w = tie(query, down_w)
     spot = block_places(CX)
     attended, log_total = flash_forward(query, key, val, own_start, spot, block, size)
     group = length // 2
@@ -786,7 +878,7 @@
 
     def to_owner(summed):
         summed = summed.reshape(2, piece, -1)
-        return part(summed, y, 0), swap(part(summed, 1 - y, 0), CX)
+        return summed, swap(part(summed, 1 - y, 0), CX)
 
     *d_ffn, block_rows = tie(*d_ffn, block_rows)
     block_rows = over_chips(block_rows)
@@ -796,12 +888,17 @@
     d_gate, d_up = zip(
         *[ffn_backward(d, w_down, g, u) for d, g, u in zip(d_ffn, gate_pre, up_pre)]
     )
-    grad_gate = both(res, d_gate)
+    block_rows, *turned = tie(block_rows, *d_gate, *d_up)
+    d_gate, d_up = turned[:2], turned[2:]
+    theirs, *turned = tie(ffn_residual(d_gate[1], d_up[1], w_both), *d_gate)
+    d_gate = turned
+    grad_gate = dot(res[0], d_gate[0], 0, 0)
+    theirs, grad_gate = tie(swap(theirs, TC), grad_gate)
+    both_ffn = ffn_residual(d_gate[0], d_up[0], w_both, theirs)
+    both_ffn, *turned = tie(both_ffn, *d_gate, *d_up)
+    d_gate, d_up = turned[:2], turned[2:]
+    grad_gate = (grad_gate + dot(res[1], d_gate[1], 0, 0)).astype(b16)
     grad_gate = to_shard(grad_gate)
-    both_ffn = ffn_residual(
-        d_gate[0], d_up[0], w_both, swap(ffn_residual(d_gate[1], d_up[1], w_both), TC)
-    )
-    both_ffn, grad_down, block_rows, *d_up = tie(both_ffn, grad_down, block_rows, *d_up)
     back_ffn = collect(both_ffn, CX)
     block_theirs = swap(block_rows, TC)
     grad_upward = both(res, d_up)
@@ -820,14 +917,13 @@
     )
     down_halves, gate_halves = to_owner(grad_down), to_owner(grad_gate)
     d_att = jnp.concatenate([dot(d, w_out, 1, 0).astype(b16) for d in d_branch], 0)
-    grad_out_w = both(d_branch, [attended[:group], attended[group:]])
-    d_att, grad_out_w = tie(d_att, grad_out_w)
     d_query, d_key, d_val = flash_backward(
         query, key, val, own_start, log_total, d_att, attended, spot, block, size
     )
-    grad_out_w = to_shard(grad_out_w)
-    d_query, grad_upward, *turned = tie(d_query, grad_upward, *down_halves, *gate_halves)
-    down_halves, gate_halves = turned[:2], turned[2:]
+    d_query, *turned = tie(d_query, *d_branch, *down_halves, *gate_halves)
+    d_branch, down_halves, gate_halves = turned[:2], turned[2:4], turned[4:]
+    grad_out_w = both(d_branch, [attended[:group], attended[group:]])
+    d_query, grad_out_w = tie(d_query, grad_out_w)
     sums, grad_heads = turned_sums(raw, inverse, head_gain, cosine, sine, d_query, d_key)
     plane_sums = plane_sum(
         jnp.concatenate([sums, grad_attn_gain[None], grad_ffn_gain[None]])
@@ -835,31 +931,31 @@
     means = plane_sums[:2] / width
     small = jnp.concatenate([plane_sums[2:].reshape(1, -1), grad_heads.reshape(1, -1)], 1)
     small = sum_axis(sum_axis(small, SL), SH)
-    means, grad_out_w, grad_upward = tie(means, grad_out_w, grad_upward)
     d_qkv, moved = raw_grads(
         raw, inverse, head_gain, cosine, sine, d_query, d_key, d_val, means, spot, block
     )
 
     sides = d_qkv.reshape(2, rows, 3 * wide)
     grad_qkv = both((inputs, remote), (part(sides, y, 0), part(sides, 1 - y, 0)))
-    grad_qkv, moved = tie(grad_qkv, moved)
-    grad_qkv = to_shard(grad_qkv)
-    up_halves = to_owner(grad_upward)
+    grad_attn = to_shard(jnp.concatenate([grad_qkv, grad_out_w], axis=1))
     both_attn = across(dot(moved[:group], w_qkv, 1, 1), dot(moved[group:], w_qkv, 1, 1))
-    both_attn, *up_halves = tie(both_attn, *up_halves)
+    both_attn, grad_upward = tie(both_attn, grad_upward)
     back_attn = collect(both_attn, CX)
     down_step = adam(*triple(6), *down_halves, y[None], turned=True)
     gate_step = adam(*triple(4), *gate_halves, y[None])
-    up_step = adam(*triple(5), *up_halves, y[None])
     block_share = assemble(block_rows, block_theirs, block)
-    back_attn, small, block_share, *turned = tie(
-        back_attn, small, block_share, *down_step, *gate_step, *up_step
-    )
-    down_step, gate_step, up_step = turned[:4], turned[4:8], turned[8:]
-    out_step = adam(*triple(3), *to_owner(grad_out_w), y[None], turned=True)
-    grad_qkv = to_owner(grad_qkv)
+    back_attn, small, grad_upward, *turned = tie(
+        back_attn, small, grad_upward, *down_step, *gate_step
+    )
+    down_step, gate_step = turned[:4], turned[4:]
     input_rows = over_chips((grad_res + back_attn).astype(b16))
+    up_step = adam(*triple(5), *to_owner(grad_upward), y[None])
+    input_rows, grad_attn, block_share, *up_step = tie(
+        input_rows, grad_attn, block_share, *up_step
+    )
+    attn_halves = to_owner(grad_attn)
     input_share = assemble(input_rows, swap(input_rows, TC), block)
+    input_share, *attn_halves = tie(input_share, *attn_halves)
 
     index = lax.axis_index(SHARD) * 2 + y
     wide_sums = lax.dynamic_slice_in_dim(
@@ -869,8 +965,8 @@
     head_sums = pair(head_sums, swap(head_sums, CX), CX, 1).reshape(2, heads_here, size)
     head_sums = lax.dynamic_slice_in_dim(head_sums, index * head_piece, head_piece, 2)
 
-    stepped = [adam(*triple(i), *grad_qkv, y[None], column=i) for i in range(3)]
-    stepped += [out_step, gate_step, up_step, down_step]
+    stepped = [adam(*triple(i), *attn_halves, y[None], i == 3, i) for i in range(4)]
+    stepped += [gate_step, up_step, down_step]
     for i, grad in enumerate((head_sums[0], head_sums[1], wide_sums[0], wide_sums[1])):
         stepped.append((grad,) + adam_step(*triple(7 + i), grad))
     return tuple(

time: 939 us -> 814 us (0.87)
  waiting for transfers between devices: 441 us -> 354 us
  Pallas kernels: 177 us -> 160 us
  starting transfers between devices: 77.8 us -> 64.8 us
    all_gather x4 -> x3, waiting for transfers between devices: 81.1 us -> 40.9 us  [over_shard(): return lax.all_gather(value, SHARD, axis=0, tiled=True)]
    ppermute x76 -> x75, waiting for transfers between devices: 342 us -> 309 us  [swap(): return lax.ppermute(value, axis, [(0, 1), (1, 0)])]
    reduce_scatter x5 -> x4, waiting for transfers between devices: 17.6 us -> 3.9 us  [to_shard(): return lax.psum_scatter(partial, SHARD, scatter_dimension=0, tiled=True)]
    ppermute x76 -> x75, starting transfers between devices: 76.5 us -> 63.7 us  [swap(): return lax.ppermute(value, axis, [(0, 1), (1, 0)])]
    pallas_call x2 -> x4, Pallas kernels: 44.5 us -> 38.9 us  [the longest x1 17.6 us: flash_backward(): pl.pallas_call(functools.partial(backward_body, span, size), grid_spec=pl...]
    unnamed x277 -> x271, local copies, waits for them, and re-layouts: 54.3 us -> 51.6 us
  transfers between devices with their start and end apart: 85 -> 82, of which waited for: 52 -> 52; matrix products, arithmetic and copies ran while one was open for 12% -> 17% of each run, Pallas kernels for 17% -> 18%
where the time goes in v2:
time: 814 us; the launch traced here: 809 us
  waiting for transfers between devices  354 us (43%)
  Pallas kernels  160 us (20%)
  matrix products  89.6 us (11%)
  local copies, waits for them, and re-layouts  68.4 us (8%)
  starting transfers between devices  64.8 us (8%)
  other arithmetic  55.7 us (7%)
  between operations  16.4 us (2%)
    ppermute x75, waiting for transfers between devices, swap(): return lax.ppermute(value, axis, [(0, 1), (1, 0)])  309 us
    dot_general x18, matrix products, dot(): lax.dot_general(a, b, (((ca,), (cb,)), ((), ())), preferred_element_type=...  89.6 us
    ppermute x75, starting transfers between devices, swap(): return lax.ppermute(value, axis, [(0, 1), (1, 0)])  63.7 us
    unnamed x271, local copies, waits for them, and re-layouts  51.6 us
    all_gather x3, waiting for transfers between devices, over_shard(): return lax.all_gather(value, SHARD, axis=0, tiled=True)  40.9 us
    pallas_call x2, Pallas kernels, ffn_forward(): pl.pallas_call(functools.partial(ffn_forward_body, len(blocks)), grid=(co...  24.9 us
    pallas_call x2, Pallas kernels, ffn_residual(): pl.pallas_call(ffn_residual_body, grid=(width // step,), in_specs=[full,...  23.3 us
    pallas_call x7, Pallas kernels, adam(): pl.pallas_call(functools.partial(adam_body, turned), grid_spec=pltpu.Pref...  23 us
  transfers between devices with their start and end apart: 82, of which 52 were waited for; matrix products, arithmetic and copies ran while one was open for 17% of the time, Pallas kernels for 18%

profile of v2, /device:TPU:0, one launch (start us, length us, event | category | flops | bytes accessed | tf_op | source)
XLA Modules:
  0.0 808.6 jit_solution(2745508831385187084)
XLA Ops:
  23.7 5.3 collective-permute-done.4
  32.0 23.6 %collective-permute-done.5 = bf16[256,2048]{1,0:T(8,128)(2,1)} collective-permute-done((bf16[256,2048]{1,0:T(8,128)(2,1)S(1)}, bf16[256,2048]{1,0:T(8,128)(2,1)}, u32[]{:S(2)}, u32[]{:S(2)}) %collective-permute-start.5) | collective-permute-done | bytes 1048608 | tf_op jit(solution)/shard_map/ppermute | solution.py:38
  58.5 10.9 %collective-permute-done.7 = bf16[256,1024]{1,0:T(8,128)(2,1)S(1)} collective-permute-done((bf16[256,1024]{1,0:T(8,128)(2,1)S(1)}, bf16[256,1024]{1,0:T(8,128)(2,1)S(1)}, u32[]{:S(2)}, u32[]{:S(2)}) %collective-permute-start.7) | collective-permute-done | bytes 524320 | tf_op jit(solution)/shard_map/ppermute | solution.py:38
  72.3 6.5 collective-permute-done.6
  85.5 13.7 %collective-permute-done.9 = bf16[256,1024]{1,0:T(8,128)(2,1)S(1)} collective-permute-done((bf16[256,1024]{1,0:T(8,128)(2,1)}, bf16[256,1024]{1,0:T(8,128)(2,1)S(1)}, u32[]{:S(2)}, u32[]{:S(2)}) %collective-permute-start.9) | collective-permute-done | bytes 524320 | tf_op jit(solution)/shard_map/ppermute | solution.py:38
  102.3 6.1 maximum_select_fusion.remote
  113.8 5.5 fusion.33
  130.9 8.8 %shard_map.701 = (f32[2048,768]{1,0:T(8,128)S(1)}, f32[2,2048]{1,0:T(2,128)S(1)}) custom-call(s32[1]{0:T(128)} %bitcast.2.side.flag, bf16[1024,2048]{1,0:T(8,128)(2,1)S(1)} %bitcast.109, bf16[1024,2048]{1,0:T(8,128)(2,1)S(1)} %copy-done.8, bf16[2048,1024]{1,0:T(8,128)(2,1)S(1)} %copy-done.11), custom_call_target="tpu_custom_call" | custom-call | bytes 6000000 | tf_op jit(solution)/shard_map/pallas_call | solution.py:168
  156.7 16.7 %shard_map.704 = (bf16[2048,256]{1,0:T(8,128)(2,1)S(1)}, f32[2,2048]{1,0:T(2,128)S(1)}) custom-call(s32[8]{0:T(128)S(1)} %fusion.44.spot, s32[8]{0:T(128)S(1)} %and_select_fusion.low, bf16[2048,256]{1,0:T(8,128)(2,1)S(1)} %get-tuple-element.195.query, bf16[2048,256]{1,0:T(8,128)(2,1)S(1)} %get-tuple-element.196.keys, ...), custom_call_target="tpu_custom_call" | custom-call | bytes 9000000 | tf_op jit(solution)/shard_map/pallas_call | solution.py:282
  174.8 7.1 collective-permute-done.14
  186.0 11.4 %collective-permute-done.15 = bf16[128,2048]{1,0:T(8,128)(2,1)S(1)} collective-permute-done((bf16[128,2048]{1,0:T(8,128)(2,1)S(1)}, bf16[128,2048]{1,0:T(8,128)(2,1)S(1)}, u32[]{:S(2)}, u32[]{:S(2)}) %collective-permute-start.15) | collective-permute-done | bytes 524320 | tf_op jit(solution)/shard_map/ppermute | solution.py:38
  201.3 21.3 %collective-permute-done.16 = bf16[256,2048]{1,0:T(8,128)(2,1)S(1)} collective-permute-done((bf16[256,2048]{1,0:T(8,128)(2,1)S(1)}, bf16[256,2048]{1,0:T(8,128)(2,1)S(1)}, u32[]{:S(2)}, u32[]{:S(2)}) %collective-permute-start.16) | collective-permute-done | bytes 1048608 | tf_op jit(solution)/shard_map/ppermute | solution.py:38
  227.6 35.6 %all-gather.6.cloned.1.call-done.refs_5_.refs_6_.w_gate.w_up = bf16[2048,2048]{1,0:T(8,128)(2,1)} async-done(((bf16[512,2048]{1,0:T(8,128)(2,1)}), bf16[2048,2048]{1,0:T(8,128)(2,1)}) %all-gather.6.cloned.1.call-update) | async-done | bytes 8388624 | tf_op jit(solution)/shard_map/all_gather | solution.py:792
  266.5 22.2 %collective-permute-done.20.refs_2_ = bf16[256,2048]{1,0:T(8,128)(2,1)S(1)} collective-permute-done((bf16[256,2048]{1,0:T(8,128)(2,1)S(1)}, bf16[256,2048]{1,0:T(8,128)(2,1)S(1)}, u32[]{:S(2)}, u32[]{:S(2)}) %collective-permute-start.20) | collective-permute-done | bytes 1048608 | tf_op jit(solution)/shard_map/ppermute | solution.py:38
  292.4 9.6 %collective-permute-done.21.refs_3_ = bf16[128,2048]{1,0:T(8,128)(2,1)S(1)} collective-permute-done((bf16[128,2048]{1,0:T(8,128)(2,1)S(1)}, bf16[128,2048]{1,0:T(8,128)(2,1)S(1)}, u32[]{:S(2)}, u32[]{:S(2)}) %collective-permute-start.21) | collective-permute-done | bytes 524320 | tf_op jit(solution)/shard_map/ppermute | solution.py:38
  306.6 11.7 %shard_map.705 = (bf16[1024,2048]{1,0:T(8,128)(2,1)S(1)}, bf16[1024,1024]{1,0:T(8,128)(2,1)S(1)}, bf16[1024,1024]{1,0:T(8,128)(2,1)S(1)}, bf16[1024,1024]{1,0:T(8,128)(2,1)S(1)}) custom-call(bf16[256,2048]{1,0:T(8,128)(2,1)S(1)} %fusion.20.refs_0_, bf16[256,2048]{1,0:T(8,128)(2,1)S(1)} %collective-permute-done.19.refs_1_, ...), custom_call_target="tpu_custom_call" | custom-call | bytes 5000000 | tf_op jit(solution)/shard_map/pallas_call | solution.py:514
  324.4 13.2 %shard_map.706 = (bf16[1024,2048]{1,0:T(8,128)(2,1)S(1)}, bf16[1024,1024]{1,0:T(8,128)(2,1)S(1)}, bf16[1024,1024]{1,0:T(8,128)(2,1)S(1)}, bf16[1024,1024]{1,0:T(8,128)(2,1)S(1)}) custom-call(bf16[256,2048]{1,0:T(8,128)(2,1)S(1)} %collective-permute-done.23.refs_0_, bf16[256,2048]{1,0:T(8,128)(2,1)} %collective-permute-done.24.refs_1_, ...), custom_call_target="tpu_custom_call" | custom-call | bytes 5000000 | tf_op jit(solution)/shard_map/pallas_call | solution.py:514
  344.4 7.5 convolution_convert_fusion.2
  352.0 7.1 collective-permute-done.28
  359.1 5.2 add_convert_fusion.4
  367.6 11.0 %collective-permute-done.29 = bf16[128,2048]{1,0:T(8,128)(2,1)S(1)} collective-permute-done((bf16[128,2048]{1,0:T(8,128)(2,1)S(1)}, bf16[128,2048]{1,0:T(8,128)(2,1)S(1)}, u32[]{:S(2)}, u32[]{:S(2)}) %collective-permute-start.29) | collective-permute-done | bytes 524320 | tf_op jit(solution)/shard_map/ppermute | solution.py:38
  382.3 21.9 %collective-permute-done.30 = bf16[256,2048]{1,0:T(8,128)(2,1)S(1)} collective-permute-done((bf16[256,2048]{1,0:T(8,128)(2,1)S(1)}, bf16[256,2048]{1,0:T(8,128)(2,1)S(1)}, u32[]{:S(2)}, u32[]{:S(2)}) %collective-permute-start.30) | collective-permute-done | bytes 1048608 | tf_op jit(solution)/shard_map/ppermute | solution.py:38
  411.3 21.7 %collective-permute-done.34 = bf16[256,2048]{1,0:T(8,128)(2,1)S(1)} collective-permute-done((bf16[256,2048]{1,0:T(8,128)(2,1)S(1)}, bf16[256,2048]{1,0:T(8,128)(2,1)S(1)}, u32[]{:S(2)}, u32[]{:S(2)}) %collective-permute-start.34) | collective-permute-done | bytes 1048608 | tf_op jit(solution)/shard_map/ppermute | solution.py:38
  437.0 7.5 collective-permute-done.35
  448.2 4.7 fusion.66
  454.9 6.4 add_convert_fusion.3
  470.4 7.6 shard_map.708
  478.1 7.6 shard_map.707
  489.9 11.4 %shard_map.709 = bf16[1024,2048]{1,0:T(8,128)(2,1)S(1)} custom-call(bf16[1024,1024]{1,0:T(8,128)(2,1)S(1)} %get-tuple-element.238.d_gate, bf16[1024,1024]{1,0:T(8,128)(2,1)S(1)} %get-tuple-element.235.d_up, bf16[2048,2048]{1,0:T(8,128)(2,1)S(1)} %bitcast.101, bf16[2048,2048]{1,0:T(8,128)(2,1)S(1)} %bitcast.101), custom_call_target="tpu_custom_call" | custom-call | bytes 4500000 | tf_op jit(solution)/shard_map/pallas_call | solution.py:571
  501.4 6.8 fusion.67
  508.5 12.0 %shard_map.710 = bf16[1024,2048]{1,0:T(8,128)(2,1)S(1)} custom-call(bf16[1024,1024]{1,0:T(8,128)(2,1)S(1)} %copy-done.43, bf16[1024,1024]{1,0:T(8,128)(2,1)S(1)} %get-tuple-element.233.d_up, bf16[2048,2048]{1,0:T(8,128)(2,1)S(1)} %bitcast.101, bf16[2048,2048]{1,0:T(8,128)(2,1)S(1)} %bitcast.101, bf16[1024,2048]{1,0:T(8,128)(2,1)S(1)} %collective-permute-done.43.rest_0_), custom_call_target="tpu_custom_call" | custom-call | bytes 4500000 | tf_op jit(solution)/shard_map/pallas_call | solution.py:571
  522.5 8.3 %add_convert_fusion.1 = bf16[2048,1024]{1,0:T(8,128)(2,1)} fusion(f32[2048,1024]{1,0:T(8,128)} %fusion.67, bf16[1024,2048]{1,0:T(8,128)(2,1)S(1)} %copy-done.81, bf16[1024,1024]{1,0:T(8,128)(2,1)S(1)} %copy-done.47), kind=kOutput, calls=%fused_computation.1 | convolution fusion | flops 4299161600 | bytes 18874368 | tf_op jit(solution)/shard_map/dot_general | solution.py:34
  535.4 6.4 fusion.68
  541.9 5.1 collective-permute-done.44
  553.8 6.1 add_convert_fusion.2
  559.9 15.1 %collective-permute-done.45 = bf16[256,2048]{1,0:T(8,128)(2,1)S(1)} collective-permute-done((bf16[256,2048]{1,0:T(8,128)(2,1)}, bf16[256,2048]{1,0:T(8,128)(2,1)S(1)}, u32[]{:S(2)}, u32[]{:S(2)}) %collective-permute-start.45) | collective-permute-done | bytes 1048608 | tf_op jit(solution)/shard_map/ppermute | solution.py:38
  584.0 20.5 %collective-permute-done.49 = bf16[256,2048]{1,0:T(8,128)(2,1)} collective-permute-done((bf16[256,2048]{1,0:T(8,128)(2,1)S(1)}, bf16[256,2048]{1,0:T(8,128)(2,1)}, u32[]{:S(2)}, u32[]{:S(2)}) %collective-permute-start.49) | collective-permute-done | bytes 1048608 | tf_op jit(solution)/shard_map/ppermute | solution.py:38
  633.6 17.6 %shard_map.711 = (f32[2048,256]{1,0:T(8,128)S(1)}, f32[2048,256]{1,0:T(8,128)S(1)}, f32[2048,256]{1,0:T(8,128)S(1)}) custom-call(s32[8]{0:T(128)S(1)} %copy-done.77, s32[8]{0:T(128)S(1)} %copy-done.79, bf16[2048,256]{1,0:T(8,128)(2,1)S(1)} %copy-done.32, bf16[2048,256]{1,0:T(8,128)(2,1)S(1)} %copy-done.34, bf16[2048,256]{1,0:T(8,128)(2,1)S(1)} %copy-done.36, ...), custom_call_target="tpu_custom_call" | custom-call | bytes 11000000 | tf_op jit(solution)/shard_map/pallas_call | solution.py:367
  674.7 5.0 convolution_convert_fusion.1
  680.4 5.9 fusion.14
  693.2 9.2 %add_convert_fusion = bf16[1024,2048]{1,0:T(8,128)(2,1)} fusion(bf16[1024,2048]{1,0:T(8,128)(2,1)} %collective-permute-done.63, bf16[2048,1024]{1,0:T(8,128)(2,1)} %all-gather.4.cloned.1.call-done.weight, bf16[2048,768]{1,0:T(8,128)(2,1)} %copy-done.85), kind=kOutput, calls=%fused_computation | convolution fusion | flops 3227516928 | bytes 13107200 | tf_op jit(solution)/shard_map/dot_general | solution.py:34
  706.6 12.6 %collective-permute-done.64 = bf16[128,2048]{1,0:T(8,128)(2,1)S(1)} collective-permute-done((bf16[128,2048]{1,0:T(8,128)(2,1)S(1)}, bf16[128,2048]{1,0:T(8,128)(2,1)S(1)}, u32[]{:S(2)}, u32[]{:S(2)}) %collective-permute-start.64) | collective-permute-done | bytes 524320 | tf_op jit(solution)/shard_map/ppermute | solution.py:38
  723.2 5.2 collective-permute-done.68
  728.6 4.9 shard_map.715
  734.5 5.4 shard_map.714
  749.1 7.5 shard_map.716
  764.4 5.4 collective-permute-done.70
  781.1 7.6 shard_map.718
  (551 shorter events, 276.7 us)
Async XLA Ops:
  7.2 105.6 %all-gather.4.cloned.1.call-start = ((), (), s32[]{:S(2)}) async-start(), calls=%async_computation.4 | async-start | bytes 5242880 | tf_op jit(solution)/shard_map/all_gather | solution.py:792
  15.4 13.8 %collective-permute-start = (bf16[256,1024]{1,0:T(8,128)(2,1)}, bf16[256,1024]{1,0:T(8,128)(2,1)}, u32[]{:S(2)}, u32[]{:S(2)}) collective-permute-start(bf16[256,1024]{1,0:T(8,128)(2,1)} %shard_map.699), channel_id=1, source_target_pairs={{0,4},{4,0},{1,5},{5,1},{2,6},{6,2},{3,7},{7,3},{8,12},{12,8},{9,1... | collective-permute-start | bytes 1572872 | tf_op jit(solution)/shard_map/ppermute | solution.py:38
  15.4 13.7 %collective-permute-start.4 = (s32[1024]{0:T(1024)}, s32[1024]{0:T(1024)S(1)}, u32[]{:S(2)}, u32[]{:S(2)}) collective-permute-start(s32[1024]{0:T(1024)} %bitcast.142), channel_id=1, source_target_pairs={{0,4},{4,0},{1,5},{5,1},{2,6},{6,2},{3,7},{7,3},{8,12},{12,8},{9,1... | collective-permute-start | bytes 12296 | tf_op jit(solution)/shard_map/ppermute | solution.py:38
  31.7 231.6 %all-gather.6.cloned.1.call-start = ((), (), s32[]{:S(2)}) async-start(), calls=%async_computation.5 | async-start | bytes 10485760 | tf_op jit(solution)/shard_map/all_gather | solution.py:792
  31.7 23.9 %collective-permute-start.5 = (bf16[256,2048]{1,0:T(8,128)(2,1)S(1)}, bf16[256,2048]{1,0:T(8,128)(2,1)}, u32[]{:S(2)}, u32[]{:S(2)}) collective-permute-start(bf16[256,2048]{1,0:T(8,128)(2,1)S(1)} %dynamic-slice_bitcast_fusion), channel_id=1, source_target_pairs={{0,4},{4,0},{1,5},{5,1},{2,6},{6,2},{3,7},{7,3},{8,12},{12,8},{9,1... | collective-permute-start | bytes 3145736 | tf_op jit(solution)/shard_map/ppermute | solution.py:38
  55.6 23.1 %collective-permute-start.6 = (bf16[256,2048]{1,0:T(8,128)(2,1)}, bf16[256,2048]{1,0:T(8,128)(2,1)}, u32[]{:S(2)}, u32[]{:S(2)}) collective-permute-start(bf16[256,2048]{1,0:T(8,128)(2,1)} %collective-permute-done.5), channel_id=1, source_target_pairs={{0,2},{2,0},{1,3},{3,1},{4,6},{6,4},{5,7},{7,5},{8,10},{10,8},{9,1... | collective-permute-start | bytes 3145736 | tf_op jit(solution)/shard_map/ppermute | solution.py:38
  83.5 18.8 %collective-permute-start.8 = (bf16[512,2048]{1,0:T(8,128)(2,1)}, bf16[512,2048]{1,0:T(8,128)(2,1)}, u32[]{:S(2)}, u32[]{:S(2)}) collective-permute-start(bf16[512,2048]{1,0:T(8,128)(2,1)} %maximum_select_fusion.1), channel_id=1, source_target_pairs={{0,1},{1,0},{2,3},{3,2},{4,5},{5,4},{6,7},{7,6},{8,9},{9,8},{10,11... | collective-permute-start | bytes 6291464 | tf_op jit(solution)/shard_map/ppermute | solution.py:38
  84.6 14.5 %collective-permute-start.9 = (bf16[256,1024]{1,0:T(8,128)(2,1)}, bf16[256,1024]{1,0:T(8,128)(2,1)S(1)}, u32[]{:S(2)}, u32[]{:S(2)}) collective-permute-start(bf16[256,1024]{1,0:T(8,128)(2,1)} %get-tuple-element.363), channel_id=1, source_target_pairs={{0,4},{4,0},{1,5},{5,1},{2,6},{6,2},{3,7},{7,3},{8,12},{12,8},{9,1... | collective-permute-start | bytes 1572872 | tf_op jit(solution)/shard_map/ppermute | solution.py:38
  112.9 231.5 %all-gather.8.cloned.1.call-start = ((), (), s32[]{:S(2)}) async-start(), calls=%async_computation.6 | async-start | bytes 5242880 | tf_op jit(solution)/shard_map/all_gather | solution.py:792
  120.8 27.7 %collective-permute-start.13 = (bf16[256,1024]{1,0:T(8,128)(2,1)}, bf16[256,1024]{1,0:T(8,128)(2,1)}, u32[]{:S(2)}, u32[]{:S(2)}) collective-permute-start(bf16[256,1024]{1,0:T(8,128)(2,1)} %get-tuple-element.367), channel_id=1, source_target_pairs={{0,4},{4,0},{1,5},{5,1},{2,6},{6,2},{3,7},{7,3},{8,12},{12,8},{9,1... | collective-permute-start | bytes 1572872 | tf_op jit(solution)/shard_map/ppermute | solution.py:38
  183.4 14.0 %collective-permute-start.15 = (bf16[128,2048]{1,0:T(8,128)(2,1)S(1)}, bf16[128,2048]{1,0:T(8,128)(2,1)S(1)}, u32[]{:S(2)}, u32[]{:S(2)}) collective-permute-start(bf16[128,2048]{1,0:T(8,128)(2,1)S(1)} %get-tuple-element.359), channel_id=1, source_target_pairs={{0,4},{4,0},{1,5},{5,1},{2,6},{6,2},{3,7},{7,3},{8,12},{12,8},{9,1... | collective-permute-start | bytes 1572872 | tf_op jit(solution)/shard_map/ppermute | solution.py:38
  184.5 13.7 %collective-permute-start.17 = (bf16[128,2048]{1,0:T(8,128)(2,1)S(1)}, bf16[128,2048]{1,0:T(8,128)(2,1)S(1)}, u32[]{:S(2)}, u32[]{:S(2)}) collective-permute-start(bf16[128,2048]{1,0:T(8,128)(2,1)S(1)} %get-tuple-element.358), channel_id=1, source_target_pairs={{0,2},{2,0},{1,3},{3,1},{4,6},{6,4},{5,7},{7,5},{8,10},{10,8},{9,1... | collective-permute-start | bytes 1572872 | tf_op jit(solution)/shard_map/ppermute | solution.py:38
  198.4 24.2 %collective-permute-start.16 = (bf16[256,2048]{1,0:T(8,128)(2,1)S(1)}, bf16[256,2048]{1,0:T(8,128)(2,1)S(1)}, u32[]{:S(2)}, u32[]{:S(2)}) collective-permute-start(bf16[256,2048]{1,0:T(8,128)(2,1)S(1)} %pad_maximum_fusion.6), channel_id=1, source_target_pairs={{0,2},{2,0},{1,3},{3,1},{4,6},{6,4},{5,7},{7,5},{8,10},{10,8},{9,1... | collective-permute-start | bytes 3145736 | tf_op jit(solution)/shard_map/ppermute | solution.py:38
  200.1 24.0 %collective-permute-start.18 = (bf16[256,2048]{1,0:T(8,128)(2,1)S(1)}, bf16[256,2048]{1,0:T(8,128)(2,1)S(1)}, u32[]{:S(2)}, u32[]{:S(2)}) collective-permute-start(bf16[256,2048]{1,0:T(8,128)(2,1)S(1)} %pad_maximum_fusion.7), channel_id=1, source_target_pairs={{0,4},{4,0},{1,5},{5,1},{2,6},{6,2},{3,7},{7,3},{8,12},{12,8},{9,1... | collective-permute-start | bytes 3145736 | tf_op jit(solution)/shard_map/ppermute | solution.py:38
  263.2 359.8 %reduce-scatter.7.cloned.1.call-start = ((), (), s32[]{:S(2)}) async-start(), calls=%async_computation.8 | async-start | bytes 5242880 | tf_op jit(solution)/shard_map/reduce_scatter | solution.py:877
  263.5 25.2 %collective-permute-start.20 = (bf16[256,2048]{1,0:T(8,128)(2,1)S(1)}, bf16[256,2048]{1,0:T(8,128)(2,1)S(1)}, u32[]{:S(2)}, u32[]{:S(2)}) collective-permute-start(bf16[256,2048]{1,0:T(8,128)(2,1)S(1)} %fusion.20.refs_0_), channel_id=1, source_target_pairs={{0,4},{4,0},{1,5},{5,1},{2,6},{6,2},{3,7},{7,3},{8,12},{12,8},{9,1... | collective-permute-start | bytes 3145736 | tf_op jit(solution)/shard_map/ppermute | solution.py:38
  265.0 25.2 %collective-permute-start.19 = (bf16[256,2048]{1,0:T(8,128)(2,1)S(1)}, bf16[256,2048]{1,0:T(8,128)(2,1)S(1)}, u32[]{:S(2)}, u32[]{:S(2)}) collective-permute-start(bf16[256,2048]{1,0:T(8,128)(2,1)S(1)} %fusion.20.refs_0_), channel_id=1, source_target_pairs={{0,2},{2,0},{1,3},{3,1},{4,6},{6,4},{5,7},{7,5},{8,10},{10,8},{9,1... | collective-permute-start | bytes 3145736 | tf_op jit(solution)/shard_map/ppermute | solution.py:38
  266.5 57.9 %collective-permute-start.23 = (bf16[256,2048]{1,0:T(8,128)(2,1)S(1)}, bf16[256,2048]{1,0:T(8,128)(2,1)S(1)}, u32[]{:S(2)}, u32[]{:S(2)}) collective-permute-start(bf16[256,2048]{1,0:T(8,128)(2,1)S(1)} %fusion.20.refs_0_), channel_id=1, source_target_pairs={{0,1},{1,0},{2,3},{3,2},{4,5},{5,4},{6,7},{7,6},{8,9},{9,8},{10,11... | collective-permute-start | bytes 3145736 | tf_op jit(solution)/shard_map/ppermute | solution.py:38
  291.8 32.5 %collective-permute-start.24 = (bf16[256,2048]{1,0:T(8,128)(2,1)S(1)}, bf16[256,2048]{1,0:T(8,128)(2,1)}, u32[]{:S(2)}, u32[]{:S(2)}) collective-permute-start(bf16[256,2048]{1,0:T(8,128)(2,1)S(1)} %collective-permute-done.19.refs_1_), channel_id=1, source_target_pairs={{0,1},{1,0},{2,3},{3,2},{4,5},{5,4},{6,7},{7,6},{8,9},{9,8},{10,11... | collective-permute-start | bytes 3145736 | tf_op jit(solution)/shard_map/ppermute | solution.py:38
  291.8 32.5 %collective-permute-start.25 = (bf16[256,2048]{1,0:T(8,128)(2,1)S(1)}, bf16[256,2048]{1,0:T(8,128)(2,1)}, u32[]{:S(2)}, u32[]{:S(2)}) collective-permute-start(bf16[256,2048]{1,0:T(8,128)(2,1)S(1)} %collective-permute-done.20.refs_2_), channel_id=1, source_target_pairs={{0,1},{1,0},{2,3},{3,2},{4,5},{5,4},{6,7},{7,6},{8,9},{9,8},{10,11... | collective-permute-start | bytes 3145736 | tf_op jit(solution)/shard_map/ppermute | solution.py:38
  301.9 22.4 %collective-permute-start.26 = (bf16[128,2048]{1,0:T(8,128)(2,1)S(1)}, bf16[128,2048]{1,0:T(8,128)(2,1)S(1)}, u32[]{:S(2)}, u32[]{:S(2)}) collective-permute-start(bf16[128,2048]{1,0:T(8,128)(2,1)S(1)} %collective-permute-done.21.refs_3_), channel_id=1, source_target_pairs={{0,1},{1,0},{2,3},{3,2},{4,5},{5,4},{6,7},{7,6},{8,9},{9,8},{10,11... | collective-permute-start | bytes 1572872 | tf_op jit(solution)/shard_map/ppermute | solution.py:38
  303.2 21.1 %collective-permute-start.27 = (bf16[128,2048]{1,0:T(8,128)(2,1)S(1)}, bf16[128,2048]{1,0:T(8,128)(2,1)}, u32[]{:S(2)}, u32[]{:S(2)}) collective-permute-start(bf16[128,2048]{1,0:T(8,128)(2,1)S(1)} %collective-permute-done.22.refs_4_), channel_id=1, source_target_pairs={{0,1},{1,0},{2,3},{3,2},{4,5},{5,4},{6,7},{7,6},{8,9},{9,8},{10,11... | collective-permute-start | bytes 1572872 | tf_op jit(solution)/shard_map/ppermute | solution.py:38
  364.6 14.0 %collective-permute-start.29 = (bf16[128,2048]{1,0:T(8,128)(2,1)S(1)}, bf16[128,2048]{1,0:T(8,128)(2,1)S(1)}, u32[]{:S(2)}, u32[]{:S(2)}) collective-permute-start(bf16[128,2048]{1,0:T(8,128)(2,1)S(1)} %get-tuple-element.353), channel_id=1, source_target_pairs={{0,4},{4,0},{1,5},{5,1},{2,6},{6,2},{3,7},{7,3},{8,12},{12,8},{9,1... | collective-permute-start | bytes 1572872 | tf_op jit(solution)/shard_map/ppermute | solution.py:38
  380.1 24.1 %collective-permute-start.30 = (bf16[256,2048]{1,0:T(8,128)(2,1)S(1)}, bf16[256,2048]{1,0:T(8,128)(2,1)S(1)}, u32[]{:S(2)}, u32[]{:S(2)}) collective-permute-start(bf16[256,2048]{1,0:T(8,128)(2,1)S(1)} %pad_maximum_fusion.8), channel_id=1, source_target_pairs={{0,2},{2,0},{1,3},{3,1},{4,6},{6,4},{5,7},{7,5},{8,10},{10,8},{9,1... | collective-permute-start | bytes 3145736 | tf_op jit(solution)/shard_map/ppermute | solution.py:38
  381.7 23.8 %collective-permute-start.32 = (bf16[256,2048]{1,0:T(8,128)(2,1)S(1)}, bf16[256,2048]{1,0:T(8,128)(2,1)S(1)}, u32[]{:S(2)}, u32[]{:S(2)}) collective-permute-start(bf16[256,2048]{1,0:T(8,128)(2,1)S(1)} %pad_maximum_fusion.9), channel_id=1, source_target_pairs={{0,4},{4,0},{1,5},{5,1},{2,6},{6,2},{3,7},{7,3},{8,12},{12,8},{9,1... | collective-permute-start | bytes 3145736 | tf_op jit(solution)/shard_map/ppermute | solution.py:38
  410.0 22.9 %collective-permute-start.34 = (bf16[256,2048]{1,0:T(8,128)(2,1)S(1)}, bf16[256,2048]{1,0:T(8,128)(2,1)S(1)}, u32[]{:S(2)}, u32[]{:S(2)}) collective-permute-start(bf16[256,2048]{1,0:T(8,128)(2,1)S(1)} %get-tuple-element.334), channel_id=1, source_target_pairs={{0,4},{4,0},{1,5},{5,1},{2,6},{6,2},{3,7},{7,3},{8,12},{12,8},{9,1... | collective-permute-start | bytes 3145736 | tf_op jit(solution)/shard_map/ppermute | solution.py:38
  410.7 23.3 %collective-permute-start.33 = (bf16[256,2048]{1,0:T(8,128)(2,1)S(1)}, bf16[256,2048]{1,0:T(8,128)(2,1)S(1)}, u32[]{:S(2)}, u32[]{:S(2)}) collective-permute-start(bf16[256,2048]{1,0:T(8,128)(2,1)S(1)} %get-tuple-element.334), channel_id=1, source_target_pairs={{0,2},{2,0},{1,3},{3,1},{4,6},{6,4},{5,7},{7,5},{8,10},{10,8},{9,1... | collective-permute-start | bytes 3145736 | tf_op jit(solution)/shard_map/ppermute | solution.py:38
  411.3 25.5 %collective-permute-start.37 = (bf16[256,2048]{1,0:T(8,128)(2,1)S(1)}, bf16[256,2048]{1,0:T(8,128)(2,1)S(1)}, u32[]{:S(2)}, u32[]{:S(2)}) collective-permute-start(bf16[256,2048]{1,0:T(8,128)(2,1)S(1)} %get-tuple-element.334), channel_id=1, source_target_pairs={{0,1},{1,0},{2,3},{3,2},{4,5},{5,4},{6,7},{7,6},{8,9},{9,8},{10,11... | collective-permute-start | bytes 3145736 | tf_op jit(solution)/shard_map/ppermute | solution.py:38
  461.4 161.6 %reduce-scatter.5.cloned.1.call-start = ((), (), s32[]{:S(2)}) async-start(), calls=%async_computation.7 | async-start | bytes 5242880 | tf_op jit(solution)/shard_map/reduce_scatter | solution.py:877
  461.6 25.2 %collective-permute-start.42 = (bf16[256,2048]{1,0:T(8,128)(2,1)S(1)}, bf16[256,2048]{1,0:T(8,128)(2,1)}, u32[]{:S(2)}, u32[]{:S(2)}) collective-permute-start(bf16[256,2048]{1,0:T(8,128)(2,1)S(1)} %get-tuple-element.209), channel_id=1, source_target_pairs={{0,2},{2,0},{1,3},{3,1},{4,6},{6,4},{5,7},{7,5},{8,10},{10,8},{9,1... | collective-permute-start | bytes 3145736 | tf_op jit(solution)/shard_map/ppermute | solution.py:38
  530.8 171.5 %reduce-scatter.9.cloned.1.call-start = ((), (), s32[]{:S(2)}) async-start(), calls=%async_computation.9 | async-start | bytes 5242880 | tf_op jit(solution)/shard_map/reduce_scatter | solution.py:877
  532.9 14.1 %collective-permute-start.44 = (bf16[128,2048]{1,0:T(8,128)(2,1)S(1)}, bf16[128,2048]{1,0:T(8,128)(2,1)S(1)}, u32[]{:S(2)}, u32[]{:S(2)}) collective-permute-start(bf16[128,2048]{1,0:T(8,128)(2,1)S(1)} %get-tuple-element.347), channel_id=1, source_target_pairs={{0,4},{4,0},{1,5},{5,1},{2,6},{6,2},{3,7},{7,3},{8,12},{12,8},{9,1... | collective-permute-start | bytes 1572872 | tf_op jit(solution)/shard_map/ppermute | solution.py:38
  534.4 13.8 %collective-permute-start.46 = (bf16[128,2048]{1,0:T(8,128)(2,1)S(1)}, bf16[128,2048]{1,0:T(8,128)(2,1)S(1)}, u32[]{:S(2)}, u32[]{:S(2)}) collective-permute-start(bf16[128,2048]{1,0:T(8,128)(2,1)S(1)} %get-tuple-element.346), channel_id=1, source_target_pairs={{0,2},{2,0},{1,3},{3,1},{4,6},{6,4},{5,7},{7,5},{8,10},{10,8},{9,1... | collective-permute-start | bytes 1572872 | tf_op jit(solution)/shard_map/ppermute | solution.py:38
  550.6 24.5 %collective-permute-start.45 = (bf16[256,2048]{1,0:T(8,128)(2,1)}, bf16[256,2048]{1,0:T(8,128)(2,1)S(1)}, u32[]{:S(2)}, u32[]{:S(2)}) collective-permute-start(bf16[256,2048]{1,0:T(8,128)(2,1)} %pad_maximum_fusion.10), channel_id=1, source_target_pairs={{0,2},{2,0},{1,3},{3,1},{4,6},{6,4},{5,7},{7,5},{8,10},{10,8},{9,1... | collective-permute-start | bytes 3145736 | tf_op jit(solution)/shard_map/ppermute | solution.py:38
  552.6 24.1 %collective-permute-start.47 = (bf16[256,2048]{1,0:T(8,128)(2,1)}, bf16[256,2048]{1,0:T(8,128)(2,1)}, u32[]{:S(2)}, u32[]{:S(2)}) collective-permute-start(bf16[256,2048]{1,0:T(8,128)(2,1)} %pad_maximum_fusion.11), channel_id=1, source_target_pairs={{0,4},{4,0},{1,5},{5,1},{2,6},{6,2},{3,7},{7,3},{8,12},{12,8},{9,1... | collective-permute-start | bytes 3145736 | tf_op jit(solution)/shard_map/ppermute | solution.py:38
  581.5 23.0 %collective-permute-start.49 = (bf16[256,2048]{1,0:T(8,128)(2,1)S(1)}, bf16[256,2048]{1,0:T(8,128)(2,1)}, u32[]{:S(2)}, u32[]{:S(2)}) collective-permute-start(bf16[256,2048]{1,0:T(8,128)(2,1)S(1)} %multiply_convert_fusion), channel_id=1, source_target_pairs={{0,4},{4,0},{1,5},{5,1},{2,6},{6,2},{3,7},{7,3},{8,12},{12,8},{9,1... | collective-permute-start | bytes 3145736 | tf_op jit(solution)/shard_map/ppermute | solution.py:38
  582.8 24.3 %collective-permute-start.48 = (bf16[256,2048]{1,0:T(8,128)(2,1)S(1)}, bf16[256,2048]{1,0:T(8,128)(2,1)}, u32[]{:S(2)}, u32[]{:S(2)}) collective-permute-start(bf16[256,2048]{1,0:T(8,128)(2,1)S(1)} %multiply_convert_fusion), channel_id=1, source_target_pairs={{0,2},{2,0},{1,3},{3,1},{4,6},{6,4},{5,7},{7,5},{8,10},{10,8},{9,1... | collective-permute-start | bytes 3145736 | tf_op jit(solution)/shard_map/ppermute | solution.py:38
  583.3 25.5 %collective-permute-start.52 = (bf16[256,2048]{1,0:T(8,128)(2,1)S(1)}, bf16[256,2048]{1,0:T(8,128)(2,1)}, u32[]{:S(2)}, u32[]{:S(2)}) collective-permute-start(bf16[256,2048]{1,0:T(8,128)(2,1)S(1)} %multiply_convert_fusion), channel_id=1, source_target_pairs={{0,1},{1,0},{2,3},{3,2},{4,5},{5,4},{6,7},{7,6},{8,9},{9,8},{10,11... | collective-permute-start | bytes 3145736 | tf_op jit(solution)/shard_map/ppermute | solution.py:38
  583.3 39.7 %collective-permute-start.57 = (bf16[512,2048]{1,0:T(8,128)(2,1)}, bf16[512,2048]{1,0:T(8,128)(2,1)}, u32[]{:S(2)}, u32[]{:S(2)}) collective-permute-start(bf16[512,2048]{1,0:T(8,128)(2,1)} %pad_maximum_fusion.2.mine), channel_id=1, source_target_pairs={{0,1},{1,0},{2,3},{3,2},{4,5},{5,4},{6,7},{7,6},{8,9},{9,8},{10,11... | collective-permute-start | bytes 6291464 | tf_op jit(solution)/shard_map/ppermute | solution.py:38
  583.8 191.5 %reduce-scatter.11.cloned.1.call-start = ((), (), s32[]{:S(2)}) async-start(), calls=%async_computation.10 | async-start | bytes 5242880 | tf_op jit(solution)/shard_map/reduce_scatter | solution.py:877
  624.2 27.0 %collective-permute-start.58 = (bf16[256,1024]{1,0:T(8,128)(2,1)S(1)}, bf16[256,1024]{1,0:T(8,128)(2,1)S(1)}, u32[]{:S(2)}, u32[]{:S(2)}) collective-permute-start(bf16[256,1024]{1,0:T(8,128)(2,1)S(1)} %dynamic-slice_bitcast_fusion.4), channel_id=1, source_target_pairs={{0,4},{4,0},{1,5},{5,1},{2,6},{6,2},{3,7},{7,3},{8,12},{12,8},{9,1... | collective-permute-start | bytes 1572872 | tf_op jit(solution)/shard_map/ppermute | solution.py:38
  625.9 25.3 %collective-permute-start.59 = (bf16[256,1024]{1,0:T(8,128)(2,1)S(1)}, bf16[256,1024]{1,0:T(8,128)(2,1)S(1)}, u32[]{:S(2)}, u32[]{:S(2)}) collective-permute-start(bf16[256,1024]{1,0:T(8,128)(2,1)S(1)} %dynamic-slice_bitcast_fusion.3), channel_id=1, source_target_pairs={{0,4},{4,0},{1,5},{5,1},{2,6},{6,2},{3,7},{7,3},{8,12},{12,8},{9,1... | collective-permute-start | bytes 1572872 | tf_op jit(solution)/shard_map/ppermute | solution.py:38
  704.7 14.5 %collective-permute-start.64 = (bf16[128,2048]{1,0:T(8,128)(2,1)S(1)}, bf16[128,2048]{1,0:T(8,128)(2,1)S(1)}, u32[]{:S(2)}, u32[]{:S(2)}) collective-permute-start(bf16[128,2048]{1,0:T(8,128)(2,1)S(1)} %get-tuple-element.341), channel_id=1, source_target_pairs={{0,4},{4,0},{1,5},{5,1},{2,6},{6,2},{3,7},{7,3},{8,12},{12,8},{9,1... | collective-permute-start | bytes 1572872 | tf_op jit(solution)/shard_map/ppermute | solution.py:38
  705.1 14.2 %collective-permute-start.66 = (bf16[128,2048]{1,0:T(8,128)(2,1)S(1)}, bf16[128,2048]{1,0:T(8,128)(2,1)S(1)}, u32[]{:S(2)}, u32[]{:S(2)}) collective-permute-start(bf16[128,2048]{1,0:T(8,128)(2,1)S(1)} %get-tuple-element.340), channel_id=1, source_target_pairs={{0,2},{2,0},{1,3},{3,1},{4,6},{6,4},{5,7},{7,5},{8,10},{10,8},{9,1... | collective-permute-start | bytes 1572872 | tf_op jit(solution)/shard_map/ppermute | solution.py:38
  719.6 25.0 %collective-permute-start.65 = (bf16[256,2048]{1,0:T(8,128)(2,1)S(1)}, bf16[256,2048]{1,0:T(8,128)(2,1)S(1)}, u32[]{:S(2)}, u32[]{:S(2)}) collective-permute-start(bf16[256,2048]{1,0:T(8,128)(2,1)S(1)} %pad_maximum_fusion.13), channel_id=1, source_target_pairs={{0,2},{2,0},{1,3},{3,1},{4,6},{6,4},{5,7},{7,5},{8,10},{10,8},{9,1... | collective-permute-start | bytes 3145736 | tf_op jit(solution)/shard_map/ppermute | solution.py:38
  721.0 24.3 %collective-permute-start.67 = (bf16[256,2048]{1,0:T(8,128)(2,1)S(1)}, bf16[256,2048]{1,0:T(8,128)(2,1)S(1)}, u32[]{:S(2)}, u32[]{:S(2)}) collective-permute-start(bf16[256,2048]{1,0:T(8,128)(2,1)S(1)} %pad_maximum_fusion.14), channel_id=1, source_target_pairs={{0,4},{4,0},{1,5},{5,1},{2,6},{6,2},{3,7},{7,3},{8,12},{12,8},{9,1... | collective-permute-start | bytes 3145736 | tf_op jit(solution)/shard_map/ppermute | solution.py:38
  746.3 23.5 %collective-permute-start.70 = (bf16[256,2048]{1,0:T(8,128)(2,1)S(1)}, bf16[256,2048]{1,0:T(8,128)(2,1)S(1)}, u32[]{:S(2)}, u32[]{:S(2)}) collective-permute-start(bf16[256,2048]{1,0:T(8,128)(2,1)S(1)} %add_convert_fusion.6), channel_id=1, source_target_pairs={{0,2},{2,0},{1,3},{3,1},{4,6},{6,4},{5,7},{7,5},{8,10},{10,8},{9,1... | collective-permute-start | bytes 3145736 | tf_op jit(solution)/shard_map/ppermute | solution.py:38
  779.1 14.1 %collective-permute-start.73 = (bf16[256,1024]{1,0:T(8,128)(2,1)S(1)}, bf16[256,1024]{1,0:T(8,128)(2,1)S(1)}, u32[]{:S(2)}, u32[]{:S(2)}) collective-permute-start(bf16[256,1024]{1,0:T(8,128)(2,1)S(1)} %dynamic-slice_bitcast_fusion.1), channel_id=1, source_target_pairs={{0,4},{4,0},{1,5},{5,1},{2,6},{6,2},{3,7},{7,3},{8,12},{12,8},{9,1... | collective-permute-start | bytes 1572872 | tf_op jit(solution)/shard_map/ppermute | solution.py:38
  (159 other events, 1484.2 us)
Sparse Core Ops, SparseCore 0:
  31.8 81.0 all-gather.3
  115.0 148.1 all-gather.5
  265.4 78.9 all-gather.7
  461.5 74.2 reduce-scatter.6
  538.1 77.2 reduce-scatter.4
  617.5 77.2 reduce-scatter.8
  697.2 78.0 reduce-scatter.10

commit v3 on v2

--- a/solution.py
+++ b/solution.py
@@ -79,8 +79,8 @@
         half = value.shape[0] // 2
         over_x = swap(value, TX)
         over_y = swap(value, axis)
-        near = swap(over_y[:half], TX)
-        far = swap(over_x[half:], axis)
+        over_x, over_y = tie(over_x, over_y)
+        near, far = tie(swap(over_y[:half], TX), swap(over_x[half:], axis))
         mine = [value, over_x, over_y, near, far]
     else:
         line = lax.all_gather(value, TX, axis=0, tiled=True)
@@ -90,6 +90,18 @@
 
 def joined(groups):
     return [jnp.concatenate(blocks, 0) for blocks in groups]
+
+
+def joined_halves(groups):
+    if len(groups[0]) != 5:
+        return joined(groups)
+    out = []
+    for first, second, third, near, far in groups:
+        half = near.shape[0]
+        upper = [block[:half] for block in (first, second, third)] + [near]
+        lower = [block[half:] for block in (first, second, third)] + [far]
+        out.append(jnp.concatenate(upper + lower, 0))
+    return out
 
 
 def across(mine, theirs):
@@ -116,6 +128,21 @@
         )
     line = both[: count * block] + swap(both[count * block :], axis)
     return lax.psum_scatter(line, TX, scatter_dimension=0, tiled=True).astype(f32)
+
+
+def collect_halves(both, axis, *later):
+    if lax.axis_size(TX) != 2:
+        return (collect(both, axis), *later)
+    h = both.shape[0] // 8
+    near, far, *later = tie(swap(both[3 * h : 4 * h], TX), swap(both[7 * h :], axis), *later)
+    over_x = jnp.concatenate([both[h : 2 * h], both[5 * h : 6 * h] + far], 0)
+    over_y = jnp.concatenate([both[2 * h : 3 * h] + near, both[6 * h : 7 * h]], 0)
+    total = (
+        jnp.concatenate([both[:h], both[4 * h : 5 * h]], 0).astype(f32)
+        + swap(over_x, TX).astype(f32)
+        + swap(over_y, axis).astype(f32)
+    )
+    return (total, *later)
 
 
 def block_places(axis):
@@ -492,8 +519,14 @@
 
     @pl.when(pl.program_id(0) == 0)
     def _():
+        if count == 5:
+            half = blocks[3].shape[0]
+            parts = [block.at[:half] for block in blocks[:3]] + [blocks[3]]
+            parts += [block.at[half:] for block in blocks[:3]] + [blocks[4]]
+        else:
+            parts = blocks
         at = 0
-        for block in blocks:
+        for block in parts:
             full[at : at + block.shape[0], :] = block[...]
             at += block.shape[0]
 
@@ -524,6 +557,34 @@
         compiler_params=params(1),
         cost_estimate=lasting(10),
     )(*blocks, w_both, w_both)
+
+
+def joined_dot_body(*refs):
+    blocks, (weight, full, out) = refs[:-3], refs[-3:]
+    at = 0
+    for block in blocks:
+        rows = pl.ds(at, block.shape[0])
+        full[rows, :] = block[...]
+        out[rows, :] = dot(block[...], weight[...], 1, 0).astype(b16)
+        at += block.shape[0]
+
+
+def joined_dot(blocks, weight):
+    rows = sum(block.shape[0] for block in blocks)
+    width, columns = weight.shape
+    whole = lambda shape: pl.BlockSpec(shape, lambda i: (0, 0))
+    return pl.pallas_call(
+        joined_dot_body,
+        grid=(1,),
+        in_specs=[whole(block.shape) for block in blocks] + [whole(weight.shape)],
+        out_specs=[whole((rows, width)), whole((rows, columns))],
+        out_shape=[
+            jax.ShapeDtypeStruct((rows, width), b16),
+            jax.ShapeDtypeStruct((rows, columns), b16),
+        ],
+        compiler_params=params(1),
+        cost_estimate=lasting(4),
+    )(*blocks, weight)
 
 
 def ffn_backward_body(grad, w_down, gate, up, d_gate, d_up):
@@ -614,39 +675,6 @@
     )(side, query, key, val, out_weight)
 
 
-def paired_columns_body(side, query, key, val, out_weight, other, out):
-    @pl.when(pl.program_id(0) == side[0])
-    def _():
-        columns_body(side, query, key, val, out_weight, out)
-
-    @pl.when(pl.program_id(0) != side[0])
-    def _():
-        out[...] = other[...]
-
-
-def paired_columns(side, query, key, val, out_weight, other):
-    piece, width = query.shape[0], query.shape[1] // 2
-    upper = pl.BlockSpec((piece, width), lambda i, side: (0, side[0]))
-    return pl.pallas_call(
-        paired_columns_body,
-        grid_spec=pltpu.PrefetchScalarGridSpec(
-            num_scalar_prefetch=1,
-            grid=(2,),
-            in_specs=[
-                upper,
-                upper,
-                upper,
-                pl.BlockSpec((width, piece), lambda i, side: (side[0], 0)),
-                pl.BlockSpec((piece, 4 * width), lambda i, side: (0, 0)),
-            ],
-            out_specs=pl.BlockSpec((piece, 4 * width), lambda i, side: (i, 0)),
-        ),
-        out_shape=jax.ShapeDtypeStruct((2 * piece, 4 * width), b16),
-        compiler_params=params(1, 60),
-        cost_estimate=lasting(2),
-    )(side, query, key, val, out_weight, other)
-
-
 def flip_body(value, out):
     out[...] = jnp.transpose(value[...])
 
@@ -675,35 +703,45 @@
     return (updated, new_first, new_second)
 
 
-def assemble_body(flags, mine, theirs, out):
-    own = (pl.program_id(0) // flags[1]) == flags[0]
-    out[0] = jnp.where(own, mine[...], theirs[...]).astype(f32)
-
-
-def assemble(mine, theirs, block):
-    count = lax.axis_size(TX)
-    width = mine.shape[1]
+def assemble_body(count, flags, *refs):
+    out = refs[-1]
+    spot = pl.program_id(0)
+    theirs = ((spot // count) != flags[0]).astype(i32)
+    place = theirs * count + ((spot % count) ^ flags[1])
+    for at, block in enumerate(refs[:-1]):
+
+        @pl.when(place == at)
+        def _(block=block):
+            out[0] = block[...].astype(f32)
+
+
+def assemble(mine, theirs):
+    count = len(mine)
+    block, width = mine[0].shape
     shift = lax.axis_index(TX) if count == 2 else jnp.zeros((), i32)
-    flags = jnp.stack([lax.axis_index(TC), jnp.full((), count, i32), shift])
-    here = pl.BlockSpec((block, width), lambda i, flags: ((i % count) ^ flags[2], 0))
-    return pl.pallas_call(
-        assemble_body,
+    return pl.pallas_call(
+        functools.partial(assemble_body, count),
         grid_spec=pltpu.PrefetchScalarGridSpec(
             num_scalar_prefetch=1,
             grid=(2 * count,),
-            in_specs=[here, here],
+            in_specs=[pl.BlockSpec((block, width), lambda i, flags: (0, 0))] * (2 * count),
             out_specs=pl.BlockSpec((1, block, width), lambda i, flags: (0, i, 0)),
         ),
         out_shape=jax.ShapeDtypeStruct((1, 2 * count * block, width), f32),
         compiler_params=params(1),
         cost_estimate=lasting(5),
-    )(flags, mine, theirs)
+    )(jnp.stack([lax.axis_index(TC), shift]), *mine, *theirs)
 
 
 def over_chips(value):
-    if lax.axis_size(TX) == 2:
-        return jnp.concatenate([value, swap(value, TX)], 0)
-    return lax.all_gather(value, TX, axis=0, tiled=True)
+    count = lax.axis_size(TX)
+    if count == 2:
+        return [value, swap(value, TX)]
+    return jnp.split(lax.all_gather(value, TX, axis=0, tiled=True), count)
+
+
+def over_core(blocks):
+    return [swap(block, TC) for block in blocks]
 
 
 def adam_body(turned, flag, weight, first, second, own, other, grad, updated, mean, square):
@@ -791,9 +829,11 @@
     def over_shard(value):
         return lax.all_gather(value, SHARD, axis=0, tiled=True)
 
+    attn_own = over_shard(attention_columns(y[None], *first[:4]))
     theirs = swap(attention_columns(1 - y[None], *first[:4]), CX)
     theirs, local_rows, gains, docs_all = tie(theirs, my_rows(inputs), gains, docs_all)
-    w_attn = over_shard(paired_columns(y[None], *first[:4], theirs))
+    theirs, attn_own = tie(theirs, attn_own)
+    attn_other = over_shard(theirs)
 
     remote, gate_w, up_w, down_w = tie(swap(local_rows, CX), *first[4:])
     remote = gather_axis(remote, TX)
@@ -801,8 +841,13 @@
     remote, gate_w = tie(remote, gate_w)
     remote = gather_axis(remote, TC)
     up_w = pair(*over_ctx([up_w], hidden), CX)
-    w_attn, remote, w_both = tie(w_attn, remote, jnp.concatenate([gate_w, up_w], axis=1))
+    attn_other, remote, w_both = tie(
+        attn_other, remote, jnp.concatenate([gate_w, up_w], axis=1)
+    )
     w_both = over_shard(w_both)
+    w_attn = pair(
+        *[value.reshape(ring, 1, piece, 4 * wide) for value in (attn_own, attn_other)], CX, 1
+    ).reshape(width, 4 * wide)
     w_qkv, w_out = w_attn[:, : 3 * wide], w_attn[:, 3 * wide :]
     down_w = pair(*over_ctx([flip(down_w.astype(b16))], hidden), CX)
 
@@ -857,18 +902,23 @@
 
     res, gate_pre, up_pre, activated = zip(*[ffn_forward(blocks, w_both) for blocks in res])
     *activated, w_down = tie(*activated, w_down)
-    ffn_out = collect(across(*[dot(a, w_down, 1, 1) for a in activated]), CX)
-    ffn_inv = lax.rsqrt(row_mean(ffn_out, ffn_out) + norm_eps)
-    ffn_unit = ffn_out * ffn_inv
+    parts = 2 if lax.axis_size(TX) == 2 else 1
     grad_out = my_rows(cotangent[0]).astype(f32)
-    scaled_out = grad_out * ffn_gain
-    d_ffn = joined(
-        spread(
-            (ffn_inv * (scaled_out - ffn_unit * row_mean(scaled_out, ffn_unit))).astype(b16), CX
+    d_ffn, block_rows, grad_ffn_gain = [], [], 0.0
+    for mine, theirs, rows_in, cot in zip(
+        *[jnp.split(value, parts) for value in (*activated, residual, grad_out)]
+    ):
+        ffn_out = collect(across(dot(mine, w_down, 1, 1), dot(theirs, w_down, 1, 1)), CX)
+        ffn_inv = lax.rsqrt(row_mean(ffn_out, ffn_out) + norm_eps)
+        ffn_unit = ffn_out * ffn_inv
+        scaled_out = cot * ffn_gain
+        d_ffn.append(
+            (ffn_inv * (scaled_out - ffn_unit * row_mean(scaled_out, ffn_unit))).astype(b16)
         )
-    )
-    grad_ffn_gain = jnp.sum(grad_out * ffn_unit, axis=0)
-    block_rows = (residual + ffn_unit * ffn_gain).astype(b16)
+        grad_ffn_gain = grad_ffn_gain + jnp.sum(cot * ffn_unit, axis=0)
+        block_rows.append((rows_in + ffn_unit * ffn_gain).astype(b16))
+    d_ffn = joined_halves(spread(jnp.concatenate(d_ffn, 0), CX))
+    block_rows = jnp.concatenate(block_rows, 0)
 
     def both(left, right):
         return (dot(left[0], right[0], 0, 0) + dot(left[1], right[1], 0, 0)).astype(b16)
@@ -888,35 +938,35 @@
     d_gate, d_up = zip(
         *[ffn_backward(d, w_down, g, u) for d, g, u in zip(d_ffn, gate_pre, up_pre)]
     )
-    block_rows, *turned = tie(block_rows, *d_gate, *d_up)
-    d_gate, d_up = turned[:2], turned[2:]
+    *block_rows, d_gate0, d_gate1, d_up0, d_up1 = tie(*block_rows, *d_gate, *d_up)
+    d_gate, d_up = [d_gate0, d_gate1], [d_up0, d_up1]
     theirs, *turned = tie(ffn_residual(d_gate[1], d_up[1], w_both), *d_gate)
     d_gate = turned
-    grad_gate = dot(res[0], d_gate[0], 0, 0)
+    grad_gate = dot(res[0], d_gate[0], 0, 0).astype(b16)
     theirs, grad_gate = tie(swap(theirs, TC), grad_gate)
     both_ffn = ffn_residual(d_gate[0], d_up[0], w_both, theirs)
     both_ffn, *turned = tie(both_ffn, *d_gate, *d_up)
     d_gate, d_up = turned[:2], turned[2:]
-    grad_gate = (grad_gate + dot(res[1], d_gate[1], 0, 0)).astype(b16)
+    grad_gate = (grad_gate.astype(f32) + dot(res[1], d_gate[1], 0, 0)).astype(b16)
     grad_gate = to_shard(grad_gate)
-    back_ffn = collect(both_ffn, CX)
-    block_theirs = swap(block_rows, TC)
+    back_ffn, *d_up = collect_halves(both_ffn, CX, *d_up)
+    block_theirs = over_core(block_rows)
     grad_upward = both(res, d_up)
     grad_res = grad_out + back_ffn
     scaled_res = grad_res * attn_gain
     d_branch = (
         branch_inv * (scaled_res - branch_unit * row_mean(scaled_res, branch_unit))
     ).astype(b16)
-    d_branch, grad_upward = tie(d_branch, grad_upward)
+    d_branch, grad_upward, grad_down = tie(d_branch, grad_upward, grad_down)
+    down_halves = to_owner(grad_down)
     grad_upward = to_shard(grad_upward)
     grad_attn_gain = jnp.sum(grad_res * branch_unit, axis=0)
     triple = lambda i: (masters[i], first_moments[i], second_moments[i])
 
-    *d_branch, grad_gate, grad_down, block_theirs = tie(
-        *joined(spread(d_branch, CX)), grad_gate, grad_down, block_theirs
-    )
-    down_halves, gate_halves = to_owner(grad_down), to_owner(grad_gate)
-    d_att = jnp.concatenate([dot(d, w_out, 1, 0).astype(b16) for d in d_branch], 0)
+    d_branch, d_att = zip(*[joined_dot(blocks, w_out) for blocks in spread(d_branch, CX)])
+    *d_branch, grad_gate = tie(*d_branch, grad_gate)
+    gate_halves = to_owner(grad_gate)
+    d_att = jnp.concatenate(d_att, 0)
     d_query, d_key, d_val = flash_backward(
         query, key, val, own_start, log_total, d_att, attended, spot, block, size
     )
@@ -937,26 +987,21 @@
 
     sides = d_qkv.reshape(2, rows, 3 * wide)
     grad_qkv = both((inputs, remote), (part(sides, y, 0), part(sides, 1 - y, 0)))
-    grad_attn = to_shard(jnp.concatenate([grad_qkv, grad_out_w], axis=1))
+    grad_attn, grad_upward = tie(
+        jnp.concatenate([grad_qkv, grad_out_w], axis=1), grad_upward
+    )
+    grad_attn = to_shard(grad_attn)
     both_attn = across(dot(moved[:group], w_qkv, 1, 1), dot(moved[group:], w_qkv, 1, 1))
-    both_attn, grad_upward = tie(both_attn, grad_upward)
     back_attn = collect(both_attn, CX)
     down_step = adam(*triple(6), *down_halves, y[None], turned=True)
     gate_step = adam(*triple(4), *gate_halves, y[None])
-    block_share = assemble(block_rows, block_theirs, block)
-    back_attn, small, grad_upward, *turned = tie(
-        back_attn, small, grad_upward, *down_step, *gate_step
+    block_share = assemble(block_rows, block_theirs)
+    back_attn, small, block_share, grad_upward, *turned = tie(
+        back_attn, small, block_share, grad_upward, *down_step, *gate_step
     )
     down_step, gate_step = turned[:4], turned[4:]
+    up_step = adam(*triple(5), *to_owner(grad_upward), y[None])
     input_rows = over_chips((grad_res + back_attn).astype(b16))
-    up_step = adam(*triple(5), *to_owner(grad_upward), y[None])
-    input_rows, grad_attn, block_share, *up_step = tie(
-        input_rows, grad_attn, block_share, *up_step
-    )
-    attn_halves = to_owner(grad_attn)
-    input_share = assemble(input_rows, swap(input_rows, TC), block)
-    input_share, *attn_halves = tie(input_share, *attn_halves)
-
     index = lax.axis_index(SHARD) * 2 + y
     wide_sums = lax.dynamic_slice_in_dim(
         small[0, : 2 * width].reshape(2, width), index * piece, piece, 1
@@ -965,10 +1010,16 @@
     head_sums = pair(head_sums, swap(head_sums, CX), CX, 1).reshape(2, heads_here, size)
     head_sums = lax.dynamic_slice_in_dim(head_sums, index * head_piece, head_piece, 2)
 
+    gain_steps = []
+    for i, grad in enumerate((head_sums[0], head_sums[1], wide_sums[0], wide_sums[1])):
+        gain_steps += (grad,) + adam_step(*triple(7 + i), grad)
+    _, *turned = tie(grad_attn[:1, :1], *gain_steps, *up_step, *input_rows)
+    gain_steps, up_step, input_rows = turned[:16], turned[16:20], turned[20:]
+    attn_halves = to_owner(grad_attn)
+    input_share = assemble(input_rows, over_core(input_rows))
     stepped = [adam(*triple(i), *attn_halves, y[None], i == 3, i) for i in range(4)]
     stepped += [gate_step, up_step, down_step]
-    for i, grad in enumerate((head_sums[0], head_sums[1], wide_sums[0], wide_sums[1])):
-        stepped.append((grad,) + adam_step(*triple(7 + i), grad))
+    stepped += [gain_steps[at : at + 4] for at in range(0, 16, 4)]
     return tuple(
         [block_share, input_share]
         + [result[which] for which in range(4) for result in stepped]

time: 814 us -> 805 us (0.989)
  waiting for transfers between devices: 354 us -> 337 us
  matrix products: 89.6 us -> 73.8 us
  starting transfers between devices: 64.8 us -> 75.4 us
    ppermute x75 -> x82, waiting for transfers between devices: 309 us -> 291 us  [swap(): return lax.ppermute(value, axis, [(0, 1), (1, 0)])]
    dot_general x18, matrix products: 89.6 us -> 73.8 us  [dot(): lax.dot_general(a, b, (((ca,), (cb,)), ((), ())), preferred_element_type=...]
    ppermute x75 -> x82, starting transfers between devices: 63.7 us -> 74.9 us  [swap(): return lax.ppermute(value, axis, [(0, 1), (1, 0)])]
    unnamed x271 -> x301, local copies, waits for them, and re-layouts: 51.6 us -> 60.9 us
    all_gather x3 -> x4, waiting for transfers between devices: 40.9 us -> 46.4 us  [over_shard(): return lax.all_gather(value, SHARD, axis=0, tiled=True)]
    select_n x9 -> x10, other arithmetic: 17.3 us -> 14.9 us  [pair(): jnp.where(lax.axis_index(axis) == 0, jnp.concatenate([mine, other], at),...]
    pallas_call x3 -> x4, Pallas kernels: 17.6 us -> 18.7 us  [the longest x2 11.4 us: assemble(): pl.pallas_call(functools.partial(assemble_body, count), grid_spec=pltpu.P...]
  transfers between devices with their start and end apart: 82 -> 90, of which waited for: 52 -> 57; matrix products, arithmetic and copies ran while one was open for 17% -> 16% of each run, Pallas kernels for 18% -> 19%
where the time goes in v3:
time: 805 us; the launch traced here: 796 us
  waiting for transfers between devices  337 us (42%)
  Pallas kernels  163 us (20%)
  local copies, waits for them, and re-layouts  76.3 us (9%)
  starting transfers between devices  75.4 us (9%)
  matrix products  73.8 us (9%)
  other arithmetic  54.2 us (7%)
  between operations  16.9 us (2%)
    ppermute x82, waiting for transfers between devices, swap(): return lax.ppermute(value, axis, [(0, 1), (1, 0)])  291 us
    ppermute x82, starting transfers between devices, swap(): return lax.ppermute(value, axis, [(0, 1), (1, 0)])  74.9 us
    dot_general x18, matrix products, dot(): lax.dot_general(a, b, (((ca,), (cb,)), ((), ())), preferred_element_type=...  73.8 us
    unnamed x301, local copies, waits for them, and re-layouts  60.9 us
    all_gather x4, waiting for transfers between devices, over_shard(): return lax.all_gather(value, SHARD, axis=0, tiled=True)  46.4 us
    pallas_call x7, Pallas kernels, adam(): pl.pallas_call(functools.partial(adam_body, turned), grid_spec=pltpu.Pref...  26 us
    pallas_call x2, Pallas kernels, ffn_forward(): pl.pallas_call(functools.partial(ffn_forward_body, len(blocks)), grid=(co...  25.1 us
    pallas_call x2, Pallas kernels, ffn_residual(): pl.pallas_call(ffn_residual_body, grid=(width // step,), in_specs=[full,...  23.3 us
  transfers between devices with their start and end apart: 90, of which 57 were waited for; matrix products, arithmetic and copies ran while one was open for 16% of the time, Pallas kernels for 19%

profile of v3, /device:TPU:0, one launch (start us, length us, event | category | flops | bytes accessed | tf_op | source)
XLA Modules:
  0.0 796.4 jit_solution(9060510044611204257)
XLA Ops:
  23.3 5.4 collective-permute-done.4
  29.2 23.4 %collective-permute-done.5 = bf16[256,2048]{1,0:T(8,128)(2,1)} collective-permute-done((bf16[256,2048]{1,0:T(8,128)(2,1)S(1)}, bf16[256,2048]{1,0:T(8,128)(2,1)}, u32[]{:S(2)}, u32[]{:S(2)}) %collective-permute-start.5) | collective-permute-done | bytes 1048608 | tf_op jit(solution)/shard_map/ppermute | solution.py:38
  59.1 7.2 collective-permute-done.7
  68.2 7.5 collective-permute-done.6
  81.3 13.5 %collective-permute-done.9 = bf16[256,1024]{1,0:T(8,128)(2,1)} collective-permute-done((bf16[256,1024]{1,0:T(8,128)(2,1)}, bf16[256,1024]{1,0:T(8,128)(2,1)}, u32[]{:S(2)}, u32[]{:S(2)}) %collective-permute-start.9) | collective-permute-done | bytes 524320 | tf_op jit(solution)/shard_map/ppermute | solution.py:38
  98.4 5.1 maximum_select_fusion.remote
  120.5 8.8 %shard_map.701 = (f32[2048,768]{1,0:T(8,128)S(1)}, f32[2,2048]{1,0:T(2,128)S(1)}) custom-call(s32[1]{0:T(128)} %bitcast.side.flag, bf16[1024,2048]{1,0:T(8,128)(2,1)S(1)} %bitcast.136, bf16[1024,2048]{1,0:T(8,128)(2,1)S(1)} %copy-done.11, bf16[2048,1024]{1,0:T(8,128)(2,1)S(1)} %bitcast.125), custom_call_target="tpu_custom_call" | custom-call | bytes 6000000 | tf_op jit(solution)/shard_map/pallas_call | solution.py:195
  146.3 14.8 %shard_map.704 = (bf16[2048,256]{1,0:T(8,128)(2,1)S(1)}, f32[2,2048]{1,0:T(2,128)S(1)}) custom-call(s32[8]{0:T(128)S(1)} %fusion.47.spot, s32[8]{0:T(128)S(1)} %and_select_fusion.low, bf16[2048,256]{1,0:T(8,128)(2,1)S(1)} %get-tuple-element.232.query, bf16[2048,256]{1,0:T(8,128)(2,1)S(1)} %get-tuple-element.233.keys, ...), custom_call_target="tpu_custom_call" | custom-call | bytes 9000000 | tf_op jit(solution)/shard_map/pallas_call | solution.py:309
  162.5 7.1 collective-permute-done.14
  174.1 11.1 %collective-permute-done.15 = bf16[128,2048]{1,0:T(8,128)(2,1)S(1)} collective-permute-done((bf16[128,2048]{1,0:T(8,128)(2,1)S(1)}, bf16[128,2048]{1,0:T(8,128)(2,1)S(1)}, u32[]{:S(2)}, u32[]{:S(2)}) %collective-permute-start.15) | collective-permute-done | bytes 524320 | tf_op jit(solution)/shard_map/ppermute | solution.py:38
  188.8 21.9 %collective-permute-done.18 = bf16[256,2048]{1,0:T(8,128)(2,1)S(1)} collective-permute-done((bf16[256,2048]{1,0:T(8,128)(2,1)S(1)}, bf16[256,2048]{1,0:T(8,128)(2,1)S(1)}, u32[]{:S(2)}, u32[]{:S(2)}) %collective-permute-start.18) | collective-permute-done | bytes 1048608 | tf_op jit(solution)/shard_map/ppermute | solution.py:38
  215.7 40.5 %all-gather.9.cloned.1.call-done.refs_5_.refs_6_.w_gate.w_up = bf16[2048,2048]{1,0:T(8,128)(2,1)} async-done(((bf16[512,2048]{1,0:T(8,128)(2,1)}), bf16[2048,2048]{1,0:T(8,128)(2,1)}) %all-gather.9.cloned.1.call-update) | async-done | bytes 8388624 | tf_op jit(solution)/shard_map/all_gather | solution.py:830
  259.2 22.2 %collective-permute-done.19.refs_1_ = bf16[256,2048]{1,0:T(8,128)(2,1)S(1)} collective-permute-done((bf16[256,2048]{1,0:T(8,128)(2,1)S(1)}, bf16[256,2048]{1,0:T(8,128)(2,1)S(1)}, u32[]{:S(2)}, u32[]{:S(2)}) %collective-permute-start.19) | collective-permute-done | bytes 1048608 | tf_op jit(solution)/shard_map/ppermute | solution.py:38
  285.3 10.2 %collective-permute-done.21.refs_3_ = bf16[128,2048]{1,0:T(8,128)(2,1)S(1)} collective-permute-done((bf16[128,2048]{1,0:T(8,128)(2,1)S(1)}, bf16[128,2048]{1,0:T(8,128)(2,1)S(1)}, u32[]{:S(2)}, u32[]{:S(2)}) %collective-permute-start.21) | collective-permute-done | bytes 524320 | tf_op jit(solution)/shard_map/ppermute | solution.py:38
  299.9 11.7 %shard_map.705 = (bf16[1024,2048]{1,0:T(8,128)(2,1)S(1)}, bf16[1024,1024]{1,0:T(8,128)(2,1)S(1)}, bf16[1024,1024]{1,0:T(8,128)(2,1)S(1)}, bf16[1024,1024]{1,0:T(8,128)(2,1)S(1)}) custom-call(bf16[256,2048]{1,0:T(8,128)(2,1)S(1)} %get-tuple-element.239.refs_0_, bf16[256,2048]{1,0:T(8,128)(2,1)S(1)} %collective-permute-done.19.refs_1_, ...), custom_call_target="tpu_custom_call" | custom-call | bytes 5000000 | tf_op jit(solution)/shard_map/pallas_call | solution.py:547
  317.6 13.3 %shard_map.706 = (bf16[1024,2048]{1,0:T(8,128)(2,1)S(1)}, bf16[1024,1024]{1,0:T(8,128)(2,1)S(1)}, bf16[1024,1024]{1,0:T(8,128)(2,1)S(1)}, bf16[1024,1024]{1,0:T(8,128)(2,1)S(1)}) custom-call(bf16[256,2048]{1,0:T(8,128)(2,1)S(1)} %collective-permute-done.23.refs_0_, bf16[256,2048]{1,0:T(8,128)(2,1)} %collective-permute-done.24.refs_1_, ...), custom_call_target="tpu_custom_call" | custom-call | bytes 5000000 | tf_op jit(solution)/shard_map/pallas_call | solution.py:547
  337.2 5.0 convolution_convert_fusion.4
  369.1 5.9 collective-permute-done.32
  376.9 8.5 %collective-permute-done.37 = bf16[128,2048]{1,0:T(8,128)(2,1)S(1)} collective-permute-done((bf16[128,2048]{1,0:T(8,128)(2,1)S(1)}, bf16[128,2048]{1,0:T(8,128)(2,1)S(1)}, u32[]{:S(2)}, u32[]{:S(2)}) %collective-permute-start.37) | collective-permute-done | bytes 524320 | tf_op jit(solution)/shard_map/ppermute | solution.py:38
  391.5 22.0 %collective-permute-done.38 = bf16[256,2048]{1,0:T(8,128)(2,1)S(1)} collective-permute-done((bf16[256,2048]{1,0:T(8,128)(2,1)S(1)}, bf16[256,2048]{1,0:T(8,128)(2,1)S(1)}, u32[]{:S(2)}, u32[]{:S(2)}) %collective-permute-start.38) | collective-permute-done | bytes 1048608 | tf_op jit(solution)/shard_map/ppermute | solution.py:38
  416.9 9.7 %collective-permute-done.40 = bf16[128,2048]{1,0:T(8,128)(2,1)S(1)} collective-permute-done((bf16[128,2048]{1,0:T(8,128)(2,1)S(1)}, bf16[128,2048]{1,0:T(8,128)(2,1)S(1)}, u32[]{:S(2)}, u32[]{:S(2)}) %collective-permute-start.40) | collective-permute-done | bytes 524320 | tf_op jit(solution)/shard_map/ppermute | solution.py:38
  429.6 4.7 fusion.75
  436.2 6.1 add_convert_fusion.3
  451.8 7.9 shard_map.707
  465.0 7.5 shard_map.708
  473.6 11.4 %shard_map.709 = bf16[1024,2048]{1,0:T(8,128)(2,1)S(1)} custom-call(bf16[1024,1024]{1,0:T(8,128)(2,1)S(1)} %get-tuple-element.297.d_gate, bf16[1024,1024]{1,0:T(8,128)(2,1)S(1)} %get-tuple-element.284.d_up, bf16[2048,2048]{1,0:T(8,128)(2,1)S(1)} %bitcast.122, bf16[2048,2048]{1,0:T(8,128)(2,1)S(1)} %bitcast.122), custom_call_target="tpu_custom_call" | custom-call | bytes 4500000 | tf_op jit(solution)/shard_map/pallas_call | solution.py:632
  485.1 6.1 convolution_convert_fusion.2
  492.2 11.9 %shard_map.710 = bf16[1024,2048]{1,0:T(8,128)(2,1)S(1)} custom-call(bf16[1024,1024]{1,0:T(8,128)(2,1)S(1)} %copy-done.45, bf16[1024,1024]{1,0:T(8,128)(2,1)S(1)} %get-tuple-element.282.d_up, bf16[2048,2048]{1,0:T(8,128)(2,1)S(1)} %bitcast.122, bf16[2048,2048]{1,0:T(8,128)(2,1)S(1)} %bitcast.122, bf16[1024,2048]{1,0:T(8,128)(2,1)S(1)} %collective-permute-done.48.rest_0_), custom_call_target="tpu_custom_call" | custom-call | bytes 4500000 | tf_op jit(solution)/shard_map/pallas_call | solution.py:632
  506.1 6.1 add_convert_fusion.1
  515.2 12.6 %collective-permute-done.49 = bf16[128,2048]{1,0:T(8,128)(2,1)S(1)} collective-permute-done((bf16[128,2048]{1,0:T(8,128)(2,1)S(1)}, bf16[128,2048]{1,0:T(8,128)(2,1)S(1)}, u32[]{:S(2)}, u32[]{:S(2)}) %collective-permute-start.49) | collective-permute-done | bytes 524320 | tf_op jit(solution)/shard_map/ppermute | solution.py:38
  536.0 4.6 fusion.76
  540.7 6.2 add_convert_fusion.2
  546.8 10.4 %collective-permute-done.52 = bf16[256,2048]{1,0:T(8,128)(2,1)} collective-permute-done((bf16[256,2048]{1,0:T(8,128)(2,1)}, bf16[256,2048]{1,0:T(8,128)(2,1)}, u32[]{:S(2)}, u32[]{:S(2)}) %collective-permute-start.52) | collective-permute-done | bytes 1048608 | tf_op jit(solution)/shard_map/ppermute | solution.py:38
  569.8 21.1 %collective-permute-done.53.refs_1_ = bf16[256,2048]{1,0:T(8,128)(2,1)} collective-permute-done((bf16[256,2048]{1,0:T(8,128)(2,1)}, bf16[256,2048]{1,0:T(8,128)(2,1)}, u32[]{:S(2)}, u32[]{:S(2)}) %collective-permute-start.53) | collective-permute-done | bytes 1048608 | tf_op jit(solution)/shard_map/ppermute | solution.py:38
  596.5 6.9 collective-permute-done.55.refs_3_
  625.7 15.5 %shard_map.713 = (f32[2048,256]{1,0:T(8,128)S(1)}, f32[2048,256]{1,0:T(8,128)S(1)}, f32[2048,256]{1,0:T(8,128)S(1)}) custom-call(s32[8]{0:T(128)S(1)} %copy-done.85, s32[8]{0:T(128)S(1)} %copy-done.87, bf16[2048,256]{1,0:T(8,128)(2,1)S(1)} %copy-done.33, bf16[2048,256]{1,0:T(8,128)(2,1)S(1)} %copy-done.35, bf16[2048,256]{1,0:T(8,128)(2,1)S(1)} %copy-done.37, ...), custom_call_target="tpu_custom_call" | custom-call | bytes 11000000 | tf_op jit(solution)/shard_map/pallas_call | solution.py:394
  663.4 5.0 convolution_convert_fusion.1
  669.1 6.0 fusion.8
  683.5 6.5 add_convert_fusion
  693.5 11.1 %collective-permute-done.68 = bf16[128,2048]{1,0:T(8,128)(2,1)S(1)} collective-permute-done((bf16[128,2048]{1,0:T(8,128)(2,1)S(1)}, bf16[128,2048]{1,0:T(8,128)(2,1)S(1)}, u32[]{:S(2)}, u32[]{:S(2)}) %collective-permute-start.68) | collective-permute-done | bytes 524320 | tf_op jit(solution)/shard_map/ppermute | solution.py:38
  714.8 4.9 collective-permute-start.73
  719.8 5.7 shard_map.716
  725.6 8.8 %shard_map.717 = (f32[2048,256]{1,0:T(8,128)}, f32[2048,256]{1,0:T(8,128)}, f32[2048,256]{1,0:T(8,128)}, f32[2048,256]{1,0:T(8,128)}) custom-call(s32[1]{0:T(128)} %bitcast.side.flag, f32[2048,256]{1,0:T(8,128)S(1)} %copy-done.15, f32[2048,256]{1,0:T(8,128)S(1)} %copy-done.50, f32[2048,256]{1,0:T(8,128)S(1)} %copy-done.51, ...), custom_call_target="tpu_custom_call" | custom-call | bytes 2097152 | tf_op jit(solution)/shard_map/pallas_call | solution.py:775
  734.4 4.5 shard_map.718
  748.1 7.5 collective-permute-done.77.other
  760.1 4.4 shard_map.719
  769.3 5.7 shard_map.720
  775.0 5.7 collective-permute-done.81.other
  (610 shorter events, 289.9 us)
Async XLA Ops:
  7.3 51.8 %all-gather.5.cloned.1.call-start = ((), (), s32[]{:S(2)}) async-start(), calls=%async_computation.4 | async-start | bytes 2621440 | tf_op jit(solution)/shard_map/all_gather | solution.py:830
  9.5 96.1 %all-gather.7.cloned.1.call-start = ((), (), s32[]{:S(2)}) async-start(), calls=%async_computation.5 | async-start | bytes 2621440 | tf_op jit(solution)/shard_map/all_gather | solution.py:830
  28.7 23.9 %collective-permute-start.5 = (bf16[256,2048]{1,0:T(8,128)(2,1)S(1)}, bf16[256,2048]{1,0:T(8,128)(2,1)}, u32[]{:S(2)}, u32[]{:S(2)}) collective-permute-start(bf16[256,2048]{1,0:T(8,128)(2,1)S(1)} %dynamic-slice_bitcast_fusion), channel_id=1, source_target_pairs={{0,4},{4,0},{1,5},{5,1},{2,6},{6,2},{3,7},{7,3},{8,12},{12,8},{9,1... | collective-permute-start | bytes 3145736 | tf_op jit(solution)/shard_map/ppermute | solution.py:38
  52.6 23.1 %collective-permute-start.6 = (bf16[256,2048]{1,0:T(8,128)(2,1)}, bf16[256,2048]{1,0:T(8,128)(2,1)}, u32[]{:S(2)}, u32[]{:S(2)}) collective-permute-start(bf16[256,2048]{1,0:T(8,128)(2,1)} %collective-permute-done.5), channel_id=1, source_target_pairs={{0,2},{2,0},{1,3},{3,1},{4,6},{6,4},{5,7},{7,5},{8,10},{10,8},{9,1... | collective-permute-start | bytes 3145736 | tf_op jit(solution)/shard_map/ppermute | solution.py:38
  59.1 197.1 %all-gather.9.cloned.1.call-start = ((), (), s32[]{:S(2)}) async-start(), calls=%async_computation.6 | async-start | bytes 10485760 | tf_op jit(solution)/shard_map/all_gather | solution.py:830
  79.0 19.5 %collective-permute-start.8 = (bf16[512,2048]{1,0:T(8,128)(2,1)S(1)}, bf16[512,2048]{1,0:T(8,128)(2,1)}, u32[]{:S(2)}, u32[]{:S(2)}) collective-permute-start(bf16[512,2048]{1,0:T(8,128)(2,1)S(1)} %maximum_select_fusion.2), channel_id=1, source_target_pairs={{0,1},{1,0},{2,3},{3,2},{4,5},{5,4},{6,7},{7,6},{8,9},{9,8},{10,11... | collective-permute-start | bytes 6291464 | tf_op jit(solution)/shard_map/ppermute | solution.py:38
  80.2 14.6 %collective-permute-start.9 = (bf16[256,1024]{1,0:T(8,128)(2,1)}, bf16[256,1024]{1,0:T(8,128)(2,1)}, u32[]{:S(2)}, u32[]{:S(2)}) collective-permute-start(bf16[256,1024]{1,0:T(8,128)(2,1)} %get-tuple-element.446), channel_id=1, source_target_pairs={{0,4},{4,0},{1,5},{5,1},{2,6},{6,2},{3,7},{7,3},{8,12},{12,8},{9,1... | collective-permute-start | bytes 1572872 | tf_op jit(solution)/shard_map/ppermute | solution.py:38
  105.6 231.5 %all-gather.11.cloned.1.call-start = ((), (), s32[]{:S(2)}) async-start(), calls=%async_computation.7 | async-start | bytes 5242880 | tf_op jit(solution)/shard_map/all_gather | solution.py:830
  112.5 26.0 %collective-permute-start.13 = (bf16[256,1024]{1,0:T(8,128)(2,1)S(1)}, bf16[256,1024]{1,0:T(8,128)(2,1)S(1)}, u32[]{:S(2)}, u32[]{:S(2)}) collective-permute-start(bf16[256,1024]{1,0:T(8,128)(2,1)S(1)} %get-tuple-element.454), channel_id=1, source_target_pairs={{0,4},{4,0},{1,5},{5,1},{2,6},{6,2},{3,7},{7,3},{8,12},{12,8},{9,1... | collective-permute-start | bytes 1572872 | tf_op jit(solution)/shard_map/ppermute | solution.py:38
  186.5 24.2 %collective-permute-start.18 = (bf16[256,2048]{1,0:T(8,128)(2,1)S(1)}, bf16[256,2048]{1,0:T(8,128)(2,1)S(1)}, u32[]{:S(2)}, u32[]{:S(2)}) collective-permute-start(bf16[256,2048]{1,0:T(8,128)(2,1)S(1)} %pad_maximum_fusion.5), channel_id=1, source_target_pairs={{0,4},{4,0},{1,5},{5,1},{2,6},{6,2},{3,7},{7,3},{8,12},{12,8},{9,1... | collective-permute-start | bytes 3145736 | tf_op jit(solution)/shard_map/ppermute | solution.py:38
  187.3 24.0 %collective-permute-start.16 = (bf16[256,2048]{1,0:T(8,128)(2,1)S(1)}, bf16[256,2048]{1,0:T(8,128)(2,1)S(1)}, u32[]{:S(2)}, u32[]{:S(2)}) collective-permute-start(bf16[256,2048]{1,0:T(8,128)(2,1)S(1)} %pad_maximum_fusion.4), channel_id=1, source_target_pairs={{0,2},{2,0},{1,3},{3,1},{4,6},{6,4},{5,7},{7,5},{8,10},{10,8},{9,1... | collective-permute-start | bytes 3145736 | tf_op jit(solution)/shard_map/ppermute | solution.py:38
  256.2 311.3 %reduce-scatter.5.cloned.1.call-start = ((), (), s32[]{:S(2)}) async-start(), calls=%async_computation.8 | async-start | bytes 5242880 | tf_op jit(solution)/shard_map/reduce_scatter | solution.py:927
  256.2 25.2 %collective-permute-start.19 = (bf16[256,2048]{1,0:T(8,128)(2,1)S(1)}, bf16[256,2048]{1,0:T(8,128)(2,1)S(1)}, u32[]{:S(2)}, u32[]{:S(2)}) collective-permute-start(bf16[256,2048]{1,0:T(8,128)(2,1)S(1)} %get-tuple-element.239.refs_0_), channel_id=1, source_target_pairs={{0,2},{2,0},{1,3},{3,1},{4,6},{6,4},{5,7},{7,5},{8,10},{10,8},{9,1... | collective-permute-start | bytes 3145736 | tf_op jit(solution)/shard_map/ppermute | solution.py:38
  257.7 24.8 %collective-permute-start.20 = (bf16[256,2048]{1,0:T(8,128)(2,1)S(1)}, bf16[256,2048]{1,0:T(8,128)(2,1)S(1)}, u32[]{:S(2)}, u32[]{:S(2)}) collective-permute-start(bf16[256,2048]{1,0:T(8,128)(2,1)S(1)} %get-tuple-element.239.refs_0_), channel_id=1, source_target_pairs={{0,4},{4,0},{1,5},{5,1},{2,6},{6,2},{3,7},{7,3},{8,12},{12,8},{9,1... | collective-permute-start | bytes 3145736 | tf_op jit(solution)/shard_map/ppermute | solution.py:38
  284.8 32.7 %collective-permute-start.23 = (bf16[256,2048]{1,0:T(8,128)(2,1)S(1)}, bf16[256,2048]{1,0:T(8,128)(2,1)S(1)}, u32[]{:S(2)}, u32[]{:S(2)}) collective-permute-start(bf16[256,2048]{1,0:T(8,128)(2,1)S(1)} %get-tuple-element.239.refs_0_), channel_id=1, source_target_pairs={{0,1},{1,0},{2,3},{3,2},{4,5},{5,4},{6,7},{7,6},{8,9},{9,8},{10,11... | collective-permute-start | bytes 3145736 | tf_op jit(solution)/shard_map/ppermute | solution.py:38
  284.8 32.7 %collective-permute-start.24 = (bf16[256,2048]{1,0:T(8,128)(2,1)S(1)}, bf16[256,2048]{1,0:T(8,128)(2,1)}, u32[]{:S(2)}, u32[]{:S(2)}) collective-permute-start(bf16[256,2048]{1,0:T(8,128)(2,1)S(1)} %collective-permute-done.19.refs_1_), channel_id=1, source_target_pairs={{0,1},{1,0},{2,3},{3,2},{4,5},{5,4},{6,7},{7,6},{8,9},{9,8},{10,11... | collective-permute-start | bytes 3145736 | tf_op jit(solution)/shard_map/ppermute | solution.py:38
  285.3 32.2 %collective-permute-start.25 = (bf16[256,2048]{1,0:T(8,128)(2,1)S(1)}, bf16[256,2048]{1,0:T(8,128)(2,1)}, u32[]{:S(2)}, u32[]{:S(2)}) collective-permute-start(bf16[256,2048]{1,0:T(8,128)(2,1)S(1)} %collective-permute-done.20.refs_2_), channel_id=1, source_target_pairs={{0,1},{1,0},{2,3},{3,2},{4,5},{5,4},{6,7},{7,6},{8,9},{9,8},{10,11... | collective-permute-start | bytes 3145736 | tf_op jit(solution)/shard_map/ppermute | solution.py:38
  296.0 21.6 %collective-permute-start.26 = (bf16[128,2048]{1,0:T(8,128)(2,1)S(1)}, bf16[128,2048]{1,0:T(8,128)(2,1)S(1)}, u32[]{:S(2)}, u32[]{:S(2)}) collective-permute-start(bf16[128,2048]{1,0:T(8,128)(2,1)S(1)} %collective-permute-done.21.refs_3_), channel_id=1, source_target_pairs={{0,1},{1,0},{2,3},{3,2},{4,5},{5,4},{6,7},{7,6},{8,9},{9,8},{10,11... | collective-permute-start | bytes 1572872 | tf_op jit(solution)/shard_map/ppermute | solution.py:38
  296.0 21.6 %collective-permute-start.27 = (bf16[128,2048]{1,0:T(8,128)(2,1)S(1)}, bf16[128,2048]{1,0:T(8,128)(2,1)}, u32[]{:S(2)}, u32[]{:S(2)}) collective-permute-start(bf16[128,2048]{1,0:T(8,128)(2,1)S(1)} %collective-permute-done.22.refs_4_), channel_id=1, source_target_pairs={{0,1},{1,0},{2,3},{3,2},{4,5},{5,4},{6,7},{7,6},{8,9},{9,8},{10,11... | collective-permute-start | bytes 1572872 | tf_op jit(solution)/shard_map/ppermute | solution.py:38
  359.8 15.2 %collective-permute-start.32 = (bf16[128,2048]{1,0:T(8,128)(2,1)S(1)}, bf16[128,2048]{1,0:T(8,128)(2,1)S(1)}, u32[]{:S(2)}, u32[]{:S(2)}) collective-permute-start(bf16[128,2048]{1,0:T(8,128)(2,1)S(1)} %pad_maximum_fusion.14), channel_id=1, source_target_pairs={{0,4},{4,0},{1,5},{5,1},{2,6},{6,2},{3,7},{7,3},{8,12},{12,8},{9,1... | collective-permute-start | bytes 1572872 | tf_op jit(solution)/shard_map/ppermute | solution.py:38
  359.9 16.6 %collective-permute-start.30 = (bf16[128,2048]{1,0:T(8,128)(2,1)S(1)}, bf16[128,2048]{1,0:T(8,128)(2,1)S(1)}, u32[]{:S(2)}, u32[]{:S(2)}) collective-permute-start(bf16[128,2048]{1,0:T(8,128)(2,1)S(1)} %pad_maximum_fusion.13), channel_id=1, source_target_pairs={{0,2},{2,0},{1,3},{3,1},{4,6},{6,4},{5,7},{7,5},{8,10},{10,8},{9,1... | collective-permute-start | bytes 1572872 | tf_op jit(solution)/shard_map/ppermute | solution.py:38
  365.4 20.0 %collective-permute-start.37 = (bf16[128,2048]{1,0:T(8,128)(2,1)S(1)}, bf16[128,2048]{1,0:T(8,128)(2,1)S(1)}, u32[]{:S(2)}, u32[]{:S(2)}) collective-permute-start(bf16[128,2048]{1,0:T(8,128)(2,1)S(1)} %pad_maximum_fusion.16), channel_id=1, source_target_pairs={{0,4},{4,0},{1,5},{5,1},{2,6},{6,2},{3,7},{7,3},{8,12},{12,8},{9,1... | collective-permute-start | bytes 1572872 | tf_op jit(solution)/shard_map/ppermute | solution.py:38
  366.0 20.6 %collective-permute-start.35 = (bf16[128,2048]{1,0:T(8,128)(2,1)S(1)}, bf16[128,2048]{1,0:T(8,128)(2,1)S(1)}, u32[]{:S(2)}, u32[]{:S(2)}) collective-permute-start(bf16[128,2048]{1,0:T(8,128)(2,1)S(1)} %pad_maximum_fusion.15), channel_id=1, source_target_pairs={{0,2},{2,0},{1,3},{3,1},{4,6},{6,4},{5,7},{7,5},{8,10},{10,8},{9,1... | collective-permute-start | bytes 1572872 | tf_op jit(solution)/shard_map/ppermute | solution.py:38
  389.4 24.1 %collective-permute-start.38 = (bf16[256,2048]{1,0:T(8,128)(2,1)S(1)}, bf16[256,2048]{1,0:T(8,128)(2,1)S(1)}, u32[]{:S(2)}, u32[]{:S(2)}) collective-permute-start(bf16[256,2048]{1,0:T(8,128)(2,1)S(1)} %pad_maximum_fusion.6), channel_id=1, source_target_pairs={{0,2},{2,0},{1,3},{3,1},{4,6},{6,4},{5,7},{7,5},{8,10},{10,8},{9,1... | collective-permute-start | bytes 3145736 | tf_op jit(solution)/shard_map/ppermute | solution.py:38
  390.9 23.8 %collective-permute-start.39 = (bf16[256,2048]{1,0:T(8,128)(2,1)S(1)}, bf16[256,2048]{1,0:T(8,128)(2,1)S(1)}, u32[]{:S(2)}, u32[]{:S(2)}) collective-permute-start(bf16[256,2048]{1,0:T(8,128)(2,1)S(1)} %pad_maximum_fusion.6), channel_id=1, source_target_pairs={{0,4},{4,0},{1,5},{5,1},{2,6},{6,2},{3,7},{7,3},{8,12},{12,8},{9,1... | collective-permute-start | bytes 3145736 | tf_op jit(solution)/shard_map/ppermute | solution.py:38
  391.5 25.4 %collective-permute-start.42 = (bf16[256,2048]{1,0:T(8,128)(2,1)S(1)}, bf16[256,2048]{1,0:T(8,128)(2,1)S(1)}, u32[]{:S(2)}, u32[]{:S(2)}) collective-permute-start(bf16[256,2048]{1,0:T(8,128)(2,1)S(1)} %pad_maximum_fusion.6), channel_id=1, source_target_pairs={{0,1},{1,0},{2,3},{3,2},{4,5},{5,4},{6,7},{7,6},{8,9},{9,8},{10,11... | collective-permute-start | bytes 3145736 | tf_op jit(solution)/shard_map/ppermute | solution.py:38
  442.3 179.8 %reduce-scatter.7.cloned.1.call-start = ((), (), s32[]{:S(2)}) async-start(), calls=%async_computation.9 | async-start | bytes 5242880 | tf_op jit(solution)/shard_map/reduce_scatter | solution.py:927
  442.4 30.2 %collective-permute-start.47 = (bf16[256,2048]{1,0:T(8,128)(2,1)S(1)}, bf16[256,2048]{1,0:T(8,128)(2,1)S(1)}, u32[]{:S(2)}, u32[]{:S(2)}) collective-permute-start(bf16[256,2048]{1,0:T(8,128)(2,1)S(1)} %pad_maximum_fusion.7.refs_0_), channel_id=1, source_target_pairs={{0,2},{2,0},{1,3},{3,1},{4,6},{6,4},{5,7},{7,5},{8,10},{10,8},{9,1... | collective-permute-start | bytes 3145736 | tf_op jit(solution)/shard_map/ppermute | solution.py:38
  512.2 169.4 %reduce-scatter.9.cloned.1.call-start = ((), (), s32[]{:S(2)}) async-start(), calls=%async_computation.10 | async-start | bytes 5242880 | tf_op jit(solution)/shard_map/reduce_scatter | solution.py:927
  513.7 14.0 %collective-permute-start.49 = (bf16[128,2048]{1,0:T(8,128)(2,1)S(1)}, bf16[128,2048]{1,0:T(8,128)(2,1)S(1)}, u32[]{:S(2)}, u32[]{:S(2)}) collective-permute-start(bf16[128,2048]{1,0:T(8,128)(2,1)S(1)} %get-tuple-element.424), channel_id=1, source_target_pairs={{0,2},{2,0},{1,3},{3,1},{4,6},{6,4},{5,7},{7,5},{8,10},{10,8},{9,1... | collective-permute-start | bytes 1572872 | tf_op jit(solution)/shard_map/ppermute | solution.py:38
  532.9 24.4 %collective-permute-start.52 = (bf16[256,2048]{1,0:T(8,128)(2,1)}, bf16[256,2048]{1,0:T(8,128)(2,1)}, u32[]{:S(2)}, u32[]{:S(2)}) collective-permute-start(bf16[256,2048]{1,0:T(8,128)(2,1)} %pad_maximum_fusion.9), channel_id=1, source_target_pairs={{0,4},{4,0},{1,5},{5,1},{2,6},{6,2},{3,7},{7,3},{8,12},{12,8},{9,1... | collective-permute-start | bytes 3145736 | tf_op jit(solution)/shard_map/ppermute | solution.py:38
  534.3 24.4 %collective-permute-start.51 = (bf16[256,2048]{1,0:T(8,128)(2,1)}, bf16[256,2048]{1,0:T(8,128)(2,1)}, u32[]{:S(2)}, u32[]{:S(2)}) collective-permute-start(bf16[256,2048]{1,0:T(8,128)(2,1)} %pad_maximum_fusion.8), channel_id=1, source_target_pairs={{0,2},{2,0},{1,3},{3,1},{4,6},{6,4},{5,7},{7,5},{8,10},{10,8},{9,1... | collective-permute-start | bytes 3145736 | tf_op jit(solution)/shard_map/ppermute | solution.py:38
  567.5 197.8 %reduce-scatter.11.cloned.1.call-start = ((), (), s32[]{:S(2)}) async-start(), calls=%async_computation.11 | async-start | bytes 5242880 | tf_op jit(solution)/shard_map/reduce_scatter | solution.py:927
  567.5 23.4 %collective-permute-start.53 = (bf16[256,2048]{1,0:T(8,128)(2,1)}, bf16[256,2048]{1,0:T(8,128)(2,1)}, u32[]{:S(2)}, u32[]{:S(2)}) collective-permute-start(bf16[256,2048]{1,0:T(8,128)(2,1)} %multiply_convert_fusion.refs_0_), channel_id=1, source_target_pairs={{0,2},{2,0},{1,3},{3,1},{4,6},{6,4},{5,7},{7,5},{8,10},{10,8},{9,1... | collective-permute-start | bytes 3145736 | tf_op jit(solution)/shard_map/ppermute | solution.py:38
  569.0 22.8 %collective-permute-start.54 = (bf16[256,2048]{1,0:T(8,128)(2,1)}, bf16[256,2048]{1,0:T(8,128)(2,1)}, u32[]{:S(2)}, u32[]{:S(2)}) collective-permute-start(bf16[256,2048]{1,0:T(8,128)(2,1)} %multiply_convert_fusion.refs_0_), channel_id=1, source_target_pairs={{0,4},{4,0},{1,5},{5,1},{2,6},{6,2},{3,7},{7,3},{8,12},{12,8},{9,1... | collective-permute-start | bytes 3145736 | tf_op jit(solution)/shard_map/ppermute | solution.py:38
  596.0 18.5 %collective-permute-start.57 = (bf16[256,2048]{1,0:T(8,128)(2,1)}, bf16[256,2048]{1,0:T(8,128)(2,1)}, u32[]{:S(2)}, u32[]{:S(2)}) collective-permute-start(bf16[256,2048]{1,0:T(8,128)(2,1)} %multiply_convert_fusion.refs_0_), channel_id=1, source_target_pairs={{0,1},{1,0},{2,3},{3,2},{4,5},{5,4},{6,7},{7,6},{8,9},{9,8},{10,11... | collective-permute-start | bytes 3145736 | tf_op jit(solution)/shard_map/ppermute | solution.py:38
  596.0 19.6 %collective-permute-start.58 = (bf16[256,2048]{1,0:T(8,128)(2,1)}, bf16[256,2048]{1,0:T(8,128)(2,1)}, u32[]{:S(2)}, u32[]{:S(2)}) collective-permute-start(bf16[256,2048]{1,0:T(8,128)(2,1)} %collective-permute-done.53.refs_1_), channel_id=1, source_target_pairs={{0,1},{1,0},{2,3},{3,2},{4,5},{5,4},{6,7},{7,6},{8,9},{9,8},{10,11... | collective-permute-start | bytes 3145736 | tf_op jit(solution)/shard_map/ppermute | solution.py:38
  596.5 19.1 %collective-permute-start.59 = (bf16[256,2048]{1,0:T(8,128)(2,1)}, bf16[256,2048]{1,0:T(8,128)(2,1)}, u32[]{:S(2)}, u32[]{:S(2)}) collective-permute-start(bf16[256,2048]{1,0:T(8,128)(2,1)} %collective-permute-done.54.refs_2_), channel_id=1, source_target_pairs={{0,1},{1,0},{2,3},{3,2},{4,5},{5,4},{6,7},{7,6},{8,9},{9,8},{10,11... | collective-permute-start | bytes 3145736 | tf_op jit(solution)/shard_map/ppermute | solution.py:38
  614.5 26.8 %collective-permute-start.62 = (bf16[256,1024]{1,0:T(8,128)(2,1)}, bf16[256,1024]{1,0:T(8,128)(2,1)}, u32[]{:S(2)}, u32[]{:S(2)}) collective-permute-start(bf16[256,1024]{1,0:T(8,128)(2,1)} %dynamic-slice_bitcast_fusion.4), channel_id=1, source_target_pairs={{0,4},{4,0},{1,5},{5,1},{2,6},{6,2},{3,7},{7,3},{8,12},{12,8},{9,1... | collective-permute-start | bytes 1572872 | tf_op jit(solution)/shard_map/ppermute | solution.py:38
  623.4 17.9 %collective-permute-start.63 = (bf16[256,1024]{1,0:T(8,128)(2,1)S(1)}, bf16[256,1024]{1,0:T(8,128)(2,1)S(1)}, u32[]{:S(2)}, u32[]{:S(2)}) collective-permute-start(bf16[256,1024]{1,0:T(8,128)(2,1)S(1)} %dynamic-slice_bitcast_fusion.3), channel_id=1, source_target_pairs={{0,4},{4,0},{1,5},{5,1},{2,6},{6,2},{3,7},{7,3},{8,12},{12,8},{9,1... | collective-permute-start | bytes 1572872 | tf_op jit(solution)/shard_map/ppermute | solution.py:38
  690.2 14.3 %collective-permute-start.68 = (bf16[128,2048]{1,0:T(8,128)(2,1)S(1)}, bf16[128,2048]{1,0:T(8,128)(2,1)S(1)}, u32[]{:S(2)}, u32[]{:S(2)}) collective-permute-start(bf16[128,2048]{1,0:T(8,128)(2,1)S(1)} %get-tuple-element.414), channel_id=1, source_target_pairs={{0,4},{4,0},{1,5},{5,1},{2,6},{6,2},{3,7},{7,3},{8,12},{12,8},{9,1... | collective-permute-start | bytes 1572872 | tf_op jit(solution)/shard_map/ppermute | solution.py:38
  691.3 14.1 %collective-permute-start.70 = (bf16[128,2048]{1,0:T(8,128)(2,1)S(1)}, bf16[128,2048]{1,0:T(8,128)(2,1)S(1)}, u32[]{:S(2)}, u32[]{:S(2)}) collective-permute-start(bf16[128,2048]{1,0:T(8,128)(2,1)S(1)} %get-tuple-element.413), channel_id=1, source_target_pairs={{0,2},{2,0},{1,3},{3,1},{4,6},{6,4},{5,7},{7,5},{8,10},{10,8},{9,1... | collective-permute-start | bytes 1572872 | tf_op jit(solution)/shard_map/ppermute | solution.py:38
  692.3 27.4 %collective-permute-start.74 = (bf16[256,2048]{1,0:T(8,128)(2,1)S(1)}, bf16[256,2048]{1,0:T(8,128)(2,1)S(1)}, u32[]{:S(2)}, u32[]{:S(2)}) collective-permute-start(bf16[256,2048]{1,0:T(8,128)(2,1)S(1)} %copy-done.31), channel_id=1, source_target_pairs={{0,1},{1,0},{2,3},{3,2},{4,5},{5,4},{6,7},{7,6},{8,9},{9,8},{10,11... | collective-permute-start | bytes 3145736 | tf_op jit(solution)/shard_map/ppermute | solution.py:38
  693.1 26.7 %collective-permute-start.75 = (bf16[256,2048]{1,0:T(8,128)(2,1)S(1)}, bf16[256,2048]{1,0:T(8,128)(2,1)}, u32[]{:S(2)}, u32[]{:S(2)}) collective-permute-start(bf16[256,2048]{1,0:T(8,128)(2,1)S(1)} %copy-done.65), channel_id=1, source_target_pairs={{0,1},{1,0},{2,3},{3,2},{4,5},{5,4},{6,7},{7,6},{8,9},{9,8},{10,11... | collective-permute-start | bytes 3145736 | tf_op jit(solution)/shard_map/ppermute | solution.py:38
  706.6 32.3 %collective-permute-start.71 = (bf16[256,2048]{1,0:T(8,128)(2,1)}, bf16[256,2048]{1,0:T(8,128)(2,1)}, u32[]{:S(2)}, u32[]{:S(2)}) collective-permute-start(bf16[256,2048]{1,0:T(8,128)(2,1)} %pad_maximum_fusion.12), channel_id=1, source_target_pairs={{0,4},{4,0},{1,5},{5,1},{2,6},{6,2},{3,7},{7,3},{8,12},{12,8},{9,1... | collective-permute-start | bytes 3145736 | tf_op jit(solution)/shard_map/ppermute | solution.py:38
  708.6 30.3 %collective-permute-start.69 = (bf16[256,2048]{1,0:T(8,128)(2,1)}, bf16[256,2048]{1,0:T(8,128)(2,1)}, u32[]{:S(2)}, u32[]{:S(2)}) collective-permute-start(bf16[256,2048]{1,0:T(8,128)(2,1)} %pad_maximum_fusion.11), channel_id=1, source_target_pairs={{0,2},{2,0},{1,3},{3,1},{4,6},{6,4},{5,7},{7,5},{8,10},{10,8},{9,1... | collective-permute-start | bytes 3145736 | tf_op jit(solution)/shard_map/ppermute | solution.py:38
  714.8 24.1 %collective-permute-start.73 = (f32[1,4608]{1,0:T(1,128)S(1)}, f32[1,4608]{1,0:T(1,128)S(1)}, u32[]{:S(2)}, u32[]{:S(2)}) collective-permute-start(f32[1,4608]{1,0:T(1,128)S(1)} %add.349), channel_id=1, source_target_pairs={{0,16},{16,0},{1,17},{17,1},{2,18},{18,2},{3,19},{19,3},{4,20},{20... | collective-permute-start | bytes 55304 | tf_op jit(solution)/shard_map/ppermute | solution.py:38
  742.0 22.8 %collective-permute-start.78 = (bf16[256,2048]{1,0:T(8,128)(2,1)S(1)}, bf16[256,2048]{1,0:T(8,128)(2,1)}, u32[]{:S(2)}, u32[]{:S(2)}) collective-permute-start(bf16[256,2048]{1,0:T(8,128)(2,1)S(1)} %add_convert_fusion.7.refs_0_), channel_id=1, source_target_pairs={{0,2},{2,0},{1,3},{3,1},{4,6},{6,4},{5,7},{7,5},{8,10},{10,8},{9,1... | collective-permute-start | bytes 3145736 | tf_op jit(solution)/shard_map/ppermute | solution.py:38
  (184 other events, 1568.5 us)
Sparse Core Ops, SparseCore 0:
  10.3 48.7 all-gather.4
  60.6 44.9 all-gather.6
  107.7 148.3 all-gather.8
  258.1 78.9 all-gather.10
  442.4 74.4 reduce-scatter.4
  519.1 77.2 reduce-scatter.6
  598.7 77.2 reduce-scatter.8
  681.8 79.5 reduce-scatter.10

commit v4 on v3

--- a/solution.py
+++ b/solution.py
@@ -131,18 +131,11 @@
 
 
 def collect_halves(both, axis, *later):
-    if lax.axis_size(TX) != 2:
-        return (collect(both, axis), *later)
     h = both.shape[0] // 8
     near, far, *later = tie(swap(both[3 * h : 4 * h], TX), swap(both[7 * h :], axis), *later)
     over_x = jnp.concatenate([both[h : 2 * h], both[5 * h : 6 * h] + far], 0)
     over_y = jnp.concatenate([both[2 * h : 3 * h] + near, both[6 * h : 7 * h]], 0)
-    total = (
-        jnp.concatenate([both[:h], both[4 * h : 5 * h]], 0).astype(f32)
-        + swap(over_x, TX).astype(f32)
-        + swap(over_y, axis).astype(f32)
-    )
-    return (total, *later)
+    return (both, swap(over_x, TX), swap(over_y, axis), *later)
 
 
 def block_places(axis):
@@ -559,6 +552,50 @@
     )(*blocks, w_both, w_both)
 
 
+def branch_back_body(
+    both, from_x, from_y, cot, unit, inverse, gain, grad_res, d_branch, grad_gain
+):
+    @pl.when(pl.program_id(0) == 0)
+    def _():
+        grad_gain[...] = jnp.zeros_like(grad_gain)
+
+    total = both[...].astype(f32) + from_x[...].astype(f32) + from_y[...].astype(f32)
+    total += cot[...].astype(f32)
+    grad_res[...] = total
+    grad_gain[...] += jnp.sum(total * unit[...], axis=0, keepdims=True)
+    scaled = total * gain[...]
+    mean = jnp.mean(scaled * unit[...], axis=1, keepdims=True)
+    d_branch[...] = (inverse[...] * (scaled - unit[...] * mean)).astype(b16)
+
+
+def branch_back(both, from_x, from_y, cot, unit, inverse, gain):
+    rows, width = unit.shape
+    half = rows // 2
+    by_row = pl.BlockSpec((half, width), lambda i: (i, 0))
+    line = pl.BlockSpec((1, width), lambda i: (0, 0))
+    return pl.pallas_call(
+        branch_back_body,
+        grid=(2,),
+        in_specs=[
+            pl.BlockSpec((half, width), lambda i: (4 * i, 0)),
+            by_row,
+            by_row,
+            by_row,
+            by_row,
+            pl.BlockSpec((half, 1), lambda i: (i, 0)),
+            line,
+        ],
+        out_specs=[by_row, by_row, line],
+        out_shape=[
+            jax.ShapeDtypeStruct((rows, width), f32),
+            jax.ShapeDtypeStruct((rows, width), b16),
+            jax.ShapeDtypeStruct((1, width), f32),
+        ],
+        compiler_params=params(1, 60),
+        cost_estimate=lasting(4),
+    )(both, from_x, from_y, cot, unit, inverse, gain)
+
+
 def joined_dot_body(*refs):
     blocks, (weight, full, out) = refs[:-3], refs[-3:]
     at = 0
@@ -784,6 +821,46 @@
         compiler_params=params(2),
         cost_estimate=lasting(weight.size * 8e-6),
     )(flag, weight, first, second, own, other)
+
+
+def attention_adam_body(flag, *refs):
+    states, (own, other), outs = refs[:12], refs[12:14], refs[14:]
+    mine = pl.program_id(0) == flag[0]
+    width = states[0].shape[1]
+    for which in range(4):
+        columns = slice(which * width, (which + 1) * width)
+        value = jnp.where(mine, own[:, columns].astype(f32), other[:, columns].astype(f32))
+        if which == 3:
+            value = jnp.transpose(value)
+        outs[4 * which][...] = value
+        stepped = adam_step(*[ref[...] for ref in states[3 * which : 3 * which + 3]], value)
+        for at in range(3):
+            outs[4 * which + 1 + at][...] = stepped[at]
+
+
+def attention_adam(states, own, other, flag):
+    piece, width = states[0][0].shape[0], states[0][0].shape[1] // 2
+    across_columns = pl.BlockSpec((piece, width), lambda j, flag: (0, j))
+    across_rows = pl.BlockSpec((width, piece), lambda j, flag: (j, 0))
+    specs = [across_columns] * 3 + [across_rows]
+    shapes = [jax.ShapeDtypeStruct(state[0].shape, f32) for state in states]
+    out = pl.pallas_call(
+        attention_adam_body,
+        grid_spec=pltpu.PrefetchScalarGridSpec(
+            num_scalar_prefetch=1,
+            grid=(2,),
+            in_specs=[spec for spec in specs for _ in range(3)]
+            + [
+                pl.BlockSpec((None, piece, 4 * width), lambda j, flag: (flag[0], 0, 0)),
+                pl.BlockSpec((piece, 4 * width), lambda j, flag: (0, 0)),
+            ],
+            out_specs=[spec for spec in specs for _ in range(4)],
+        ),
+        out_shape=[shape for shape in shapes for _ in range(4)],
+        compiler_params=params(1, 40),
+        cost_estimate=lasting(6),
+    )(flag, *[array for state in states for array in state], own, other)
+    return [out[at : at + 4] for at in range(0, 16, 4)]
 
 
 def row_mean(a, b):
@@ -949,18 +1026,25 @@
     d_gate, d_up = turned[:2], turned[2:]
     grad_gate = (grad_gate.astype(f32) + dot(res[1], d_gate[1], 0, 0)).astype(b16)
     grad_gate = to_shard(grad_gate)
-    back_ffn, *d_up = collect_halves(both_ffn, CX, *d_up)
+    if parts == 2:
+        *collected, d_up0, d_up1 = collect_halves(both_ffn, CX, *d_up)
+        d_up = [d_up0, d_up1]
+        grad_res, d_branch, grad_attn_gain = branch_back(
+            *collected, my_rows(cotangent[0]), branch_unit, branch_inv, attn_gain
+        )
+        grad_attn_gain = grad_attn_gain[0]
+    else:
+        grad_res = grad_out + collect(both_ffn, CX)
+        scaled_res = grad_res * attn_gain
+        d_branch = (
+            branch_inv * (scaled_res - branch_unit * row_mean(scaled_res, branch_unit))
+        ).astype(b16)
+        grad_attn_gain = jnp.sum(grad_res * branch_unit, axis=0)
     block_theirs = over_core(block_rows)
     grad_upward = both(res, d_up)
-    grad_res = grad_out + back_ffn
-    scaled_res = grad_res * attn_gain
-    d_branch = (
-        branch_inv * (scaled_res - branch_unit * row_mean(scaled_res, branch_unit))
-    ).astype(b16)
     d_branch, grad_upward, grad_down = tie(d_branch, grad_upward, grad_down)
     down_halves = to_owner(grad_down)
     grad_upward = to_shard(grad_upward)
-    grad_attn_gain = jnp.sum(grad_res * branch_unit, axis=0)
     triple = lambda i: (masters[i], first_moments[i], second_moments[i])
 
     d_branch, d_att = zip(*[joined_dot(blocks, w_out) for blocks in spread(d_branch, CX)])
@@ -1017,7 +1101,7 @@
     gain_steps, up_step, input_rows = turned[:16], turned[16:20], turned[20:]
     attn_halves = to_owner(grad_attn)
     input_share = assemble(input_rows, over_core(input_rows))
-    stepped = [adam(*triple(i), *attn_halves, y[None], i == 3, i) for i in range(4)]
+    stepped = attention_adam([triple(i) for i in range(4)], *attn_halves, y[None])
     stepped += [gate_step, up_step, down_step]
     stepped += [gain_steps[at : at + 4] for at in range(0, 16, 4)]
     return tuple(

time: 805 us -> 802 us (level)
    pallas_call x0 -> x2, Pallas kernels: none -> 9.74 us  [the longest x1 5.32 us: attention_adam(): pl.pallas_call(attention_adam_body, grid_spec=pltpu.PrefetchScalarGridSpe...]
    pallas_call x7 -> x3, Pallas kernels: 26 us -> 17.7 us  [adam(): pl.pallas_call(functools.partial(adam_body, turned), grid_spec=pltpu.Pref...]
    unnamed x301 -> x294, local copies, waits for them, and re-layouts: 60.9 us -> 66.3 us
  transfers between devices with their start and end apart: 90 -> 90, of which waited for: 57 -> 55; matrix products, arithmetic and copies ran while one was open for 16% -> 16% of each run, Pallas kernels for 19% -> 20%
where the time goes in v4:
time: 802 us; the launch traced here: 792 us
  waiting for transfers between devices  333 us (42%)
  Pallas kernels  164 us (20%)
  local copies, waits for them, and re-layouts  82.1 us (10%)
  matrix products  74.7 us (9%)
  starting transfers between devices  69.7 us (9%)
  other arithmetic  52 us (6%)
  between operations  16.8 us (2%)
    ppermute x82, waiting for transfers between devices, swap(): return lax.ppermute(value, axis, [(0, 1), (1, 0)])  290 us
    dot_general x18, matrix products, dot(): lax.dot_general(a, b, (((ca,), (cb,)), ((), ())), preferred_element_type=...  74.7 us
    ppermute x82, starting transfers between devices, swap(): return lax.ppermute(value, axis, [(0, 1), (1, 0)])  69.2 us
    unnamed x294, local copies, waits for them, and re-layouts  66.3 us
    all_gather x4, waiting for transfers between devices, over_shard(): return lax.all_gather(value, SHARD, axis=0, tiled=True)  42.1 us
    pallas_call x2, Pallas kernels, ffn_forward(): pl.pallas_call(functools.partial(ffn_forward_body, len(blocks)), grid=(co...  25.1 us
    pallas_call x2, Pallas kernels, ffn_residual(): pl.pallas_call(ffn_residual_body, grid=(width // step,), in_specs=[full,...  23.3 us
    pallas_call x3, Pallas kernels, adam(): pl.pallas_call(functools.partial(adam_body, turned), grid_spec=pltpu.Pref...  17.7 us
  transfers between devices with their start and end apart: 90, of which 55 were waited for; matrix products, arithmetic and copies ran while one was open for 16% of the time, Pallas kernels for 20%

profile of v4, /device:TPU:0, one launch (start us, length us, event | category | flops | bytes accessed | tf_op | source)
XLA Modules:
  0.0 792.4 jit_solution(14768259898620687765)
XLA Ops:
  26.1 5.4 collective-permute-done.4
  31.8 23.6 %collective-permute-done.5 = bf16[256,2048]{1,0:T(8,128)(2,1)} collective-permute-done((bf16[256,2048]{1,0:T(8,128)(2,1)S(1)}, bf16[256,2048]{1,0:T(8,128)(2,1)}, u32[]{:S(2)}, u32[]{:S(2)}) %collective-permute-start.5) | collective-permute-done | bytes 1048608 | tf_op jit(solution)/shard_map/ppermute | solution.py:38
  59.4 9.7 %collective-permute-done.7 = bf16[256,1024]{1,0:T(8,128)(2,1)S(1)} collective-permute-done((bf16[256,1024]{1,0:T(8,128)(2,1)S(1)}, bf16[256,1024]{1,0:T(8,128)(2,1)S(1)}, u32[]{:S(2)}, u32[]{:S(2)}) %collective-permute-start.7) | collective-permute-done | bytes 524320 | tf_op jit(solution)/shard_map/ppermute | solution.py:38
  71.9 6.6 collective-permute-done.6
  78.5 4.7 maximum_select_fusion.2
  85.3 13.6 %collective-permute-done.9 = bf16[256,1024]{1,0:T(8,128)(2,1)S(1)} collective-permute-done((bf16[256,1024]{1,0:T(8,128)(2,1)}, bf16[256,1024]{1,0:T(8,128)(2,1)S(1)}, u32[]{:S(2)}, u32[]{:S(2)}) %collective-permute-start.9) | collective-permute-done | bytes 524320 | tf_op jit(solution)/shard_map/ppermute | solution.py:38
  102.1 6.1 maximum_select_fusion.remote
  122.0 8.8 %shard_map.701 = (f32[2048,768]{1,0:T(8,128)S(1)}, f32[2,2048]{1,0:T(2,128)S(1)}) custom-call(s32[1]{0:T(128)} %bitcast.side.flag, bf16[1024,2048]{1,0:T(8,128)(2,1)S(1)} %bitcast.114, bf16[1024,2048]{1,0:T(8,128)(2,1)S(1)} %copy-done.11, bf16[2048,1024]{1,0:T(8,128)(2,1)S(1)} %bitcast.108), custom_call_target="tpu_custom_call" | custom-call | bytes 6000000 | tf_op jit(solution)/shard_map/pallas_call | solution.py:188
  147.8 14.8 %shard_map.704 = (bf16[2048,256]{1,0:T(8,128)(2,1)S(1)}, f32[2,2048]{1,0:T(2,128)S(1)}) custom-call(s32[8]{0:T(128)S(1)} %fusion.46.spot, s32[8]{0:T(128)S(1)} %and_select_fusion.low, bf16[2048,256]{1,0:T(8,128)(2,1)S(1)} %get-tuple-element.235.query, bf16[2048,256]{1,0:T(8,128)(2,1)S(1)} %get-tuple-element.236.keys, ...), custom_call_target="tpu_custom_call" | custom-call | bytes 9000000 | tf_op jit(solution)/shard_map/pallas_call | solution.py:302
  164.0 7.1 collective-permute-done.14
  174.2 12.4 %collective-permute-done.15 = bf16[128,2048]{1,0:T(8,128)(2,1)S(1)} collective-permute-done((bf16[128,2048]{1,0:T(8,128)(2,1)S(1)}, bf16[128,2048]{1,0:T(8,128)(2,1)S(1)}, u32[]{:S(2)}, u32[]{:S(2)}) %collective-permute-start.15) | collective-permute-done | bytes 524320 | tf_op jit(solution)/shard_map/ppermute | solution.py:38
  190.1 21.2 %collective-permute-done.18 = bf16[256,2048]{1,0:T(8,128)(2,1)S(1)} collective-permute-done((bf16[256,2048]{1,0:T(8,128)(2,1)S(1)}, bf16[256,2048]{1,0:T(8,128)(2,1)S(1)}, u32[]{:S(2)}, u32[]{:S(2)}) %collective-permute-start.18) | collective-permute-done | bytes 1048608 | tf_op jit(solution)/shard_map/ppermute | solution.py:38
  217.5 40.8 %all-gather.9.cloned.1.call-done.refs_5_.refs_6_.w_gate.w_up = bf16[2048,2048]{1,0:T(8,128)(2,1)} async-done(((bf16[512,2048]{1,0:T(8,128)(2,1)}), bf16[2048,2048]{1,0:T(8,128)(2,1)}) %all-gather.9.cloned.1.call-update) | async-done | bytes 8388624 | tf_op jit(solution)/shard_map/all_gather | solution.py:907
  261.4 22.2 %collective-permute-done.19.refs_1_ = bf16[256,2048]{1,0:T(8,128)(2,1)S(1)} collective-permute-done((bf16[256,2048]{1,0:T(8,128)(2,1)S(1)}, bf16[256,2048]{1,0:T(8,128)(2,1)S(1)}, u32[]{:S(2)}, u32[]{:S(2)}) %collective-permute-start.19) | collective-permute-done | bytes 1048608 | tf_op jit(solution)/shard_map/ppermute | solution.py:38
  287.5 10.2 %collective-permute-done.21.refs_3_ = bf16[128,2048]{1,0:T(8,128)(2,1)S(1)} collective-permute-done((bf16[128,2048]{1,0:T(8,128)(2,1)S(1)}, bf16[128,2048]{1,0:T(8,128)(2,1)S(1)}, u32[]{:S(2)}, u32[]{:S(2)}) %collective-permute-start.21) | collective-permute-done | bytes 524320 | tf_op jit(solution)/shard_map/ppermute | solution.py:38
  302.0 11.7 %shard_map.705 = (bf16[1024,2048]{1,0:T(8,128)(2,1)S(1)}, bf16[1024,1024]{1,0:T(8,128)(2,1)S(1)}, bf16[1024,1024]{1,0:T(8,128)(2,1)S(1)}, bf16[1024,1024]{1,0:T(8,128)(2,1)S(1)}) custom-call(bf16[256,2048]{1,0:T(8,128)(2,1)S(1)} %get-tuple-element.242.refs_0_, bf16[256,2048]{1,0:T(8,128)(2,1)S(1)} %collective-permute-done.19.refs_1_, ...), custom_call_target="tpu_custom_call" | custom-call | bytes 5000000 | tf_op jit(solution)/shard_map/pallas_call | solution.py:540
  319.7 13.3 %shard_map.706 = (bf16[1024,2048]{1,0:T(8,128)(2,1)S(1)}, bf16[1024,1024]{1,0:T(8,128)(2,1)S(1)}, bf16[1024,1024]{1,0:T(8,128)(2,1)S(1)}, bf16[1024,1024]{1,0:T(8,128)(2,1)S(1)}) custom-call(bf16[256,2048]{1,0:T(8,128)(2,1)S(1)} %collective-permute-done.23.refs_0_, bf16[256,2048]{1,0:T(8,128)(2,1)} %collective-permute-done.24.refs_1_, ...), custom_call_target="tpu_custom_call" | custom-call | bytes 5000000 | tf_op jit(solution)/shard_map/pallas_call | solution.py:540
  339.3 5.0 convolution_convert_fusion.4
  372.2 4.9 collective-permute-done.32
  379.0 8.5 %collective-permute-done.37 = bf16[128,2048]{1,0:T(8,128)(2,1)S(1)} collective-permute-done((bf16[128,2048]{1,0:T(8,128)(2,1)S(1)}, bf16[128,2048]{1,0:T(8,128)(2,1)S(1)}, u32[]{:S(2)}, u32[]{:S(2)}) %collective-permute-start.37) | collective-permute-done | bytes 524320 | tf_op jit(solution)/shard_map/ppermute | solution.py:38
  393.6 22.0 %collective-permute-done.38 = bf16[256,2048]{1,0:T(8,128)(2,1)S(1)} collective-permute-done((bf16[256,2048]{1,0:T(8,128)(2,1)S(1)}, bf16[256,2048]{1,0:T(8,128)(2,1)S(1)}, u32[]{:S(2)}, u32[]{:S(2)}) %collective-permute-start.38) | collective-permute-done | bytes 1048608 | tf_op jit(solution)/shard_map/ppermute | solution.py:38
  419.0 9.7 %collective-permute-done.40 = bf16[128,2048]{1,0:T(8,128)(2,1)S(1)} collective-permute-done((bf16[128,2048]{1,0:T(8,128)(2,1)S(1)}, bf16[128,2048]{1,0:T(8,128)(2,1)S(1)}, u32[]{:S(2)}, u32[]{:S(2)}) %collective-permute-start.40) | collective-permute-done | bytes 524320 | tf_op jit(solution)/shard_map/ppermute | solution.py:38
  431.7 4.7 fusion.75
  438.4 6.1 add_convert_fusion.3
  454.0 7.9 %shard_map.707 = (bf16[1024,1024]{1,0:T(8,128)(2,1)S(1)}, bf16[1024,1024]{1,0:T(8,128)(2,1)S(1)}) custom-call(bf16[1024,2048]{1,0:T(8,128)(2,1)S(1)} %copy-done.21, bf16[2048,1024]{1,0:T(8,128)(2,1)S(1)} %copy-done.9, bf16[1024,1024]{1,0:T(8,128)(2,1)S(1)} %copy-done.57, bf16[1024,1024]{1,0:T(8,128)(2,1)S(1)} %copy-done.59), custom_call_target="tpu_custom_call" | custom-call | bytes 3000000 | tf_op jit(solution)/shard_map/pallas_call | solution.py:640
  467.2 7.6 shard_map.708
  475.9 11.4 %shard_map.709 = bf16[1024,2048]{1,0:T(8,128)(2,1)S(1)} custom-call(bf16[1024,1024]{1,0:T(8,128)(2,1)S(1)} %get-tuple-element.301.d_gate, bf16[1024,1024]{1,0:T(8,128)(2,1)S(1)} %get-tuple-element.288.d_up, bf16[2048,2048]{1,0:T(8,128)(2,1)S(1)} %bitcast.105, bf16[2048,2048]{1,0:T(8,128)(2,1)S(1)} %bitcast.105), custom_call_target="tpu_custom_call" | custom-call | bytes 4500000 | tf_op jit(solution)/shard_map/pallas_call | solution.py:669
  487.3 6.1 convolution_convert_fusion.2
  494.5 12.0 %shard_map.710.both = bf16[1024,2048]{1,0:T(8,128)(2,1)S(1)} custom-call(bf16[1024,1024]{1,0:T(8,128)(2,1)S(1)} %copy-done.45, bf16[1024,1024]{1,0:T(8,128)(2,1)S(1)} %get-tuple-element.286.d_up, bf16[2048,2048]{1,0:T(8,128)(2,1)S(1)} %bitcast.105, bf16[2048,2048]{1,0:T(8,128)(2,1)S(1)} %bitcast.105, bf16[1024,2048]{1,0:T(8,128)(2,1)S(1)} %collective-permute-done.48.rest_0_), custom_call_target="tpu_custom_call" | custom-call | bytes 4500000 | tf_op jit(solution)/shard_map/pallas_call | solution.py:669
  508.4 6.1 add_convert_fusion.1
  519.8 11.4 %collective-permute-done.49 = bf16[128,2048]{1,0:T(8,128)(2,1)S(1)} collective-permute-done((bf16[128,2048]{1,0:T(8,128)(2,1)}, bf16[128,2048]{1,0:T(8,128)(2,1)S(1)}, u32[]{:S(2)}, u32[]{:S(2)}) %collective-permute-start.49) | collective-permute-done | bytes 524320 | tf_op jit(solution)/shard_map/ppermute | solution.py:38
  536.9 4.6 fusion.76
  541.6 6.2 add_convert_fusion.2
  547.7 10.3 %collective-permute-done.51.from_x = bf16[256,2048]{1,0:T(8,128)(2,1)} collective-permute-done((bf16[256,2048]{1,0:T(8,128)(2,1)S(1)}, bf16[256,2048]{1,0:T(8,128)(2,1)}, u32[]{:S(2)}, u32[]{:S(2)}) %collective-permute-start.51) | collective-permute-done | bytes 1048608 | tf_op jit(solution)/shard_map/ppermute | solution.py:38
  566.2 21.4 %collective-permute-done.53.refs_1_ = bf16[256,2048]{1,0:T(8,128)(2,1)} collective-permute-done((bf16[256,2048]{1,0:T(8,128)(2,1)}, bf16[256,2048]{1,0:T(8,128)(2,1)}, u32[]{:S(2)}, u32[]{:S(2)}) %collective-permute-start.53) | collective-permute-done | bytes 1048608 | tf_op jit(solution)/shard_map/ppermute | solution.py:38
  593.3 7.0 collective-permute-done.55.refs_3_
  626.9 15.5 %shard_map.714 = (f32[2048,256]{1,0:T(8,128)S(1)}, f32[2048,256]{1,0:T(8,128)S(1)}, f32[2048,256]{1,0:T(8,128)S(1)}) custom-call(s32[8]{0:T(128)S(1)} %copy-done.90, s32[8]{0:T(128)S(1)} %copy-done.92, bf16[2048,256]{1,0:T(8,128)(2,1)S(1)} %copy-done.33, bf16[2048,256]{1,0:T(8,128)(2,1)S(1)} %copy-done.35, bf16[2048,256]{1,0:T(8,128)(2,1)S(1)} %copy-done.37, ...), custom_call_target="tpu_custom_call" | custom-call | bytes 11000000 | tf_op jit(solution)/shard_map/pallas_call | solution.py:387
  664.6 5.0 convolution_convert_fusion.1
  670.3 5.9 fusion.8
  682.9 7.1 add_convert_fusion
  693.7 11.1 %collective-permute-done.68 = bf16[128,2048]{1,0:T(8,128)(2,1)S(1)} collective-permute-done((bf16[128,2048]{1,0:T(8,128)(2,1)S(1)}, bf16[128,2048]{1,0:T(8,128)(2,1)S(1)}, u32[]{:S(2)}, u32[]{:S(2)}) %collective-permute-start.68) | collective-permute-done | bytes 524320 | tf_op jit(solution)/shard_map/ppermute | solution.py:38
  716.8 5.7 shard_map.717
  722.5 8.8 %shard_map.718 = (f32[2048,256]{1,0:T(8,128)}, f32[2048,256]{1,0:T(8,128)}, f32[2048,256]{1,0:T(8,128)}, f32[2048,256]{1,0:T(8,128)}) custom-call(s32[1]{0:T(128)} %bitcast.side.flag, f32[2048,256]{1,0:T(8,128)S(1)} %copy-done.15, f32[2048,256]{1,0:T(8,128)S(1)} %copy-done.50, f32[2048,256]{1,0:T(8,128)S(1)} %copy-done.51, ...), custom_call_target="tpu_custom_call" | custom-call | bytes 2097152 | tf_op jit(solution)/shard_map/pallas_call | solution.py:812
  731.4 4.5 shard_map.719
  745.8 8.5 %collective-permute-done.77.other = bf16[256,1024]{1,0:T(8,128)(2,1)S(1)} collective-permute-done((bf16[256,1024]{1,0:T(8,128)(2,1)S(1)}, bf16[256,1024]{1,0:T(8,128)(2,1)S(1)}, u32[]{:S(2)}, u32[]{:S(2)}) %collective-permute-start.77) | collective-permute-done | bytes 524320 | tf_op jit(solution)/shard_map/ppermute | solution.py:38
  757.6 4.4 shard_map.720
  772.0 6.0 shard_map.721
  779.8 5.3 shard_map.722
  (599 shorter events, 282.8 us)
Async XLA Ops:
  7.3 52.1 %all-gather.5.cloned.1.call-start = ((), (), s32[]{:S(2)}) async-start(), calls=%async_computation.4 | async-start | bytes 2621440 | tf_op jit(solution)/shard_map/all_gather | solution.py:907
  9.6 98.6 %all-gather.7.cloned.1.call-start = ((), (), s32[]{:S(2)}) async-start(), calls=%async_computation.5 | async-start | bytes 2621440 | tf_op jit(solution)/shard_map/all_gather | solution.py:907
  31.5 23.9 %collective-permute-start.5 = (bf16[256,2048]{1,0:T(8,128)(2,1)S(1)}, bf16[256,2048]{1,0:T(8,128)(2,1)}, u32[]{:S(2)}, u32[]{:S(2)}) collective-permute-start(bf16[256,2048]{1,0:T(8,128)(2,1)S(1)} %dynamic-slice_bitcast_fusion.1), channel_id=1, source_target_pairs={{0,4},{4,0},{1,5},{5,1},{2,6},{6,2},{3,7},{7,3},{8,12},{12,8},{9,1... | collective-permute-start | bytes 3145736 | tf_op jit(solution)/shard_map/ppermute | solution.py:38
  55.4 23.1 %collective-permute-start.6 = (bf16[256,2048]{1,0:T(8,128)(2,1)}, bf16[256,2048]{1,0:T(8,128)(2,1)}, u32[]{:S(2)}, u32[]{:S(2)}) collective-permute-start(bf16[256,2048]{1,0:T(8,128)(2,1)} %collective-permute-done.5), channel_id=1, source_target_pairs={{0,2},{2,0},{1,3},{3,1},{4,6},{6,4},{5,7},{7,5},{8,10},{10,8},{9,1... | collective-permute-start | bytes 3145736 | tf_op jit(solution)/shard_map/ppermute | solution.py:38
  59.4 198.9 %all-gather.9.cloned.1.call-start = ((), (), s32[]{:S(2)}) async-start(), calls=%async_computation.6 | async-start | bytes 10485760 | tf_op jit(solution)/shard_map/all_gather | solution.py:907
  83.2 18.8 %collective-permute-start.8 = (bf16[512,2048]{1,0:T(8,128)(2,1)}, bf16[512,2048]{1,0:T(8,128)(2,1)}, u32[]{:S(2)}, u32[]{:S(2)}) collective-permute-start(bf16[512,2048]{1,0:T(8,128)(2,1)} %maximum_select_fusion.2), channel_id=1, source_target_pairs={{0,1},{1,0},{2,3},{3,2},{4,5},{5,4},{6,7},{7,6},{8,9},{9,8},{10,11... | collective-permute-start | bytes 6291464 | tf_op jit(solution)/shard_map/ppermute | solution.py:38
  84.4 14.5 %collective-permute-start.9 = (bf16[256,1024]{1,0:T(8,128)(2,1)}, bf16[256,1024]{1,0:T(8,128)(2,1)S(1)}, u32[]{:S(2)}, u32[]{:S(2)}) collective-permute-start(bf16[256,1024]{1,0:T(8,128)(2,1)} %get-tuple-element.450), channel_id=1, source_target_pairs={{0,4},{4,0},{1,5},{5,1},{2,6},{6,2},{3,7},{7,3},{8,12},{12,8},{9,1... | collective-permute-start | bytes 1572872 | tf_op jit(solution)/shard_map/ppermute | solution.py:38
  108.2 231.1 %all-gather.11.cloned.1.call-start = ((), (), s32[]{:S(2)}) async-start(), calls=%async_computation.7 | async-start | bytes 5242880 | tf_op jit(solution)/shard_map/all_gather | solution.py:907
  114.2 25.0 %collective-permute-start.13 = (bf16[256,1024]{1,0:T(8,128)(2,1)S(1)}, bf16[256,1024]{1,0:T(8,128)(2,1)S(1)}, u32[]{:S(2)}, u32[]{:S(2)}) collective-permute-start(bf16[256,1024]{1,0:T(8,128)(2,1)S(1)} %get-tuple-element.458), channel_id=1, source_target_pairs={{0,4},{4,0},{1,5},{5,1},{2,6},{6,2},{3,7},{7,3},{8,12},{12,8},{9,1... | collective-permute-start | bytes 1572872 | tf_op jit(solution)/shard_map/ppermute | solution.py:38
  187.1 24.3 %collective-permute-start.18 = (bf16[256,2048]{1,0:T(8,128)(2,1)S(1)}, bf16[256,2048]{1,0:T(8,128)(2,1)S(1)}, u32[]{:S(2)}, u32[]{:S(2)}) collective-permute-start(bf16[256,2048]{1,0:T(8,128)(2,1)S(1)} %pad_maximum_fusion.5), channel_id=1, source_target_pairs={{0,4},{4,0},{1,5},{5,1},{2,6},{6,2},{3,7},{7,3},{8,12},{12,8},{9,1... | collective-permute-start | bytes 3145736 | tf_op jit(solution)/shard_map/ppermute | solution.py:38
  188.7 23.9 %collective-permute-start.16 = (bf16[256,2048]{1,0:T(8,128)(2,1)S(1)}, bf16[256,2048]{1,0:T(8,128)(2,1)S(1)}, u32[]{:S(2)}, u32[]{:S(2)}) collective-permute-start(bf16[256,2048]{1,0:T(8,128)(2,1)S(1)} %pad_maximum_fusion.4), channel_id=1, source_target_pairs={{0,2},{2,0},{1,3},{3,1},{4,6},{6,4},{5,7},{7,5},{8,10},{10,8},{9,1... | collective-permute-start | bytes 3145736 | tf_op jit(solution)/shard_map/ppermute | solution.py:38
  258.3 306.0 %reduce-scatter.5.cloned.1.call-start = ((), (), s32[]{:S(2)}) async-start(), calls=%async_computation.8 | async-start | bytes 5242880 | tf_op jit(solution)/shard_map/reduce_scatter | solution.py:1004
  258.3 25.2 %collective-permute-start.19 = (bf16[256,2048]{1,0:T(8,128)(2,1)S(1)}, bf16[256,2048]{1,0:T(8,128)(2,1)S(1)}, u32[]{:S(2)}, u32[]{:S(2)}) collective-permute-start(bf16[256,2048]{1,0:T(8,128)(2,1)S(1)} %get-tuple-element.242.refs_0_), channel_id=1, source_target_pairs={{0,2},{2,0},{1,3},{3,1},{4,6},{6,4},{5,7},{7,5},{8,10},{10,8},{9,1... | collective-permute-start | bytes 3145736 | tf_op jit(solution)/shard_map/ppermute | solution.py:38
  259.9 24.8 %collective-permute-start.20 = (bf16[256,2048]{1,0:T(8,128)(2,1)S(1)}, bf16[256,2048]{1,0:T(8,128)(2,1)S(1)}, u32[]{:S(2)}, u32[]{:S(2)}) collective-permute-start(bf16[256,2048]{1,0:T(8,128)(2,1)S(1)} %get-tuple-element.242.refs_0_), channel_id=1, source_target_pairs={{0,4},{4,0},{1,5},{5,1},{2,6},{6,2},{3,7},{7,3},{8,12},{12,8},{9,1... | collective-permute-start | bytes 3145736 | tf_op jit(solution)/shard_map/ppermute | solution.py:38
  287.0 32.7 %collective-permute-start.23 = (bf16[256,2048]{1,0:T(8,128)(2,1)S(1)}, bf16[256,2048]{1,0:T(8,128)(2,1)S(1)}, u32[]{:S(2)}, u32[]{:S(2)}) collective-permute-start(bf16[256,2048]{1,0:T(8,128)(2,1)S(1)} %get-tuple-element.242.refs_0_), channel_id=1, source_target_pairs={{0,1},{1,0},{2,3},{3,2},{4,5},{5,4},{6,7},{7,6},{8,9},{9,8},{10,11... | collective-permute-start | bytes 3145736 | tf_op jit(solution)/shard_map/ppermute | solution.py:38
  287.0 32.7 %collective-permute-start.24 = (bf16[256,2048]{1,0:T(8,128)(2,1)S(1)}, bf16[256,2048]{1,0:T(8,128)(2,1)}, u32[]{:S(2)}, u32[]{:S(2)}) collective-permute-start(bf16[256,2048]{1,0:T(8,128)(2,1)S(1)} %collective-permute-done.19.refs_1_), channel_id=1, source_target_pairs={{0,1},{1,0},{2,3},{3,2},{4,5},{5,4},{6,7},{7,6},{8,9},{9,8},{10,11... | collective-permute-start | bytes 3145736 | tf_op jit(solution)/shard_map/ppermute | solution.py:38
  287.5 32.2 %collective-permute-start.25 = (bf16[256,2048]{1,0:T(8,128)(2,1)S(1)}, bf16[256,2048]{1,0:T(8,128)(2,1)}, u32[]{:S(2)}, u32[]{:S(2)}) collective-permute-start(bf16[256,2048]{1,0:T(8,128)(2,1)S(1)} %collective-permute-done.20.refs_2_), channel_id=1, source_target_pairs={{0,1},{1,0},{2,3},{3,2},{4,5},{5,4},{6,7},{7,6},{8,9},{9,8},{10,11... | collective-permute-start | bytes 3145736 | tf_op jit(solution)/shard_map/ppermute | solution.py:38
  298.1 21.6 %collective-permute-start.26 = (bf16[128,2048]{1,0:T(8,128)(2,1)S(1)}, bf16[128,2048]{1,0:T(8,128)(2,1)S(1)}, u32[]{:S(2)}, u32[]{:S(2)}) collective-permute-start(bf16[128,2048]{1,0:T(8,128)(2,1)S(1)} %collective-permute-done.21.refs_3_), channel_id=1, source_target_pairs={{0,1},{1,0},{2,3},{3,2},{4,5},{5,4},{6,7},{7,6},{8,9},{9,8},{10,11... | collective-permute-start | bytes 1572872 | tf_op jit(solution)/shard_map/ppermute | solution.py:38
  298.1 21.6 %collective-permute-start.27 = (bf16[128,2048]{1,0:T(8,128)(2,1)S(1)}, bf16[128,2048]{1,0:T(8,128)(2,1)}, u32[]{:S(2)}, u32[]{:S(2)}) collective-permute-start(bf16[128,2048]{1,0:T(8,128)(2,1)S(1)} %collective-permute-done.22.refs_4_), channel_id=1, source_target_pairs={{0,1},{1,0},{2,3},{3,2},{4,5},{5,4},{6,7},{7,6},{8,9},{9,8},{10,11... | collective-permute-start | bytes 1572872 | tf_op jit(solution)/shard_map/ppermute | solution.py:38
  361.9 15.2 %collective-permute-start.32 = (bf16[128,2048]{1,0:T(8,128)(2,1)S(1)}, bf16[128,2048]{1,0:T(8,128)(2,1)S(1)}, u32[]{:S(2)}, u32[]{:S(2)}) collective-permute-start(bf16[128,2048]{1,0:T(8,128)(2,1)S(1)} %pad_maximum_fusion.14), channel_id=1, source_target_pairs={{0,4},{4,0},{1,5},{5,1},{2,6},{6,2},{3,7},{7,3},{8,12},{12,8},{9,1... | collective-permute-start | bytes 1572872 | tf_op jit(solution)/shard_map/ppermute | solution.py:38
  362.1 16.6 %collective-permute-start.30 = (bf16[128,2048]{1,0:T(8,128)(2,1)S(1)}, bf16[128,2048]{1,0:T(8,128)(2,1)S(1)}, u32[]{:S(2)}, u32[]{:S(2)}) collective-permute-start(bf16[128,2048]{1,0:T(8,128)(2,1)S(1)} %pad_maximum_fusion.13), channel_id=1, source_target_pairs={{0,2},{2,0},{1,3},{3,1},{4,6},{6,4},{5,7},{7,5},{8,10},{10,8},{9,1... | collective-permute-start | bytes 1572872 | tf_op jit(solution)/shard_map/ppermute | solution.py:38
  367.6 20.0 %collective-permute-start.37 = (bf16[128,2048]{1,0:T(8,128)(2,1)S(1)}, bf16[128,2048]{1,0:T(8,128)(2,1)S(1)}, u32[]{:S(2)}, u32[]{:S(2)}) collective-permute-start(bf16[128,2048]{1,0:T(8,128)(2,1)S(1)} %pad_maximum_fusion.16), channel_id=1, source_target_pairs={{0,4},{4,0},{1,5},{5,1},{2,6},{6,2},{3,7},{7,3},{8,12},{12,8},{9,1... | collective-permute-start | bytes 1572872 | tf_op jit(solution)/shard_map/ppermute | solution.py:38
  368.1 20.6 %collective-permute-start.35 = (bf16[128,2048]{1,0:T(8,128)(2,1)S(1)}, bf16[128,2048]{1,0:T(8,128)(2,1)S(1)}, u32[]{:S(2)}, u32[]{:S(2)}) collective-permute-start(bf16[128,2048]{1,0:T(8,128)(2,1)S(1)} %pad_maximum_fusion.15), channel_id=1, source_target_pairs={{0,2},{2,0},{1,3},{3,1},{4,6},{6,4},{5,7},{7,5},{8,10},{10,8},{9,1... | collective-permute-start | bytes 1572872 | tf_op jit(solution)/shard_map/ppermute | solution.py:38
  391.5 24.1 %collective-permute-start.38 = (bf16[256,2048]{1,0:T(8,128)(2,1)S(1)}, bf16[256,2048]{1,0:T(8,128)(2,1)S(1)}, u32[]{:S(2)}, u32[]{:S(2)}) collective-permute-start(bf16[256,2048]{1,0:T(8,128)(2,1)S(1)} %pad_maximum_fusion.6), channel_id=1, source_target_pairs={{0,2},{2,0},{1,3},{3,1},{4,6},{6,4},{5,7},{7,5},{8,10},{10,8},{9,1... | collective-permute-start | bytes 3145736 | tf_op jit(solution)/shard_map/ppermute | solution.py:38
  393.0 23.8 %collective-permute-start.39 = (bf16[256,2048]{1,0:T(8,128)(2,1)S(1)}, bf16[256,2048]{1,0:T(8,128)(2,1)S(1)}, u32[]{:S(2)}, u32[]{:S(2)}) collective-permute-start(bf16[256,2048]{1,0:T(8,128)(2,1)S(1)} %pad_maximum_fusion.6), channel_id=1, source_target_pairs={{0,4},{4,0},{1,5},{5,1},{2,6},{6,2},{3,7},{7,3},{8,12},{12,8},{9,1... | collective-permute-start | bytes 3145736 | tf_op jit(solution)/shard_map/ppermute | solution.py:38
  393.6 25.3 %collective-permute-start.42 = (bf16[256,2048]{1,0:T(8,128)(2,1)S(1)}, bf16[256,2048]{1,0:T(8,128)(2,1)S(1)}, u32[]{:S(2)}, u32[]{:S(2)}) collective-permute-start(bf16[256,2048]{1,0:T(8,128)(2,1)S(1)} %pad_maximum_fusion.6), channel_id=1, source_target_pairs={{0,1},{1,0},{2,3},{3,2},{4,5},{5,4},{6,7},{7,6},{8,9},{9,8},{10,11... | collective-permute-start | bytes 3145736 | tf_op jit(solution)/shard_map/ppermute | solution.py:38
  444.5 175.0 %reduce-scatter.7.cloned.1.call-start = ((), (), s32[]{:S(2)}) async-start(), calls=%async_computation.9 | async-start | bytes 5242880 | tf_op jit(solution)/shard_map/reduce_scatter | solution.py:1004
  444.6 30.2 %collective-permute-start.47 = (bf16[256,2048]{1,0:T(8,128)(2,1)S(1)}, bf16[256,2048]{1,0:T(8,128)(2,1)S(1)}, u32[]{:S(2)}, u32[]{:S(2)}) collective-permute-start(bf16[256,2048]{1,0:T(8,128)(2,1)S(1)} %pad_maximum_fusion.7.refs_0_), channel_id=1, source_target_pairs={{0,2},{2,0},{1,3},{3,1},{4,6},{6,4},{5,7},{7,5},{8,10},{10,8},{9,1... | collective-permute-start | bytes 3145736 | tf_op jit(solution)/shard_map/ppermute | solution.py:38
  514.5 168.4 %reduce-scatter.9.cloned.1.call-start = ((), (), s32[]{:S(2)}) async-start(), calls=%async_computation.10 | async-start | bytes 5242880 | tf_op jit(solution)/shard_map/reduce_scatter | solution.py:1004
  517.0 14.2 %collective-permute-start.49 = (bf16[128,2048]{1,0:T(8,128)(2,1)}, bf16[128,2048]{1,0:T(8,128)(2,1)S(1)}, u32[]{:S(2)}, u32[]{:S(2)}) collective-permute-start(bf16[128,2048]{1,0:T(8,128)(2,1)} %get-tuple-element.428), channel_id=1, source_target_pairs={{0,2},{2,0},{1,3},{3,1},{4,6},{6,4},{5,7},{7,5},{8,10},{10,8},{9,1... | collective-permute-start | bytes 1572872 | tf_op jit(solution)/shard_map/ppermute | solution.py:38
  533.7 24.3 %collective-permute-start.51 = (bf16[256,2048]{1,0:T(8,128)(2,1)S(1)}, bf16[256,2048]{1,0:T(8,128)(2,1)}, u32[]{:S(2)}, u32[]{:S(2)}) collective-permute-start(bf16[256,2048]{1,0:T(8,128)(2,1)S(1)} %pad_maximum_fusion.8), channel_id=1, source_target_pairs={{0,2},{2,0},{1,3},{3,1},{4,6},{6,4},{5,7},{7,5},{8,10},{10,8},{9,1... | collective-permute-start | bytes 3145736 | tf_op jit(solution)/shard_map/ppermute | solution.py:38
  535.8 24.1 %collective-permute-start.52 = (bf16[256,2048]{1,0:T(8,128)(2,1)}, bf16[256,2048]{1,0:T(8,128)(2,1)}, u32[]{:S(2)}, u32[]{:S(2)}) collective-permute-start(bf16[256,2048]{1,0:T(8,128)(2,1)} %pad_maximum_fusion.9), channel_id=1, source_target_pairs={{0,4},{4,0},{1,5},{5,1},{2,6},{6,2},{3,7},{7,3},{8,12},{12,8},{9,1... | collective-permute-start | bytes 3145736 | tf_op jit(solution)/shard_map/ppermute | solution.py:38
  564.4 199.7 %reduce-scatter.11.cloned.1.call-start = ((), (), s32[]{:S(2)}) async-start(), calls=%async_computation.11 | async-start | bytes 5242880 | tf_op jit(solution)/shard_map/reduce_scatter | solution.py:1004
  564.4 23.2 %collective-permute-start.53 = (bf16[256,2048]{1,0:T(8,128)(2,1)}, bf16[256,2048]{1,0:T(8,128)(2,1)}, u32[]{:S(2)}, u32[]{:S(2)}) collective-permute-start(bf16[256,2048]{1,0:T(8,128)(2,1)} %get-tuple-element.290.refs_0_), channel_id=1, source_target_pairs={{0,2},{2,0},{1,3},{3,1},{4,6},{6,4},{5,7},{7,5},{8,10},{10,8},{9,1... | collective-permute-start | bytes 3145736 | tf_op jit(solution)/shard_map/ppermute | solution.py:38
  565.6 23.0 %collective-permute-start.54 = (bf16[256,2048]{1,0:T(8,128)(2,1)}, bf16[256,2048]{1,0:T(8,128)(2,1)}, u32[]{:S(2)}, u32[]{:S(2)}) collective-permute-start(bf16[256,2048]{1,0:T(8,128)(2,1)} %get-tuple-element.290.refs_0_), channel_id=1, source_target_pairs={{0,4},{4,0},{1,5},{5,1},{2,6},{6,2},{3,7},{7,3},{8,12},{12,8},{9,1... | collective-permute-start | bytes 3145736 | tf_op jit(solution)/shard_map/ppermute | solution.py:38
  592.8 19.3 %collective-permute-start.57 = (bf16[256,2048]{1,0:T(8,128)(2,1)}, bf16[256,2048]{1,0:T(8,128)(2,1)}, u32[]{:S(2)}, u32[]{:S(2)}) collective-permute-start(bf16[256,2048]{1,0:T(8,128)(2,1)} %get-tuple-element.290.refs_0_), channel_id=1, source_target_pairs={{0,1},{1,0},{2,3},{3,2},{4,5},{5,4},{6,7},{7,6},{8,9},{9,8},{10,11... | collective-permute-start | bytes 3145736 | tf_op jit(solution)/shard_map/ppermute | solution.py:38
  592.8 20.3 %collective-permute-start.58 = (bf16[256,2048]{1,0:T(8,128)(2,1)}, bf16[256,2048]{1,0:T(8,128)(2,1)}, u32[]{:S(2)}, u32[]{:S(2)}) collective-permute-start(bf16[256,2048]{1,0:T(8,128)(2,1)} %collective-permute-done.53.refs_1_), channel_id=1, source_target_pairs={{0,1},{1,0},{2,3},{3,2},{4,5},{5,4},{6,7},{7,6},{8,9},{9,8},{10,11... | collective-permute-start | bytes 3145736 | tf_op jit(solution)/shard_map/ppermute | solution.py:38
  593.3 19.8 %collective-permute-start.59 = (bf16[256,2048]{1,0:T(8,128)(2,1)}, bf16[256,2048]{1,0:T(8,128)(2,1)}, u32[]{:S(2)}, u32[]{:S(2)}) collective-permute-start(bf16[256,2048]{1,0:T(8,128)(2,1)} %collective-permute-done.54.refs_2_), channel_id=1, source_target_pairs={{0,1},{1,0},{2,3},{3,2},{4,5},{5,4},{6,7},{7,6},{8,9},{9,8},{10,11... | collective-permute-start | bytes 3145736 | tf_op jit(solution)/shard_map/ppermute | solution.py:38
  612.2 30.3 %collective-permute-start.62 = (bf16[256,1024]{1,0:T(8,128)(2,1)}, bf16[256,1024]{1,0:T(8,128)(2,1)}, u32[]{:S(2)}, u32[]{:S(2)}) collective-permute-start(bf16[256,1024]{1,0:T(8,128)(2,1)} %dynamic-slice_bitcast_fusion.5), channel_id=1, source_target_pairs={{0,4},{4,0},{1,5},{5,1},{2,6},{6,2},{3,7},{7,3},{8,12},{12,8},{9,1... | collective-permute-start | bytes 1572872 | tf_op jit(solution)/shard_map/ppermute | solution.py:38
  620.7 21.8 %collective-permute-start.63 = (bf16[256,1024]{1,0:T(8,128)(2,1)S(1)}, bf16[256,1024]{1,0:T(8,128)(2,1)S(1)}, u32[]{:S(2)}, u32[]{:S(2)}) collective-permute-start(bf16[256,1024]{1,0:T(8,128)(2,1)S(1)} %dynamic-slice_bitcast_fusion.4), channel_id=1, source_target_pairs={{0,4},{4,0},{1,5},{5,1},{2,6},{6,2},{3,7},{7,3},{8,12},{12,8},{9,1... | collective-permute-start | bytes 1572872 | tf_op jit(solution)/shard_map/ppermute | solution.py:38
  690.3 14.5 %collective-permute-start.68 = (bf16[128,2048]{1,0:T(8,128)(2,1)S(1)}, bf16[128,2048]{1,0:T(8,128)(2,1)S(1)}, u32[]{:S(2)}, u32[]{:S(2)}) collective-permute-start(bf16[128,2048]{1,0:T(8,128)(2,1)S(1)} %get-tuple-element.420), channel_id=1, source_target_pairs={{0,4},{4,0},{1,5},{5,1},{2,6},{6,2},{3,7},{7,3},{8,12},{12,8},{9,1... | collective-permute-start | bytes 1572872 | tf_op jit(solution)/shard_map/ppermute | solution.py:38
  691.3 14.0 %collective-permute-start.70 = (bf16[128,2048]{1,0:T(8,128)(2,1)S(1)}, bf16[128,2048]{1,0:T(8,128)(2,1)S(1)}, u32[]{:S(2)}, u32[]{:S(2)}) collective-permute-start(bf16[128,2048]{1,0:T(8,128)(2,1)S(1)} %get-tuple-element.419), channel_id=1, source_target_pairs={{0,2},{2,0},{1,3},{3,1},{4,6},{6,4},{5,7},{7,5},{8,10},{10,8},{9,1... | collective-permute-start | bytes 1572872 | tf_op jit(solution)/shard_map/ppermute | solution.py:38
  692.6 24.2 %collective-permute-start.74 = (bf16[256,2048]{1,0:T(8,128)(2,1)S(1)}, bf16[256,2048]{1,0:T(8,128)(2,1)S(1)}, u32[]{:S(2)}, u32[]{:S(2)}) collective-permute-start(bf16[256,2048]{1,0:T(8,128)(2,1)S(1)} %copy-done.31), channel_id=1, source_target_pairs={{0,1},{1,0},{2,3},{3,2},{4,5},{5,4},{6,7},{7,6},{8,9},{9,8},{10,11... | collective-permute-start | bytes 3145736 | tf_op jit(solution)/shard_map/ppermute | solution.py:38
  693.1 23.7 %collective-permute-start.75 = (bf16[256,2048]{1,0:T(8,128)(2,1)S(1)}, bf16[256,2048]{1,0:T(8,128)(2,1)}, u32[]{:S(2)}, u32[]{:S(2)}) collective-permute-start(bf16[256,2048]{1,0:T(8,128)(2,1)S(1)} %copy-done.65), channel_id=1, source_target_pairs={{0,1},{1,0},{2,3},{3,2},{4,5},{5,4},{6,7},{7,6},{8,9},{9,8},{10,11... | collective-permute-start | bytes 3145736 | tf_op jit(solution)/shard_map/ppermute | solution.py:38
  706.5 29.4 %collective-permute-start.71 = (bf16[256,2048]{1,0:T(8,128)(2,1)}, bf16[256,2048]{1,0:T(8,128)(2,1)}, u32[]{:S(2)}, u32[]{:S(2)}) collective-permute-start(bf16[256,2048]{1,0:T(8,128)(2,1)} %pad_maximum_fusion.12), channel_id=1, source_target_pairs={{0,4},{4,0},{1,5},{5,1},{2,6},{6,2},{3,7},{7,3},{8,12},{12,8},{9,1... | collective-permute-start | bytes 3145736 | tf_op jit(solution)/shard_map/ppermute | solution.py:38
  708.8 27.1 %collective-permute-start.69 = (bf16[256,2048]{1,0:T(8,128)(2,1)}, bf16[256,2048]{1,0:T(8,128)(2,1)}, u32[]{:S(2)}, u32[]{:S(2)}) collective-permute-start(bf16[256,2048]{1,0:T(8,128)(2,1)} %pad_maximum_fusion.11), channel_id=1, source_target_pairs={{0,2},{2,0},{1,3},{3,1},{4,6},{6,4},{5,7},{7,5},{8,10},{10,8},{9,1... | collective-permute-start | bytes 3145736 | tf_op jit(solution)/shard_map/ppermute | solution.py:38
  714.3 21.6 %collective-permute-start.73 = (f32[1,4608]{1,0:T(1,128)S(1)}, f32[1,4608]{1,0:T(1,128)S(1)}, u32[]{:S(2)}, u32[]{:S(2)}) collective-permute-start(f32[1,4608]{1,0:T(1,128)S(1)} %add.343), channel_id=1, source_target_pairs={{0,16},{16,0},{1,17},{17,1},{2,18},{18,2},{3,19},{19,3},{4,20},{20... | collective-permute-start | bytes 55304 | tf_op jit(solution)/shard_map/ppermute | solution.py:38
  739.9 23.6 %collective-permute-start.78 = (bf16[256,2048]{1,0:T(8,128)(2,1)}, bf16[256,2048]{1,0:T(8,128)(2,1)}, u32[]{:S(2)}, u32[]{:S(2)}) collective-permute-start(bf16[256,2048]{1,0:T(8,128)(2,1)} %add_convert_fusion.7.refs_0_), channel_id=1, source_target_pairs={{0,2},{2,0},{1,3},{3,1},{4,6},{6,4},{5,7},{7,5},{8,10},{10,8},{9,1... | collective-permute-start | bytes 3145736 | tf_op jit(solution)/shard_map/ppermute | solution.py:38
  (180 other events, 1576.6 us)
Sparse Core Ops, SparseCore 0:
  10.2 49.0 all-gather.4
  60.9 44.6 all-gather.6
  108.3 149.9 all-gather.8
  260.3 78.9 all-gather.10
  444.7 74.3 reduce-scatter.4
  521.3 77.2 reduce-scatter.6
  600.9 77.2 reduce-scatter.8
  683.1 78.1 reduce-scatter.10

commit v5 on v4

--- a/solution.py
+++ b/solution.py
@@ -1078,12 +1078,12 @@
     both_attn = across(dot(moved[:group], w_qkv, 1, 1), dot(moved[group:], w_qkv, 1, 1))
     back_attn = collect(both_attn, CX)
     down_step = adam(*triple(6), *down_halves, y[None], turned=True)
-    gate_step = adam(*triple(4), *gate_halves, y[None])
     block_share = assemble(block_rows, block_theirs)
     back_attn, small, block_share, grad_upward, *turned = tie(
-        back_attn, small, block_share, grad_upward, *down_step, *gate_step
-    )
-    down_step, gate_step = turned[:4], turned[4:]
+        back_attn, small, block_share, grad_upward, *down_step, *gate_halves
+    )
+    down_step, gate_halves = turned[:4], turned[4:]
+    gate_step = adam(*triple(4), *gate_halves, y[None])
     up_step = adam(*triple(5), *to_owner(grad_upward), y[None])
     input_rows = over_chips((grad_res + back_attn).astype(b16))
     index = lax.axis_index(SHARD) * 2 + y
@@ -1097,8 +1097,9 @@
     gain_steps = []
     for i, grad in enumerate((head_sums[0], head_sums[1], wide_sums[0], wide_sums[1])):
         gain_steps += (grad,) + adam_step(*triple(7 + i), grad)
-    _, *turned = tie(grad_attn[:1, :1], *gain_steps, *up_step, *input_rows)
-    gain_steps, up_step, input_rows = turned[:16], turned[16:20], turned[20:]
+    _, *turned = tie(grad_attn[:1, :1], *gain_steps, *up_step, *gate_step, *input_rows)
+    gain_steps, up_step, gate_step = turned[:16], turned[16:20], turned[20:24]
+    input_rows = turned[24:]
     attn_halves = to_owner(grad_attn)
     input_share = assemble(input_rows, over_core(input_rows))
     stepped = attention_adam([triple(i) for i in range(4)], *attn_halves, y[None])

time: 802 us -> 799 us (level)
  transfers between devices with their start and end apart: 90 -> 90, of which waited for: 55 -> 56; matrix products, arithmetic and copies ran while one was open for 16% -> 16% of each run, Pallas kernels for 20% -> 20%
where the time goes in v5:
time: 799 us; the launch traced here: 791 us
  waiting for transfers between devices  329 us (41%)
  Pallas kernels  167 us (21%)
  local copies, waits for them, and re-layouts  84.2 us (11%)
  matrix products  74.7 us (9%)
  starting transfers between devices  67.1 us (8%)
  other arithmetic  51.9 us (6%)
  between operations  16.8 us (2%)
    ppermute x82, waiting for transfers between devices, swap(): return lax.ppermute(value, axis, [(0, 1), (1, 0)])  289 us
    dot_general x18, matrix products, dot(): lax.dot_general(a, b, (((ca,), (cb,)), ((), ())), preferred_element_type=...  74.7 us
    unnamed x294, local copies, waits for them, and re-layouts  67.3 us
    ppermute x82, starting transfers between devices, swap(): return lax.ppermute(value, axis, [(0, 1), (1, 0)])  66.6 us
    all_gather x4, waiting for transfers between devices, over_shard(): return lax.all_gather(value, SHARD, axis=0, tiled=True)  40.1 us
    pallas_call x2, Pallas kernels, ffn_forward(): pl.pallas_call(functools.partial(ffn_forward_body, len(blocks)), grid=(co...  25.1 us
    pallas_call x2, Pallas kernels, ffn_residual(): pl.pallas_call(ffn_residual_body, grid=(width // step,), in_specs=[full,...  23.3 us
    pallas_call x1, Pallas kernels, flash_backward(): pl.pallas_call(functools.partial(backward_body, span, size), grid_spec=pl...  17.4 us
  transfers between devices with their start and end apart: 90, of which 56 were waited for; matrix products, arithmetic and copies ran while one was open for 16% of the time, Pallas kernels for 20%

profile of v5, /device:TPU:0, one launch (start us, length us, event | category | flops | bytes accessed | tf_op | source)
XLA Modules:
  0.0 791.2 jit_solution(4521742815797822363)
XLA Ops:
  26.1 5.4 collective-permute-done.4
  31.8 23.6 %collective-permute-done.5 = bf16[256,2048]{1,0:T(8,128)(2,1)} collective-permute-done((bf16[256,2048]{1,0:T(8,128)(2,1)S(1)}, bf16[256,2048]{1,0:T(8,128)(2,1)}, u32[]{:S(2)}, u32[]{:S(2)}) %collective-permute-start.5) | collective-permute-done | bytes 1048608 | tf_op jit(solution)/shard_map/ppermute | solution.py:38
  59.4 9.7 %collective-permute-done.7 = bf16[256,1024]{1,0:T(8,128)(2,1)S(1)} collective-permute-done((bf16[256,1024]{1,0:T(8,128)(2,1)S(1)}, bf16[256,1024]{1,0:T(8,128)(2,1)S(1)}, u32[]{:S(2)}, u32[]{:S(2)}) %collective-permute-start.7) | collective-permute-done | bytes 524320 | tf_op jit(solution)/shard_map/ppermute | solution.py:38
  71.9 6.6 collective-permute-done.6
  78.5 4.7 maximum_select_fusion.2
  85.3 13.6 %collective-permute-done.9 = bf16[256,1024]{1,0:T(8,128)(2,1)S(1)} collective-permute-done((bf16[256,1024]{1,0:T(8,128)(2,1)}, bf16[256,1024]{1,0:T(8,128)(2,1)S(1)}, u32[]{:S(2)}, u32[]{:S(2)}) %collective-permute-start.9) | collective-permute-done | bytes 524320 | tf_op jit(solution)/shard_map/ppermute | solution.py:38
  102.1 6.1 maximum_select_fusion.remote
  122.0 8.8 %shard_map.701 = (f32[2048,768]{1,0:T(8,128)S(1)}, f32[2,2048]{1,0:T(2,128)S(1)}) custom-call(s32[1]{0:T(128)} %bitcast.side.flag, bf16[1024,2048]{1,0:T(8,128)(2,1)S(1)} %bitcast.114, bf16[1024,2048]{1,0:T(8,128)(2,1)S(1)} %copy-done.11, bf16[2048,1024]{1,0:T(8,128)(2,1)S(1)} %bitcast.108), custom_call_target="tpu_custom_call" | custom-call | bytes 6000000 | tf_op jit(solution)/shard_map/pallas_call | solution.py:188
  147.8 16.8 %shard_map.704 = (bf16[2048,256]{1,0:T(8,128)(2,1)S(1)}, f32[2,2048]{1,0:T(2,128)S(1)}) custom-call(s32[8]{0:T(128)S(1)} %fusion.46.spot, s32[8]{0:T(128)S(1)} %and_select_fusion.low, bf16[2048,256]{1,0:T(8,128)(2,1)S(1)} %get-tuple-element.237.query, bf16[2048,256]{1,0:T(8,128)(2,1)S(1)} %get-tuple-element.238.keys, ...), custom_call_target="tpu_custom_call" | custom-call | bytes 9000000 | tf_op jit(solution)/shard_map/pallas_call | solution.py:302
  166.0 7.1 collective-permute-done.14
  176.2 12.4 %collective-permute-done.15 = bf16[128,2048]{1,0:T(8,128)(2,1)S(1)} collective-permute-done((bf16[128,2048]{1,0:T(8,128)(2,1)S(1)}, bf16[128,2048]{1,0:T(8,128)(2,1)S(1)}, u32[]{:S(2)}, u32[]{:S(2)}) %collective-permute-start.15) | collective-permute-done | bytes 524320 | tf_op jit(solution)/shard_map/ppermute | solution.py:38
  192.1 21.2 %collective-permute-done.18 = bf16[256,2048]{1,0:T(8,128)(2,1)S(1)} collective-permute-done((bf16[256,2048]{1,0:T(8,128)(2,1)S(1)}, bf16[256,2048]{1,0:T(8,128)(2,1)S(1)}, u32[]{:S(2)}, u32[]{:S(2)}) %collective-permute-start.18) | collective-permute-done | bytes 1048608 | tf_op jit(solution)/shard_map/ppermute | solution.py:38
  219.5 38.8 %all-gather.9.cloned.1.call-done.refs_5_.refs_6_.w_gate.w_up = bf16[2048,2048]{1,0:T(8,128)(2,1)} async-done(((bf16[512,2048]{1,0:T(8,128)(2,1)}), bf16[2048,2048]{1,0:T(8,128)(2,1)}) %all-gather.9.cloned.1.call-update) | async-done | bytes 8388624 | tf_op jit(solution)/shard_map/all_gather | solution.py:907
  261.4 22.2 %collective-permute-done.19.refs_1_ = bf16[256,2048]{1,0:T(8,128)(2,1)S(1)} collective-permute-done((bf16[256,2048]{1,0:T(8,128)(2,1)S(1)}, bf16[256,2048]{1,0:T(8,128)(2,1)S(1)}, u32[]{:S(2)}, u32[]{:S(2)}) %collective-permute-start.19) | collective-permute-done | bytes 1048608 | tf_op jit(solution)/shard_map/ppermute | solution.py:38
  287.5 10.2 %collective-permute-done.21.refs_3_ = bf16[128,2048]{1,0:T(8,128)(2,1)S(1)} collective-permute-done((bf16[128,2048]{1,0:T(8,128)(2,1)S(1)}, bf16[128,2048]{1,0:T(8,128)(2,1)S(1)}, u32[]{:S(2)}, u32[]{:S(2)}) %collective-permute-start.21) | collective-permute-done | bytes 524320 | tf_op jit(solution)/shard_map/ppermute | solution.py:38
  302.0 11.7 %shard_map.705 = (bf16[1024,2048]{1,0:T(8,128)(2,1)S(1)}, bf16[1024,1024]{1,0:T(8,128)(2,1)S(1)}, bf16[1024,1024]{1,0:T(8,128)(2,1)S(1)}, bf16[1024,1024]{1,0:T(8,128)(2,1)S(1)}) custom-call(bf16[256,2048]{1,0:T(8,128)(2,1)S(1)} %get-tuple-element.244.refs_0_, bf16[256,2048]{1,0:T(8,128)(2,1)S(1)} %collective-permute-done.19.refs_1_, ...), custom_call_target="tpu_custom_call" | custom-call | bytes 5000000 | tf_op jit(solution)/shard_map/pallas_call | solution.py:540
  319.7 13.3 %shard_map.706 = (bf16[1024,2048]{1,0:T(8,128)(2,1)S(1)}, bf16[1024,1024]{1,0:T(8,128)(2,1)S(1)}, bf16[1024,1024]{1,0:T(8,128)(2,1)S(1)}, bf16[1024,1024]{1,0:T(8,128)(2,1)S(1)}) custom-call(bf16[256,2048]{1,0:T(8,128)(2,1)S(1)} %collective-permute-done.23.refs_0_, bf16[256,2048]{1,0:T(8,128)(2,1)} %collective-permute-done.24.refs_1_, ...), custom_call_target="tpu_custom_call" | custom-call | bytes 5000000 | tf_op jit(solution)/shard_map/pallas_call | solution.py:540
  339.3 5.0 convolution_convert_fusion.4
  372.2 4.9 collective-permute-done.32
  379.0 8.5 %collective-permute-done.37 = bf16[128,2048]{1,0:T(8,128)(2,1)S(1)} collective-permute-done((bf16[128,2048]{1,0:T(8,128)(2,1)S(1)}, bf16[128,2048]{1,0:T(8,128)(2,1)S(1)}, u32[]{:S(2)}, u32[]{:S(2)}) %collective-permute-start.37) | collective-permute-done | bytes 524320 | tf_op jit(solution)/shard_map/ppermute | solution.py:38
  393.6 22.0 %collective-permute-done.38 = bf16[256,2048]{1,0:T(8,128)(2,1)S(1)} collective-permute-done((bf16[256,2048]{1,0:T(8,128)(2,1)S(1)}, bf16[256,2048]{1,0:T(8,128)(2,1)S(1)}, u32[]{:S(2)}, u32[]{:S(2)}) %collective-permute-start.38) | collective-permute-done | bytes 1048608 | tf_op jit(solution)/shard_map/ppermute | solution.py:38
  419.0 9.7 %collective-permute-done.40 = bf16[128,2048]{1,0:T(8,128)(2,1)S(1)} collective-permute-done((bf16[128,2048]{1,0:T(8,128)(2,1)S(1)}, bf16[128,2048]{1,0:T(8,128)(2,1)S(1)}, u32[]{:S(2)}, u32[]{:S(2)}) %collective-permute-start.40) | collective-permute-done | bytes 524320 | tf_op jit(solution)/shard_map/ppermute | solution.py:38
  431.7 4.7 fusion.75
  438.4 6.1 add_convert_fusion.3
  454.0 7.9 %shard_map.707 = (bf16[1024,1024]{1,0:T(8,128)(2,1)S(1)}, bf16[1024,1024]{1,0:T(8,128)(2,1)S(1)}) custom-call(bf16[1024,2048]{1,0:T(8,128)(2,1)S(1)} %copy-done.21, bf16[2048,1024]{1,0:T(8,128)(2,1)S(1)} %copy-done.9, bf16[1024,1024]{1,0:T(8,128)(2,1)S(1)} %copy-done.57, bf16[1024,1024]{1,0:T(8,128)(2,1)S(1)} %copy-done.59), custom_call_target="tpu_custom_call" | custom-call | bytes 3000000 | tf_op jit(solution)/shard_map/pallas_call | solution.py:640
  467.2 7.6 shard_map.708
  475.9 11.4 %shard_map.709 = bf16[1024,2048]{1,0:T(8,128)(2,1)S(1)} custom-call(bf16[1024,1024]{1,0:T(8,128)(2,1)S(1)} %get-tuple-element.303.d_gate, bf16[1024,1024]{1,0:T(8,128)(2,1)S(1)} %get-tuple-element.290.d_up, bf16[2048,2048]{1,0:T(8,128)(2,1)S(1)} %bitcast.105, bf16[2048,2048]{1,0:T(8,128)(2,1)S(1)} %bitcast.105), custom_call_target="tpu_custom_call" | custom-call | bytes 4500000 | tf_op jit(solution)/shard_map/pallas_call | solution.py:669
  487.3 6.1 convolution_convert_fusion.2
  494.5 12.0 %shard_map.710.both = bf16[1024,2048]{1,0:T(8,128)(2,1)S(1)} custom-call(bf16[1024,1024]{1,0:T(8,128)(2,1)S(1)} %copy-done.45, bf16[1024,1024]{1,0:T(8,128)(2,1)S(1)} %get-tuple-element.288.d_up, bf16[2048,2048]{1,0:T(8,128)(2,1)S(1)} %bitcast.105, bf16[2048,2048]{1,0:T(8,128)(2,1)S(1)} %bitcast.105, bf16[1024,2048]{1,0:T(8,128)(2,1)S(1)} %collective-permute-done.48.rest_0_), custom_call_target="tpu_custom_call" | custom-call | bytes 4500000 | tf_op jit(solution)/shard_map/pallas_call | solution.py:669
  508.4 6.1 add_convert_fusion.1
  519.8 11.4 %collective-permute-done.49 = bf16[128,2048]{1,0:T(8,128)(2,1)S(1)} collective-permute-done((bf16[128,2048]{1,0:T(8,128)(2,1)}, bf16[128,2048]{1,0:T(8,128)(2,1)S(1)}, u32[]{:S(2)}, u32[]{:S(2)}) %collective-permute-start.49) | collective-permute-done | bytes 524320 | tf_op jit(solution)/shard_map/ppermute | solution.py:38
  536.9 4.6 fusion.76
  541.6 6.2 add_convert_fusion.2
  547.7 10.3 %collective-permute-done.51.from_x = bf16[256,2048]{1,0:T(8,128)(2,1)} collective-permute-done((bf16[256,2048]{1,0:T(8,128)(2,1)S(1)}, bf16[256,2048]{1,0:T(8,128)(2,1)}, u32[]{:S(2)}, u32[]{:S(2)}) %collective-permute-start.51) | collective-permute-done | bytes 1048608 | tf_op jit(solution)/shard_map/ppermute | solution.py:38
  559.9 4.4 shard_map.711
  566.2 21.4 %collective-permute-done.53.refs_1_ = bf16[256,2048]{1,0:T(8,128)(2,1)} collective-permute-done((bf16[256,2048]{1,0:T(8,128)(2,1)}, bf16[256,2048]{1,0:T(8,128)(2,1)}, u32[]{:S(2)}, u32[]{:S(2)}) %collective-permute-start.53) | collective-permute-done | bytes 1048608 | tf_op jit(solution)/shard_map/ppermute | solution.py:38
  593.3 7.0 collective-permute-done.55.refs_3_
  626.9 17.4 %shard_map.714 = (f32[2048,256]{1,0:T(8,128)S(1)}, f32[2048,256]{1,0:T(8,128)S(1)}, f32[2048,256]{1,0:T(8,128)S(1)}) custom-call(s32[8]{0:T(128)S(1)} %copy-done.90, s32[8]{0:T(128)S(1)} %copy-done.92, bf16[2048,256]{1,0:T(8,128)(2,1)S(1)} %copy-done.33, bf16[2048,256]{1,0:T(8,128)(2,1)S(1)} %copy-done.35, bf16[2048,256]{1,0:T(8,128)(2,1)S(1)} %copy-done.37, ...), custom_call_target="tpu_custom_call" | custom-call | bytes 11000000 | tf_op jit(solution)/shard_map/pallas_call | solution.py:387
  666.4 5.0 convolution_convert_fusion.1
  672.1 6.0 fusion.8
  684.9 7.1 add_convert_fusion
  695.5 11.1 %collective-permute-done.68 = bf16[128,2048]{1,0:T(8,128)(2,1)S(1)} collective-permute-done((bf16[128,2048]{1,0:T(8,128)(2,1)S(1)}, bf16[128,2048]{1,0:T(8,128)(2,1)S(1)}, u32[]{:S(2)}, u32[]{:S(2)}) %collective-permute-start.68) | collective-permute-done | bytes 524320 | tf_op jit(solution)/shard_map/ppermute | solution.py:38
  716.8 6.0 shard_map.717
  722.8 7.3 shard_map.718
  748.9 4.5 shard_map.720
  754.3 4.5 shard_map.719
  770.3 6.0 shard_map.721
  778.6 5.3 shard_map.722
  (599 shorter events, 285.0 us)
Async XLA Ops:
  7.3 52.1 %all-gather.5.cloned.1.call-start = ((), (), s32[]{:S(2)}) async-start(), calls=%async_computation.4 | async-start | bytes 2621440 | tf_op jit(solution)/shard_map/all_gather | solution.py:907
  9.6 98.6 %all-gather.7.cloned.1.call-start = ((), (), s32[]{:S(2)}) async-start(), calls=%async_computation.5 | async-start | bytes 2621440 | tf_op jit(solution)/shard_map/all_gather | solution.py:907
  31.5 23.9 %collective-permute-start.5 = (bf16[256,2048]{1,0:T(8,128)(2,1)S(1)}, bf16[256,2048]{1,0:T(8,128)(2,1)}, u32[]{:S(2)}, u32[]{:S(2)}) collective-permute-start(bf16[256,2048]{1,0:T(8,128)(2,1)S(1)} %dynamic-slice_bitcast_fusion.1), channel_id=1, source_target_pairs={{0,4},{4,0},{1,5},{5,1},{2,6},{6,2},{3,7},{7,3},{8,12},{12,8},{9,1... | collective-permute-start | bytes 3145736 | tf_op jit(solution)/shard_map/ppermute | solution.py:38
  55.4 23.1 %collective-permute-start.6 = (bf16[256,2048]{1,0:T(8,128)(2,1)}, bf16[256,2048]{1,0:T(8,128)(2,1)}, u32[]{:S(2)}, u32[]{:S(2)}) collective-permute-start(bf16[256,2048]{1,0:T(8,128)(2,1)} %collective-permute-done.5), channel_id=1, source_target_pairs={{0,2},{2,0},{1,3},{3,1},{4,6},{6,4},{5,7},{7,5},{8,10},{10,8},{9,1... | collective-permute-start | bytes 3145736 | tf_op jit(solution)/shard_map/ppermute | solution.py:38
  59.4 198.9 %all-gather.9.cloned.1.call-start = ((), (), s32[]{:S(2)}) async-start(), calls=%async_computation.6 | async-start | bytes 10485760 | tf_op jit(solution)/shard_map/all_gather | solution.py:907
  83.2 18.8 %collective-permute-start.8 = (bf16[512,2048]{1,0:T(8,128)(2,1)}, bf16[512,2048]{1,0:T(8,128)(2,1)}, u32[]{:S(2)}, u32[]{:S(2)}) collective-permute-start(bf16[512,2048]{1,0:T(8,128)(2,1)} %maximum_select_fusion.2), channel_id=1, source_target_pairs={{0,1},{1,0},{2,3},{3,2},{4,5},{5,4},{6,7},{7,6},{8,9},{9,8},{10,11... | collective-permute-start | bytes 6291464 | tf_op jit(solution)/shard_map/ppermute | solution.py:38
  84.4 14.5 %collective-permute-start.9 = (bf16[256,1024]{1,0:T(8,128)(2,1)}, bf16[256,1024]{1,0:T(8,128)(2,1)S(1)}, u32[]{:S(2)}, u32[]{:S(2)}) collective-permute-start(bf16[256,1024]{1,0:T(8,128)(2,1)} %get-tuple-element.454), channel_id=1, source_target_pairs={{0,4},{4,0},{1,5},{5,1},{2,6},{6,2},{3,7},{7,3},{8,12},{12,8},{9,1... | collective-permute-start | bytes 1572872 | tf_op jit(solution)/shard_map/ppermute | solution.py:38
  108.2 231.1 %all-gather.11.cloned.1.call-start = ((), (), s32[]{:S(2)}) async-start(), calls=%async_computation.7 | async-start | bytes 5242880 | tf_op jit(solution)/shard_map/all_gather | solution.py:907
  114.2 25.0 %collective-permute-start.13 = (bf16[256,1024]{1,0:T(8,128)(2,1)S(1)}, bf16[256,1024]{1,0:T(8,128)(2,1)S(1)}, u32[]{:S(2)}, u32[]{:S(2)}) collective-permute-start(bf16[256,1024]{1,0:T(8,128)(2,1)S(1)} %get-tuple-element.462), channel_id=1, source_target_pairs={{0,4},{4,0},{1,5},{5,1},{2,6},{6,2},{3,7},{7,3},{8,12},{12,8},{9,1... | collective-permute-start | bytes 1572872 | tf_op jit(solution)/shard_map/ppermute | solution.py:38
  174.6 14.0 %collective-permute-start.15 = (bf16[128,2048]{1,0:T(8,128)(2,1)S(1)}, bf16[128,2048]{1,0:T(8,128)(2,1)S(1)}, u32[]{:S(2)}, u32[]{:S(2)}) collective-permute-start(bf16[128,2048]{1,0:T(8,128)(2,1)S(1)} %get-tuple-element.436), channel_id=1, source_target_pairs={{0,4},{4,0},{1,5},{5,1},{2,6},{6,2},{3,7},{7,3},{8,12},{12,8},{9,1... | collective-permute-start | bytes 1572872 | tf_op jit(solution)/shard_map/ppermute | solution.py:38
  189.1 24.3 %collective-permute-start.18 = (bf16[256,2048]{1,0:T(8,128)(2,1)S(1)}, bf16[256,2048]{1,0:T(8,128)(2,1)S(1)}, u32[]{:S(2)}, u32[]{:S(2)}) collective-permute-start(bf16[256,2048]{1,0:T(8,128)(2,1)S(1)} %pad_maximum_fusion.5), channel_id=1, source_target_pairs={{0,4},{4,0},{1,5},{5,1},{2,6},{6,2},{3,7},{7,3},{8,12},{12,8},{9,1... | collective-permute-start | bytes 3145736 | tf_op jit(solution)/shard_map/ppermute | solution.py:38
  190.7 23.9 %collective-permute-start.16 = (bf16[256,2048]{1,0:T(8,128)(2,1)S(1)}, bf16[256,2048]{1,0:T(8,128)(2,1)S(1)}, u32[]{:S(2)}, u32[]{:S(2)}) collective-permute-start(bf16[256,2048]{1,0:T(8,128)(2,1)S(1)} %pad_maximum_fusion.4), channel_id=1, source_target_pairs={{0,2},{2,0},{1,3},{3,1},{4,6},{6,4},{5,7},{7,5},{8,10},{10,8},{9,1... | collective-permute-start | bytes 3145736 | tf_op jit(solution)/shard_map/ppermute | solution.py:38
  258.3 306.0 %reduce-scatter.5.cloned.1.call-start = ((), (), s32[]{:S(2)}) async-start(), calls=%async_computation.8 | async-start | bytes 5242880 | tf_op jit(solution)/shard_map/reduce_scatter | solution.py:1004
  258.3 25.2 %collective-permute-start.19 = (bf16[256,2048]{1,0:T(8,128)(2,1)S(1)}, bf16[256,2048]{1,0:T(8,128)(2,1)S(1)}, u32[]{:S(2)}, u32[]{:S(2)}) collective-permute-start(bf16[256,2048]{1,0:T(8,128)(2,1)S(1)} %get-tuple-element.244.refs_0_), channel_id=1, source_target_pairs={{0,2},{2,0},{1,3},{3,1},{4,6},{6,4},{5,7},{7,5},{8,10},{10,8},{9,1... | collective-permute-start | bytes 3145736 | tf_op jit(solution)/shard_map/ppermute | solution.py:38
  259.9 24.8 %collective-permute-start.20 = (bf16[256,2048]{1,0:T(8,128)(2,1)S(1)}, bf16[256,2048]{1,0:T(8,128)(2,1)S(1)}, u32[]{:S(2)}, u32[]{:S(2)}) collective-permute-start(bf16[256,2048]{1,0:T(8,128)(2,1)S(1)} %get-tuple-element.244.refs_0_), channel_id=1, source_target_pairs={{0,4},{4,0},{1,5},{5,1},{2,6},{6,2},{3,7},{7,3},{8,12},{12,8},{9,1... | collective-permute-start | bytes 3145736 | tf_op jit(solution)/shard_map/ppermute | solution.py:38
  287.0 32.7 %collective-permute-start.23 = (bf16[256,2048]{1,0:T(8,128)(2,1)S(1)}, bf16[256,2048]{1,0:T(8,128)(2,1)S(1)}, u32[]{:S(2)}, u32[]{:S(2)}) collective-permute-start(bf16[256,2048]{1,0:T(8,128)(2,1)S(1)} %get-tuple-element.244.refs_0_), channel_id=1, source_target_pairs={{0,1},{1,0},{2,3},{3,2},{4,5},{5,4},{6,7},{7,6},{8,9},{9,8},{10,11... | collective-permute-start | bytes 3145736 | tf_op jit(solution)/shard_map/ppermute | solution.py:38
  287.0 32.7 %collective-permute-start.24 = (bf16[256,2048]{1,0:T(8,128)(2,1)S(1)}, bf16[256,2048]{1,0:T(8,128)(2,1)}, u32[]{:S(2)}, u32[]{:S(2)}) collective-permute-start(bf16[256,2048]{1,0:T(8,128)(2,1)S(1)} %collective-permute-done.19.refs_1_), channel_id=1, source_target_pairs={{0,1},{1,0},{2,3},{3,2},{4,5},{5,4},{6,7},{7,6},{8,9},{9,8},{10,11... | collective-permute-start | bytes 3145736 | tf_op jit(solution)/shard_map/ppermute | solution.py:38
  287.5 32.2 %collective-permute-start.25 = (bf16[256,2048]{1,0:T(8,128)(2,1)S(1)}, bf16[256,2048]{1,0:T(8,128)(2,1)}, u32[]{:S(2)}, u32[]{:S(2)}) collective-permute-start(bf16[256,2048]{1,0:T(8,128)(2,1)S(1)} %collective-permute-done.20.refs_2_), channel_id=1, source_target_pairs={{0,1},{1,0},{2,3},{3,2},{4,5},{5,4},{6,7},{7,6},{8,9},{9,8},{10,11... | collective-permute-start | bytes 3145736 | tf_op jit(solution)/shard_map/ppermute | solution.py:38
  298.1 21.6 %collective-permute-start.26 = (bf16[128,2048]{1,0:T(8,128)(2,1)S(1)}, bf16[128,2048]{1,0:T(8,128)(2,1)S(1)}, u32[]{:S(2)}, u32[]{:S(2)}) collective-permute-start(bf16[128,2048]{1,0:T(8,128)(2,1)S(1)} %collective-permute-done.21.refs_3_), channel_id=1, source_target_pairs={{0,1},{1,0},{2,3},{3,2},{4,5},{5,4},{6,7},{7,6},{8,9},{9,8},{10,11... | collective-permute-start | bytes 1572872 | tf_op jit(solution)/shard_map/ppermute | solution.py:38
  298.1 21.6 %collective-permute-start.27 = (bf16[128,2048]{1,0:T(8,128)(2,1)S(1)}, bf16[128,2048]{1,0:T(8,128)(2,1)}, u32[]{:S(2)}, u32[]{:S(2)}) collective-permute-start(bf16[128,2048]{1,0:T(8,128)(2,1)S(1)} %collective-permute-done.22.refs_4_), channel_id=1, source_target_pairs={{0,1},{1,0},{2,3},{3,2},{4,5},{5,4},{6,7},{7,6},{8,9},{9,8},{10,11... | collective-permute-start | bytes 1572872 | tf_op jit(solution)/shard_map/ppermute | solution.py:38
  361.9 15.2 %collective-permute-start.32 = (bf16[128,2048]{1,0:T(8,128)(2,1)S(1)}, bf16[128,2048]{1,0:T(8,128)(2,1)S(1)}, u32[]{:S(2)}, u32[]{:S(2)}) collective-permute-start(bf16[128,2048]{1,0:T(8,128)(2,1)S(1)} %pad_maximum_fusion.14), channel_id=1, source_target_pairs={{0,4},{4,0},{1,5},{5,1},{2,6},{6,2},{3,7},{7,3},{8,12},{12,8},{9,1... | collective-permute-start | bytes 1572872 | tf_op jit(solution)/shard_map/ppermute | solution.py:38
  362.1 16.6 %collective-permute-start.30 = (bf16[128,2048]{1,0:T(8,128)(2,1)S(1)}, bf16[128,2048]{1,0:T(8,128)(2,1)S(1)}, u32[]{:S(2)}, u32[]{:S(2)}) collective-permute-start(bf16[128,2048]{1,0:T(8,128)(2,1)S(1)} %pad_maximum_fusion.13), channel_id=1, source_target_pairs={{0,2},{2,0},{1,3},{3,1},{4,6},{6,4},{5,7},{7,5},{8,10},{10,8},{9,1... | collective-permute-start | bytes 1572872 | tf_op jit(solution)/shard_map/ppermute | solution.py:38
  367.6 20.0 %collective-permute-start.37 = (bf16[128,2048]{1,0:T(8,128)(2,1)S(1)}, bf16[128,2048]{1,0:T(8,128)(2,1)S(1)}, u32[]{:S(2)}, u32[]{:S(2)}) collective-permute-start(bf16[128,2048]{1,0:T(8,128)(2,1)S(1)} %pad_maximum_fusion.16), channel_id=1, source_target_pairs={{0,4},{4,0},{1,5},{5,1},{2,6},{6,2},{3,7},{7,3},{8,12},{12,8},{9,1... | collective-permute-start | bytes 1572872 | tf_op jit(solution)/shard_map/ppermute | solution.py:38
  368.1 20.6 %collective-permute-start.35 = (bf16[128,2048]{1,0:T(8,128)(2,1)S(1)}, bf16[128,2048]{1,0:T(8,128)(2,1)S(1)}, u32[]{:S(2)}, u32[]{:S(2)}) collective-permute-start(bf16[128,2048]{1,0:T(8,128)(2,1)S(1)} %pad_maximum_fusion.15), channel_id=1, source_target_pairs={{0,2},{2,0},{1,3},{3,1},{4,6},{6,4},{5,7},{7,5},{8,10},{10,8},{9,1... | collective-permute-start | bytes 1572872 | tf_op jit(solution)/shard_map/ppermute | solution.py:38
  391.5 24.1 %collective-permute-start.38 = (bf16[256,2048]{1,0:T(8,128)(2,1)S(1)}, bf16[256,2048]{1,0:T(8,128)(2,1)S(1)}, u32[]{:S(2)}, u32[]{:S(2)}) collective-permute-start(bf16[256,2048]{1,0:T(8,128)(2,1)S(1)} %pad_maximum_fusion.6), channel_id=1, source_target_pairs={{0,2},{2,0},{1,3},{3,1},{4,6},{6,4},{5,7},{7,5},{8,10},{10,8},{9,1... | collective-permute-start | bytes 3145736 | tf_op jit(solution)/shard_map/ppermute | solution.py:38
  393.0 23.8 %collective-permute-start.39 = (bf16[256,2048]{1,0:T(8,128)(2,1)S(1)}, bf16[256,2048]{1,0:T(8,128)(2,1)S(1)}, u32[]{:S(2)}, u32[]{:S(2)}) collective-permute-start(bf16[256,2048]{1,0:T(8,128)(2,1)S(1)} %pad_maximum_fusion.6), channel_id=1, source_target_pairs={{0,4},{4,0},{1,5},{5,1},{2,6},{6,2},{3,7},{7,3},{8,12},{12,8},{9,1... | collective-permute-start | bytes 3145736 | tf_op jit(solution)/shard_map/ppermute | solution.py:38
  393.6 25.3 %collective-permute-start.42 = (bf16[256,2048]{1,0:T(8,128)(2,1)S(1)}, bf16[256,2048]{1,0:T(8,128)(2,1)S(1)}, u32[]{:S(2)}, u32[]{:S(2)}) collective-permute-start(bf16[256,2048]{1,0:T(8,128)(2,1)S(1)} %pad_maximum_fusion.6), channel_id=1, source_target_pairs={{0,1},{1,0},{2,3},{3,2},{4,5},{5,4},{6,7},{7,6},{8,9},{9,8},{10,11... | collective-permute-start | bytes 3145736 | tf_op jit(solution)/shard_map/ppermute | solution.py:38
  444.5 175.0 %reduce-scatter.7.cloned.1.call-start = ((), (), s32[]{:S(2)}) async-start(), calls=%async_computation.9 | async-start | bytes 5242880 | tf_op jit(solution)/shard_map/reduce_scatter | solution.py:1004
  444.6 30.2 %collective-permute-start.47 = (bf16[256,2048]{1,0:T(8,128)(2,1)S(1)}, bf16[256,2048]{1,0:T(8,128)(2,1)S(1)}, u32[]{:S(2)}, u32[]{:S(2)}) collective-permute-start(bf16[256,2048]{1,0:T(8,128)(2,1)S(1)} %pad_maximum_fusion.7.refs_0_), channel_id=1, source_target_pairs={{0,2},{2,0},{1,3},{3,1},{4,6},{6,4},{5,7},{7,5},{8,10},{10,8},{9,1... | collective-permute-start | bytes 3145736 | tf_op jit(solution)/shard_map/ppermute | solution.py:38
  514.5 170.3 %reduce-scatter.9.cloned.1.call-start = ((), (), s32[]{:S(2)}) async-start(), calls=%async_computation.10 | async-start | bytes 5242880 | tf_op jit(solution)/shard_map/reduce_scatter | solution.py:1004
  517.0 14.2 %collective-permute-start.49 = (bf16[128,2048]{1,0:T(8,128)(2,1)}, bf16[128,2048]{1,0:T(8,128)(2,1)S(1)}, u32[]{:S(2)}, u32[]{:S(2)}) collective-permute-start(bf16[128,2048]{1,0:T(8,128)(2,1)} %get-tuple-element.432), channel_id=1, source_target_pairs={{0,2},{2,0},{1,3},{3,1},{4,6},{6,4},{5,7},{7,5},{8,10},{10,8},{9,1... | collective-permute-start | bytes 1572872 | tf_op jit(solution)/shard_map/ppermute | solution.py:38
  533.7 24.3 %collective-permute-start.51 = (bf16[256,2048]{1,0:T(8,128)(2,1)S(1)}, bf16[256,2048]{1,0:T(8,128)(2,1)}, u32[]{:S(2)}, u32[]{:S(2)}) collective-permute-start(bf16[256,2048]{1,0:T(8,128)(2,1)S(1)} %pad_maximum_fusion.8), channel_id=1, source_target_pairs={{0,2},{2,0},{1,3},{3,1},{4,6},{6,4},{5,7},{7,5},{8,10},{10,8},{9,1... | collective-permute-start | bytes 3145736 | tf_op jit(solution)/shard_map/ppermute | solution.py:38
  535.8 24.1 %collective-permute-start.52 = (bf16[256,2048]{1,0:T(8,128)(2,1)}, bf16[256,2048]{1,0:T(8,128)(2,1)}, u32[]{:S(2)}, u32[]{:S(2)}) collective-permute-start(bf16[256,2048]{1,0:T(8,128)(2,1)} %pad_maximum_fusion.9), channel_id=1, source_target_pairs={{0,4},{4,0},{1,5},{5,1},{2,6},{6,2},{3,7},{7,3},{8,12},{12,8},{9,1... | collective-permute-start | bytes 3145736 | tf_op jit(solution)/shard_map/ppermute | solution.py:38
  564.4 198.7 %reduce-scatter.11.cloned.1.call-start = ((), (), s32[]{:S(2)}) async-start(), calls=%async_computation.11 | async-start | bytes 5242880 | tf_op jit(solution)/shard_map/reduce_scatter | solution.py:1004
  564.4 23.2 %collective-permute-start.53 = (bf16[256,2048]{1,0:T(8,128)(2,1)}, bf16[256,2048]{1,0:T(8,128)(2,1)}, u32[]{:S(2)}, u32[]{:S(2)}) collective-permute-start(bf16[256,2048]{1,0:T(8,128)(2,1)} %get-tuple-element.292.refs_0_), channel_id=1, source_target_pairs={{0,2},{2,0},{1,3},{3,1},{4,6},{6,4},{5,7},{7,5},{8,10},{10,8},{9,1... | collective-permute-start | bytes 3145736 | tf_op jit(solution)/shard_map/ppermute | solution.py:38
  565.6 23.0 %collective-permute-start.54 = (bf16[256,2048]{1,0:T(8,128)(2,1)}, bf16[256,2048]{1,0:T(8,128)(2,1)}, u32[]{:S(2)}, u32[]{:S(2)}) collective-permute-start(bf16[256,2048]{1,0:T(8,128)(2,1)} %get-tuple-element.292.refs_0_), channel_id=1, source_target_pairs={{0,4},{4,0},{1,5},{5,1},{2,6},{6,2},{3,7},{7,3},{8,12},{12,8},{9,1... | collective-permute-start | bytes 3145736 | tf_op jit(solution)/shard_map/ppermute | solution.py:38
  592.8 19.3 %collective-permute-start.57 = (bf16[256,2048]{1,0:T(8,128)(2,1)}, bf16[256,2048]{1,0:T(8,128)(2,1)}, u32[]{:S(2)}, u32[]{:S(2)}) collective-permute-start(bf16[256,2048]{1,0:T(8,128)(2,1)} %get-tuple-element.292.refs_0_), channel_id=1, source_target_pairs={{0,1},{1,0},{2,3},{3,2},{4,5},{5,4},{6,7},{7,6},{8,9},{9,8},{10,11... | collective-permute-start | bytes 3145736 | tf_op jit(solution)/shard_map/ppermute | solution.py:38
  592.8 20.3 %collective-permute-start.58 = (bf16[256,2048]{1,0:T(8,128)(2,1)}, bf16[256,2048]{1,0:T(8,128)(2,1)}, u32[]{:S(2)}, u32[]{:S(2)}) collective-permute-start(bf16[256,2048]{1,0:T(8,128)(2,1)} %collective-permute-done.53.refs_1_), channel_id=1, source_target_pairs={{0,1},{1,0},{2,3},{3,2},{4,5},{5,4},{6,7},{7,6},{8,9},{9,8},{10,11... | collective-permute-start | bytes 3145736 | tf_op jit(solution)/shard_map/ppermute | solution.py:38
  593.3 19.8 %collective-permute-start.59 = (bf16[256,2048]{1,0:T(8,128)(2,1)}, bf16[256,2048]{1,0:T(8,128)(2,1)}, u32[]{:S(2)}, u32[]{:S(2)}) collective-permute-start(bf16[256,2048]{1,0:T(8,128)(2,1)} %collective-permute-done.54.refs_2_), channel_id=1, source_target_pairs={{0,1},{1,0},{2,3},{3,2},{4,5},{5,4},{6,7},{7,6},{8,9},{9,8},{10,11... | collective-permute-start | bytes 3145736 | tf_op jit(solution)/shard_map/ppermute | solution.py:38
  612.2 32.1 %collective-permute-start.62 = (bf16[256,1024]{1,0:T(8,128)(2,1)}, bf16[256,1024]{1,0:T(8,128)(2,1)}, u32[]{:S(2)}, u32[]{:S(2)}) collective-permute-start(bf16[256,1024]{1,0:T(8,128)(2,1)} %dynamic-slice_bitcast_fusion.5), channel_id=1, source_target_pairs={{0,4},{4,0},{1,5},{5,1},{2,6},{6,2},{3,7},{7,3},{8,12},{12,8},{9,1... | collective-permute-start | bytes 1572872 | tf_op jit(solution)/shard_map/ppermute | solution.py:38
  620.7 23.6 %collective-permute-start.63 = (bf16[256,1024]{1,0:T(8,128)(2,1)S(1)}, bf16[256,1024]{1,0:T(8,128)(2,1)S(1)}, u32[]{:S(2)}, u32[]{:S(2)}) collective-permute-start(bf16[256,1024]{1,0:T(8,128)(2,1)S(1)} %dynamic-slice_bitcast_fusion.4), channel_id=1, source_target_pairs={{0,4},{4,0},{1,5},{5,1},{2,6},{6,2},{3,7},{7,3},{8,12},{12,8},{9,1... | collective-permute-start | bytes 1572872 | tf_op jit(solution)/shard_map/ppermute | solution.py:38
  692.2 14.3 %collective-permute-start.68 = (bf16[128,2048]{1,0:T(8,128)(2,1)S(1)}, bf16[128,2048]{1,0:T(8,128)(2,1)S(1)}, u32[]{:S(2)}, u32[]{:S(2)}) collective-permute-start(bf16[128,2048]{1,0:T(8,128)(2,1)S(1)} %get-tuple-element.424), channel_id=1, source_target_pairs={{0,4},{4,0},{1,5},{5,1},{2,6},{6,2},{3,7},{7,3},{8,12},{12,8},{9,1... | collective-permute-start | bytes 1572872 | tf_op jit(solution)/shard_map/ppermute | solution.py:38
  693.2 14.0 %collective-permute-start.70 = (bf16[128,2048]{1,0:T(8,128)(2,1)S(1)}, bf16[128,2048]{1,0:T(8,128)(2,1)S(1)}, u32[]{:S(2)}, u32[]{:S(2)}) collective-permute-start(bf16[128,2048]{1,0:T(8,128)(2,1)S(1)} %get-tuple-element.423), channel_id=1, source_target_pairs={{0,2},{2,0},{1,3},{3,1},{4,6},{6,4},{5,7},{7,5},{8,10},{10,8},{9,1... | collective-permute-start | bytes 1572872 | tf_op jit(solution)/shard_map/ppermute | solution.py:38
  694.5 22.3 %collective-permute-start.74 = (bf16[256,2048]{1,0:T(8,128)(2,1)S(1)}, bf16[256,2048]{1,0:T(8,128)(2,1)}, u32[]{:S(2)}, u32[]{:S(2)}) collective-permute-start(bf16[256,2048]{1,0:T(8,128)(2,1)S(1)} %copy-done.31), channel_id=1, source_target_pairs={{0,1},{1,0},{2,3},{3,2},{4,5},{5,4},{6,7},{7,6},{8,9},{9,8},{10,11... | collective-permute-start | bytes 3145736 | tf_op jit(solution)/shard_map/ppermute | solution.py:38
  695.0 21.8 %collective-permute-start.75 = (bf16[256,2048]{1,0:T(8,128)(2,1)S(1)}, bf16[256,2048]{1,0:T(8,128)(2,1)}, u32[]{:S(2)}, u32[]{:S(2)}) collective-permute-start(bf16[256,2048]{1,0:T(8,128)(2,1)S(1)} %copy-done.65), channel_id=1, source_target_pairs={{0,1},{1,0},{2,3},{3,2},{4,5},{5,4},{6,7},{7,6},{8,9},{9,8},{10,11... | collective-permute-start | bytes 3145736 | tf_op jit(solution)/shard_map/ppermute | solution.py:38
  708.4 24.8 %collective-permute-start.71 = (bf16[256,2048]{1,0:T(8,128)(2,1)}, bf16[256,2048]{1,0:T(8,128)(2,1)}, u32[]{:S(2)}, u32[]{:S(2)}) collective-permute-start(bf16[256,2048]{1,0:T(8,128)(2,1)} %pad_maximum_fusion.12), channel_id=1, source_target_pairs={{0,4},{4,0},{1,5},{5,1},{2,6},{6,2},{3,7},{7,3},{8,12},{12,8},{9,1... | collective-permute-start | bytes 3145736 | tf_op jit(solution)/shard_map/ppermute | solution.py:38
  710.6 24.5 %collective-permute-start.69 = (bf16[256,2048]{1,0:T(8,128)(2,1)}, bf16[256,2048]{1,0:T(8,128)(2,1)}, u32[]{:S(2)}, u32[]{:S(2)}) collective-permute-start(bf16[256,2048]{1,0:T(8,128)(2,1)} %pad_maximum_fusion.11), channel_id=1, source_target_pairs={{0,2},{2,0},{1,3},{3,1},{4,6},{6,4},{5,7},{7,5},{8,10},{10,8},{9,1... | collective-permute-start | bytes 3145736 | tf_op jit(solution)/shard_map/ppermute | solution.py:38
  739.0 23.6 %collective-permute-start.78 = (bf16[256,2048]{1,0:T(8,128)(2,1)}, bf16[256,2048]{1,0:T(8,128)(2,1)}, u32[]{:S(2)}, u32[]{:S(2)}) collective-permute-start(bf16[256,2048]{1,0:T(8,128)(2,1)} %add_convert_fusion.7.refs_0_), channel_id=1, source_target_pairs={{0,2},{2,0},{1,3},{3,1},{4,6},{6,4},{5,7},{7,5},{8,10},{10,8},{9,1... | collective-permute-start | bytes 3145736 | tf_op jit(solution)/shard_map/ppermute | solution.py:38
  (180 other events, 1611.9 us)
Sparse Core Ops, SparseCore 0:
  10.2 49.0 all-gather.4
  60.9 44.6 all-gather.6
  108.3 149.9 all-gather.8
  260.3 78.9 all-gather.10
  444.7 74.3 reduce-scatter.4
  521.3 77.2 reduce-scatter.6
  600.9 77.2 reduce-scatter.8
  685.0 76.1 reduce-scatter.10
